TPU v7x, 32 devices: a whole 2x2x4 slice. The times are simulated.
32 devices in a mesh: row: 8 (over z, y), col: 4 (over x, core).
Axes of the slice: x: 2, y: 2, z: 4, core: 2. Of those that a mesh axis runs over, the one named last changes fastest.
Arguments:
- frames_in: bfloat16 [24000, 1024], P(('col', 'row')), may hold values from -6 to 6
- text_states: bfloat16 [1024, 1024], P(('col', 'row')), may hold values from -6 to 6
- self_query: bfloat16 [1024, 1024], P('row', 'col'), may hold values from -0.1875 to 0.1875
- self_key: bfloat16 [1024, 1024], P('row', 'col'), may hold values from -0.1875 to 0.1875
- self_value: bfloat16 [1024, 1024], P('row', 'col'), may hold values from -0.1875 to 0.1875
- self_output: bfloat16 [1024, 1024], P('row', 'col'), may hold values from -0.75 to 0.75
- cross_query: bfloat16 [1024, 1024], P('row', 'col'), may hold values from -0.1875 to 0.1875
- cross_key: bfloat16 [1024, 1024], P('row', 'col'), may hold values from -0.1875 to 0.1875
- cross_value: bfloat16 [1024, 1024], P('row', 'col'), may hold values from -0.1875 to 0.1875
- cross_output: bfloat16 [1024, 1024], P('row', 'col'), may hold values from -0.5 to 0.5
- up_weight: bfloat16 [1024, 4096], P('row', 'col'), may hold values from -0.1875 to 0.1875
- down_weight: bfloat16 [4096, 1024], P('row', 'col'), may hold values from -0.09375 to 0.09375
- first_gain: bfloat16 [1024], P(('row', 'col')), may hold values from 0.5 to 1.5
- first_bias: bfloat16 [1024], P(('row', 'col')), may hold values from -2.5 to 2.5
- second_gain: bfloat16 [1024], P(('row', 'col')), may hold values from 0.5 to 1.5
- second_bias: bfloat16 [1024], P(('row', 'col')), may hold values from -2.5 to 2.5
- third_gain: bfloat16 [1024], P(('row', 'col')), may hold values from 0.5 to 1.5
- third_bias: bfloat16 [1024], P(('row', 'col')), may hold values from -2.5 to 2.5
- cotangent: bfloat16 [24000, 1024], P(('col', 'row')), may hold values from -6 to 6
Outputs:
- layer_out: bfloat16 [24000, 1024], P(('col', 'row'))
- input_grad: float32 [24000, 1024], P(('col', 'row'))
- text_grad: float32 [1024, 1024], P(('col', 'row'))
- self_query_grad: float32 [1024, 1024], P('row', 'col')
- self_key_grad: float32 [1024, 1024], P('row', 'col')
- self_value_grad: float32 [1024, 1024], P('row', 'col')
- self_output_grad: float32 [1024, 1024], P('row', 'col')
- cross_query_grad: float32 [1024, 1024], P('row', 'col')
- cross_key_grad: float32 [1024, 1024], P('row', 'col')
- cross_value_grad: float32 [1024, 1024], P('row', 'col')
- cross_output_grad: float32 [1024, 1024], P('row', 'col')
- up_weight_grad: float32 [1024, 4096], P('row', 'col')
- down_weight_grad: float32 [4096, 1024], P('row', 'col')
- first_gain_grad: float32 [1024], P(('row', 'col'))
- first_bias_grad: float32 [1024], P(('row', 'col'))
- second_gain_grad: float32 [1024], P(('row', 'col'))
- second_bias_grad: float32 [1024], P(('row', 'col'))
- third_gain_grad: float32 [1024], P(('row', 'col'))
- third_bias_grad: float32 [1024], P(('row', 'col'))
All inputs are finite; a program needn't handle non-finite values.
Results may differ from a plain program's by a relative error of at most 0.023.
Values may be sent and summed in bfloat16 or wider, within the bound.
A program may use at most 256 MiB of HBM per device.

v0:
```python
from functools import partial

import jax
import jax.numpy as jnp
from jax import lax
from jax.sharding import PartitionSpec as P

HEADS = 16
HEAD_DIM = 64
FRAMES = 1500
TEXT = 64


def norm_forward(values, norm_gain, norm_bias):
    center = values - jnp.mean(values, axis=-1, keepdims=True)
    variance = jnp.mean(center * center, axis=-1, keepdims=True)
    return center * lax.rsqrt(variance + 1e-05) * norm_gain + norm_bias


def matmul(left, right):
    return jnp.dot(left, right, preferred_element_type=jnp.float32)


def by_transposed(left, right):
    return lax.dot_general(
        left, right, (((1,), (1,)), ((), ())), preferred_element_type=jnp.float32
    )


def over_tokens(left, right):
    return lax.dot_general(
        left, right, (((0,), (0,)), ((), ())), preferred_element_type=jnp.float32
    )


def collect(blocks):
    partly = (
        lax.all_gather(blocks[0], "col", axis=1, tiled=True),
        lax.all_gather(blocks[1], "col", axis=1, tiled=True),
        lax.all_gather(blocks[2], "col", axis=1, tiled=True),
        lax.all_gather(blocks[3], "col", axis=1, tiled=True),
        lax.all_gather(blocks[4], "col", axis=1, tiled=True),
        lax.all_gather(blocks[5], "col", axis=1, tiled=True),
        lax.all_gather(blocks[6], "col", axis=1, tiled=True),
        lax.all_gather(blocks[7], "col", axis=1, tiled=True),
        lax.all_gather(blocks[8], "col", axis=1, tiled=True),
        lax.all_gather(blocks[9], "col", axis=1, tiled=True),
        lax.all_gather(blocks[10], "col", axis=1, tiled=True),
    )
    return (
        lax.all_gather(partly[0], "row", axis=0, tiled=True),
        lax.all_gather(partly[1], "row", axis=0, tiled=True),
        lax.all_gather(partly[2], "row", axis=0, tiled=True),
        lax.all_gather(partly[3], "row", axis=0, tiled=True),
        lax.all_gather(partly[4], "row", axis=0, tiled=True),
        lax.all_gather(partly[5], "row", axis=0, tiled=True),
        lax.all_gather(partly[6], "row", axis=0, tiled=True),
        lax.all_gather(partly[7], "row", axis=0, tiled=True),
        lax.all_gather(partly[8], "row", axis=0, tiled=True),
        lax.all_gather(partly[9], "row", axis=0, tiled=True),
        lax.all_gather(partly[10], "row", axis=0, tiled=True),
    )


def spread(grads):
    partly = (
        lax.psum_scatter(
            grads[0].astype(jnp.bfloat16), "row", scatter_dimension=0, tiled=True
        ).astype(jnp.float32),
        lax.psum_scatter(
            grads[1].astype(jnp.bfloat16), "row", scatter_dimension=0, tiled=True
        ).astype(jnp.float32),
        lax.psum_scatter(
            grads[2].astype(jnp.bfloat16), "row", scatter_dimension=0, tiled=True
        ).astype(jnp.float32),
        lax.psum_scatter(
            grads[3].astype(jnp.bfloat16), "row", scatter_dimension=0, tiled=True
        ).astype(jnp.float32),
        lax.psum_scatter(
            grads[4].astype(jnp.bfloat16), "row", scatter_dimension=0, tiled=True
        ).astype(jnp.float32),
        lax.psum_scatter(
            grads[5].astype(jnp.bfloat16), "row", scatter_dimension=0, tiled=True
        ).astype(jnp.float32),
        lax.psum_scatter(
            grads[6].astype(jnp.bfloat16), "row", scatter_dimension=0, tiled=True
        ).astype(jnp.float32),
        lax.psum_scatter(
            grads[7].astype(jnp.bfloat16), "row", scatter_dimension=0, tiled=True
        ).astype(jnp.float32),
        lax.psum_scatter(
            grads[8].astype(jnp.bfloat16), "row", scatter_dimension=0, tiled=True
        ).astype(jnp.float32),
        lax.psum_scatter(
            grads[9].astype(jnp.bfloat16), "row", scatter_dimension=0, tiled=True
        ).astype(jnp.float32),
        lax.psum_scatter(
            grads[10].astype(jnp.bfloat16), "row", scatter_dimension=0, tiled=True
        ).astype(jnp.float32),
    )
    return (
        lax.psum_scatter(
            partly[0].astype(jnp.bfloat16), "col", scatter_dimension=1, tiled=True
        ).astype(jnp.float32),
        lax.psum_scatter(
            partly[1].astype(jnp.bfloat16), "col", scatter_dimension=1, tiled=True
        ).astype(jnp.float32),
        lax.psum_scatter(
            partly[2].astype(jnp.bfloat16), "col", scatter_dimension=1, tiled=True
        ).astype(jnp.float32),
        lax.psum_scatter(
            partly[3].astype(jnp.bfloat16), "col", scatter_dimension=1, tiled=True
        ).astype(jnp.float32),
        lax.psum_scatter(
            partly[4].astype(jnp.bfloat16), "col", scatter_dimension=1, tiled=True
        ).astype(jnp.float32),
        lax.psum_scatter(
            partly[5].astype(jnp.bfloat16), "col", scatter_dimension=1, tiled=True
        ).astype(jnp.float32),
        lax.psum_scatter(
            partly[6].astype(jnp.bfloat16), "col", scatter_dimension=1, tiled=True
        ).astype(jnp.float32),
        lax.psum_scatter(
            partly[7].astype(jnp.bfloat16), "col", scatter_dimension=1, tiled=True
        ).astype(jnp.float32),
        lax.psum_scatter(
            partly[8].astype(jnp.bfloat16), "col", scatter_dimension=1, tiled=True
        ).astype(jnp.float32),
        lax.psum_scatter(
            partly[9].astype(jnp.bfloat16), "col", scatter_dimension=1, tiled=True
        ).astype(jnp.float32),
        lax.psum_scatter(
            partly[10].astype(jnp.bfloat16), "col", scatter_dimension=1, tiled=True
        ).astype(jnp.float32),
    )


def heads_layout(stacked):
    return lax.all_to_all(stacked, "row", split_axis=1, concat_axis=0, tiled=True)


def tokens_layout(stacked):
    return lax.all_to_all(stacked, "row", split_axis=0, concat_axis=2, tiled=True)


def by_clips(arranged, start, count, length, heads_dev):
    section = arranged[:, start : start + count]
    return section.reshape(-1, length, heads_dev, HEAD_DIM)


def causal_scores(query_clip, key_clip, causal):
    scores = jnp.einsum(
        "qhd,khd->hqk", query_clip, key_clip, preferred_element_type=jnp.float32
    ) * HEAD_DIM ** (-0.5)
    if causal:
        allowed = jnp.arange(scores.shape[1])[:, None] >= jnp.arange(scores.shape[2])[None, :]
        scores = jnp.where(allowed, scores, -1e30)
    return scores


def attend_forward(query_clips, key_clips, value_clips, causal):

    def one_clip(operands):
        query_clip, key_clip, value_clip = operands
        scores = causal_scores(query_clip, key_clip, causal)
        highest = jnp.max(scores, axis=-1, keepdims=True)
        powers = jnp.exp(scores - highest)
        totals = jnp.sum(powers, axis=-1, keepdims=True)
        weights_low = (powers / totals).astype(jnp.bfloat16)
        mixture = jnp.einsum(
            "hqk,khd->qhd", weights_low, value_clip, preferred_element_type=jnp.float32
        )
        return (mixture.astype(jnp.bfloat16), (highest + jnp.log(totals))[..., 0])

    return lax.map(one_clip, (query_clips, key_clips, value_clips))


def attend_backward(query_clips, key_clips, value_clips, log_sums, grad_clips, causal):

    def one_clip(operands):
        query_clip, key_clip, value_clip, log_clip, grad_clip = operands
        scores = causal_scores(query_clip, key_clip, causal)
        probs_full = jnp.exp(scores - log_clip[..., None])
        grad_probs = jnp.einsum(
            "qhd,khd->hqk", grad_clip, value_clip, preferred_element_type=jnp.float32
        )
        grad_value = jnp.einsum(
            "hqk,qhd->khd",
            probs_full.astype(jnp.bfloat16),
            grad_clip,
            preferred_element_type=jnp.float32,
        )
        centered = grad_probs - jnp.sum(probs_full * grad_probs, axis=-1, keepdims=True)
        grad_scores = (probs_full * centered).astype(jnp.bfloat16)
        grad_query = jnp.einsum(
            "hqk,khd->qhd", grad_scores, key_clip, preferred_element_type=jnp.float32
        ) * HEAD_DIM ** (-0.5)
        grad_key = jnp.einsum(
            "hqk,qhd->khd", grad_scores, query_clip, preferred_element_type=jnp.float32
        ) * HEAD_DIM ** (-0.5)
        return (
            grad_query.astype(jnp.bfloat16),
            grad_key.astype(jnp.bfloat16),
            grad_value.astype(jnp.bfloat16),
        )

    return lax.map(one_clip, (query_clips, key_clips, value_clips, log_sums, grad_clips))


def local(
    frames_in,
    text_states,
    self_query,
    self_key,
    self_value,
    self_output,
    cross_query,
    cross_key,
    cross_value,
    cross_output,
    up_weight,
    down_weight,
    first_gain,
    first_bias,
    second_gain,
    second_bias,
    third_gain,
    third_bias,
    cotangent,
):
    row_count = lax.axis_size("row")
    col_count = lax.axis_size("col")
    heads_dev = HEADS // row_count
    width_dev = heads_dev * HEAD_DIM
    tok_rows = frames_in.shape[0]
    text_rows = text_states.shape[0]
    piece_len = first_gain.shape[0]
    gain_block = jnp.stack(
        [first_gain, first_bias, second_gain, second_bias, third_gain, third_bias]
    ).reshape(1, 6 * piece_len)
    param_blocks = (
        self_query,
        self_key,
        self_value,
        self_output,
        cross_query,
        cross_key,
        cross_value,
        cross_output,
        up_weight,
        down_weight,
        gain_block,
    )

    def unpack_gains(gathered_gains):
        arranged = gathered_gains.reshape(row_count, col_count, 6, piece_len).transpose(2, 0, 1, 3)
        return arranged.reshape(6, row_count * col_count * piece_len).astype(jnp.float32)

    gathered = collect(param_blocks)
    (
        query_self,
        key_self,
        value_self,
        out_self,
        query_cross,
        key_cross,
        value_cross,
        out_cross,
        up_full,
        down_full,
    ) = gathered[:10]
    norm_params = unpack_gains(gathered[10])
    frames = frames_in.astype(jnp.float32)
    hidden_one = norm_forward(frames, norm_params[0], norm_params[1]).astype(jnp.bfloat16)
    self_q = matmul(hidden_one, query_self).astype(jnp.bfloat16)
    self_k = matmul(hidden_one, key_self).astype(jnp.bfloat16)
    self_v = matmul(hidden_one, value_self).astype(jnp.bfloat16)
    text_k = matmul(text_states, key_cross).astype(jnp.bfloat16)
    text_v = matmul(text_states, value_cross).astype(jnp.bfloat16)
    sent_rows = 3 * tok_rows + 2 * text_rows
    arranged = heads_layout(jnp.concatenate([self_q, self_k, self_v, text_k, text_v], axis=0))
    arranged = arranged.reshape(row_count, sent_rows, width_dev)
    query_clips = by_clips(arranged, 0, tok_rows, FRAMES, heads_dev)
    key_clips = by_clips(arranged, tok_rows, tok_rows, FRAMES, heads_dev)
    value_clips = by_clips(arranged, 2 * tok_rows, tok_rows, FRAMES, heads_dev)
    text_keys = by_clips(arranged, 3 * tok_rows, text_rows, TEXT, heads_dev)
    text_values = by_clips(arranged, 3 * tok_rows + text_rows, text_rows, TEXT, heads_dev)
    self_clips, self_logs = attend_forward(query_clips, key_clips, value_clips, True)
    self_mix = tokens_layout(self_clips.reshape(row_count, tok_rows, width_dev))[0]
    resid_one = frames + matmul(self_mix, out_self)
    hidden_two = norm_forward(resid_one, norm_params[2], norm_params[3]).astype(jnp.bfloat16)
    cross_q = matmul(hidden_two, query_cross).astype(jnp.bfloat16)
    cross_arranged = heads_layout(cross_q).reshape(row_count, tok_rows, width_dev)
    cross_queries = by_clips(cross_arranged, 0, tok_rows, FRAMES, heads_dev)
    cross_clips, cross_logs = attend_forward(cross_queries, text_keys, text_values, False)
    cross_mix = tokens_layout(cross_clips.reshape(row_count, tok_rows, width_dev))[0]
    resid_two = resid_one + matmul(cross_mix, out_cross)
    hidden_three = norm_forward(resid_two, norm_params[4], norm_params[5]).astype(jnp.bfloat16)
    pre_act = matmul(hidden_three, up_full)
    inner = jax.nn.gelu(pre_act, approximate=False).astype(jnp.bfloat16)
    layer_out = (resid_two + matmul(inner, down_full)).astype(jnp.bfloat16)
    gathered = collect(param_blocks)
    (
        query_self,
        key_self,
        value_self,
        out_self,
        query_cross,
        key_cross,
        value_cross,
        out_cross,
        up_full,
        down_full,
    ) = gathered[:10]
    norm_params = unpack_gains(gathered[10])
    cotan_full = cotangent.astype(jnp.float32)
    down_grad = over_tokens(inner, cotangent)
    grad_inner = by_transposed(cotangent, down_full)
    unused_gelu, gelu_pull = jax.vjp(partial(jax.nn.gelu, approximate=False), pre_act)
    grad_pre = gelu_pull(grad_inner)[0].astype(jnp.bfloat16)
    up_grad = over_tokens(hidden_three, grad_pre)
    grad_three = by_transposed(grad_pre, up_full)
    unused_three, pull_three = jax.vjp(norm_forward, resid_two, norm_params[4], norm_params[5])
    through_three, third_gain_part, third_bias_part = pull_three(grad_three)
    grad_resid_two = cotan_full + through_three
    grad_cross = grad_resid_two.astype(jnp.bfloat16)
    cross_out_grad = over_tokens(cross_mix, grad_cross)
    grad_cross_mix = by_transposed(grad_cross, out_cross).astype(jnp.bfloat16)
    grad_cross_arr = heads_layout(grad_cross_mix).reshape(row_count, tok_rows, width_dev)
    grad_cross_clips = by_clips(grad_cross_arr, 0, tok_rows, FRAMES, heads_dev)
    cq_clips, tk_clips, tv_clips = attend_backward(
        cross_queries, text_keys, text_values, cross_logs, grad_cross_clips, False
    )
    back_cross = jnp.concatenate(
        [
            cq_clips.reshape(row_count, tok_rows, width_dev),
            tk_clips.reshape(row_count, text_rows, width_dev),
            tv_clips.reshape(row_count, text_rows, width_dev),
        ],
        axis=1,
    )
    back_cross = tokens_layout(back_cross)[0]
    grad_cross_q = back_cross[:tok_rows]
    grad_text_k = back_cross[tok_rows : tok_rows + text_rows]
    grad_text_v = back_cross[tok_rows + text_rows :]
    cross_query_part = over_tokens(hidden_two, grad_cross_q)
    cross_key_part = over_tokens(text_states, grad_text_k)
    cross_value_part = over_tokens(text_states, grad_text_v)
    text_grad = by_transposed(grad_text_k, key_cross) + by_transposed(grad_text_v, value_cross)
    grad_two = by_transposed(grad_cross_q, query_cross)
    unused_two, pull_two = jax.vjp(norm_forward, resid_one, norm_params[2], norm_params[3])
    through_two, second_gain_part, second_bias_part = pull_two(grad_two)
    grad_resid_one = grad_resid_two + through_two
    grad_self = grad_resid_one.astype(jnp.bfloat16)
    self_out_grad = over_tokens(self_mix, grad_self)
    grad_self_mix = by_transposed(grad_self, out_self).astype(jnp.bfloat16)
    grad_self_arr = heads_layout(grad_self_mix).reshape(row_count, tok_rows, width_dev)
    grad_self_clips = by_clips(grad_self_arr, 0, tok_rows, FRAMES, heads_dev)
    sq_clips, sk_clips, sv_clips = attend_backward(
        query_clips, key_clips, value_clips, self_logs, grad_self_clips, True
    )
    back_self = jnp.concatenate(
        [
            sq_clips.reshape(row_count, tok_rows, width_dev),
            sk_clips.reshape(row_count, tok_rows, width_dev),
            sv_clips.reshape(row_count, tok_rows, width_dev),
        ],
        axis=1,
    )
    back_self = tokens_layout(back_self)[0]
    grad_self_q = back_self[:tok_rows]
    grad_self_k = back_self[tok_rows : 2 * tok_rows]
    grad_self_v = back_self[2 * tok_rows :]
    self_query_part = over_tokens(hidden_one, grad_self_q)
    self_key_part = over_tokens(hidden_one, grad_self_k)
    self_value_part = over_tokens(hidden_one, grad_self_v)
    grad_one = (
        by_transposed(grad_self_q, query_self)
        + by_transposed(grad_self_k, key_self)
        + by_transposed(grad_self_v, value_self)
    )
    unused_one, pull_one = jax.vjp(norm_forward, frames, norm_params[0], norm_params[1])
    through_one, first_gain_part, first_bias_part = pull_one(grad_one)
    input_grad = grad_resid_one + through_one
    norm_grads = jnp.stack(
        [
            first_gain_part,
            first_bias_part,
            second_gain_part,
            second_bias_part,
            third_gain_part,
            third_bias_part,
        ]
    )
    norm_grads = norm_grads.reshape(6, row_count, col_count, piece_len).transpose(1, 2, 0, 3)
    norm_grads = norm_grads.reshape(row_count, col_count * 6 * piece_len)
    summed = spread(
        (
            self_query_part,
            self_key_part,
            self_value_part,
            self_out_grad,
            cross_query_part,
            cross_key_part,
            cross_value_part,
            cross_out_grad,
            up_grad,
            down_grad,
            norm_grads,
        )
    )
    norm_parts = summed[10].reshape(6, piece_len)
    return (
        layer_out,
        input_grad,
        text_grad,
        summed[0],
        summed[1],
        summed[2],
        summed[3],
        summed[4],
        summed[5],
        summed[6],
        summed[7],
        summed[8],
        summed[9],
        norm_parts[0],
        norm_parts[1],
        norm_parts[2],
        norm_parts[3],
        norm_parts[4],
        norm_parts[5],
    )


def solution(mesh):
    placed = (
        P(("col", "row"), None),
        P(("col", "row"), None),
        P("row", "col"),
        P("row", "col"),
        P("row", "col"),
        P("row", "col"),
        P("row", "col"),
        P("row", "col"),
        P("row", "col"),
        P("row", "col"),
        P("row", "col"),
        P("row", "col"),
        P(("row", "col")),
        P(("row", "col")),
        P(("row", "col")),
        P(("row", "col")),
        P(("row", "col")),
        P(("row", "col")),
        P(("col", "row"), None),
    )
    return jax.shard_map(
        local,
        mesh=mesh,
        in_specs=placed,
        out_specs=(
            P(("col", "row"), None),
            P(("col", "row"), None),
            P(("col", "row"), None),
            P("row", "col"),
            P("row", "col"),
            P("row", "col"),
            P("row", "col"),
            P("row", "col"),
            P("row", "col"),
            P("row", "col"),
            P("row", "col"),
            P("row", "col"),
            P("row", "col"),
            P(("row", "col")),
            P(("row", "col")),
            P(("row", "col")),
            P(("row", "col")),
            P(("row", "col")),
            P(("row", "col")),
        ),
        check_vma=False,
    )
```

profile of v0, /device:TPU:0, one launch (start us, length us, event | category | flops | bytes accessed | tf_op | source)
XLA Modules:
  0.0 2184.4 jit_solution(17821377741065539188)
XLA Ops:
  62.1 31.0 %all-gather = bf16[8,1,768]{2,1,0:T(2,128)(2,1)S(1)} all-gather(bf16[1,1,768]{2,1,0:T(2,128)(2,1)S(1)} %reshape.320), channel_id=1, replica_groups=mesh['row'=8,'col'=4] {'row'}, dimensions={0}, use_global_device_ids=true | all-gather | bytes 13824 | tf_op jit(solution)/shard_map/all_gather | solution.py:61
  118.2 47.9 %all-gather.18.cloned.1.call-done = bf16[1024,1024]{1,0:T(8,128)(2,1)} async-done(((bf16[128,1024]{1,0:T(8,128)(2,1)}), bf16[1024,1024]{1,0:T(8,128)(2,1)}) %all-gather.18.cloned.1.call-update) | async-done | bytes 2097168 | tf_op jit(solution)/shard_map/all_gather | solution.py:53
  169.5 46.4 %all-gather.16.cloned.1.call-done = bf16[1024,1024]{1,0:T(8,128)(2,1)} async-done(((bf16[128,1024]{1,0:T(8,128)(2,1)}), bf16[1024,1024]{1,0:T(8,128)(2,1)}) %all-gather.16.cloned.1.call-update) | async-done | bytes 2097168 | tf_op jit(solution)/shard_map/all_gather | solution.py:52
  220.4 45.3 %all-gather.14.cloned.1.call-done = bf16[1024,1024]{1,0:T(8,128)(2,1)} async-done(((bf16[128,1024]{1,0:T(8,128)(2,1)}), bf16[1024,1024]{1,0:T(8,128)(2,1)}) %all-gather.14.cloned.1.call-update) | async-done | bytes 2097168 | tf_op jit(solution)/shard_map/all_gather | solution.py:51
  270.2 26.2 %concatenate.11 = bf16[2314,1024]{1,0:T(8,128)(2,1)} concatenate(bf16[750,1024]{1,0:T(8,128)(2,1)} %convolution_convert_fusion.15, bf16[750,1024]{1,0:T(8,128)(2,1)} %convolution_convert_fusion.14, bf16[750,1024]{1,0:T(8,128)(2,1)S(1)} %convolution_convert_fusion.13, bf16[32,1024]{1,0:T(8,128)(2,1)S(1)} %convolution_convert_fusion.17, bf16[32,1024]{1,0:T(8,128)(2,1)S(1)} %convolution_convert_fusion.16), dimensions={0} | concatenate | bytes 9478144 | tf_op jit(solution)/shard_map/concatenate | solution.py:281
  321.5 123.9 %all-to-all-done = bf16[2314,8,128]{2,0,1:T(8,128)(2,1)} async-done(((bf16[2314,8,128]{2,0,1:T(8,128)(2,1)}), bf16[2314,8,128]{2,0,1:T(8,128)(2,1)}, u32[]{:S(2)}, u32[]{:S(2)}) %all-to-all-start) | async-done | bytes 4739104 | tf_op jit(solution)/shard_map/all_to_all | solution.py:139
  483.1 68.9 %while.52 = (s32[]{:T(128)}, bf16[4,1500,2,64]{1,3,2,0:T(8,128)(2,1)}, f32[4,2,1500]{2,1,0:T(2,128)S(1)}, bf16[4,1500,2,64]{1,3,2,0:T(8,128)(2,1)}, bf16[4,1500,...) while((s32[]{:T(128)}, bf16[4,1500,2,64]{1,3,2,0:T(8,128)(2,1)}, ...), condition=%wide.region_5.6_spmd, body=%wide.region_2.5_spmd.sunk | while | flops 1208438912 | bytes 64732008 | solution.py:175
  569.6 64.7 %all-to-all-done.1 = bf16[8,750,128]{2,1,0:T(8,128)(2,1)S(1)} async-done(((bf16[8,750,128]{2,1,0:T(8,128)(2,1)}), bf16[8,750,128]{2,1,0:T(8,128)(2,1)S(1)}, u32[]{:S(2)}, u32[]{:S(2)}) %all-to-all-start.1) | async-done | bytes 1536032 | tf_op jit(solution)/shard_map/all_to_all | solution.py:143
  658.3 46.8 %all-to-all-done.2 = bf16[750,8,128]{2,0,1:T(8,128)(2,1)S(1)} async-done(((bf16[750,8,128]{2,0,1:T(8,128)(2,1)}), bf16[750,8,128]{2,0,1:T(8,128)(2,1)S(1)}, u32[]{:S(2)}, u32[]{:S(2)}) %all-to-all-start.2) | async-done | bytes 1536032 | tf_op jit(solution)/shard_map/all_to_all | solution.py:139
  735.8 68.9 %all-to-all-done.3 = bf16[8,750,128]{2,1,0:T(8,128)(2,1)S(1)} async-done(((bf16[8,750,128]{2,1,0:T(8,128)(2,1)}), bf16[8,750,128]{2,1,0:T(8,128)(2,1)S(1)}, u32[]{:S(2)}, u32[]{:S(2)}) %all-to-all-start.3) | async-done | bytes 1536032 | tf_op jit(solution)/shard_map/all_to_all | solution.py:143
  825.5 24.1 %all-gather.36.cloned.1.call-done = bf16[4096,1024]{1,0:T(8,128)(2,1)} async-done(((bf16[512,1024]{1,0:T(8,128)(2,1)}), bf16[4096,1024]{1,0:T(8,128)(2,1)}) %all-gather.36.cloned.1.call-update) | async-done | bytes 8388624 | tf_op jit(solution)/shard_map/all_gather | solution.py:60
  849.6 38.1 %add_convert_fusion = (bf16[750,4096]{1,0:T(8,128)(2,1)S(1)}, f32[750,4096]{1,0:T(8,128)}) fusion(f32[750,4096]{1,0:T(8,128)} %fusion.127, bf16[750,1024]{1,0:T(8,128)(2,1)} %param.45, bf16[4096,1024]{1,0:T(8,128)(2,1)} %all-gather.36.cloned.1.call-done), kind=kOutput, calls=%fused_computation.117 | convolution fusion | flops 6512640000 | bytes 40644608 | tf_op jit(solution)/shard_map/dot_general | solution.py:25
  911.1 47.7 %all-to-all-done.4 = bf16[750,8,128]{2,0,1:T(8,128)(2,1)S(1)} async-done(((bf16[750,8,128]{2,0,1:T(8,128)(2,1)}), bf16[750,8,128]{2,0,1:T(8,128)(2,1)S(1)}, u32[]{:S(2)}, u32[]{:S(2)}) %all-to-all-start.4) | async-done | bytes 1536032 | tf_op jit(solution)/shard_map/all_to_all | solution.py:139
  998.7 44.0 %all_to_all.124 = bf16[8,814,128]{2,1,0:T(8,128)(2,1)S(1)} all-to-all(bf16[8,814,128]{2,1,0:T(8,128)(2,1)} %copy.127), channel_id=1, replica_groups=mesh['row'=8,'col'=4] {'row'}, dimensions={0} | all-to-all | bytes 3334144 | tf_op jit(solution)/shard_map/all_to_all | solution.py:143
  1123.3 22.9 %all-to-all-done.6 = bf16[750,8,128]{2,0,1:T(8,128)(2,1)S(1)} async-done(((bf16[750,8,128]{2,0,1:T(8,128)(2,1)}), bf16[750,8,128]{2,0,1:T(8,128)(2,1)S(1)}, u32[]{:S(2)}, u32[]{:S(2)}) %all-to-all-start.6) | async-done | bytes 1536032 | tf_op jit(solution)/shard_map/all_to_all | solution.py:139
  1160.3 231.5 %while.55 = (s32[]{:T(128)}, bf16[4,1500,2,64]{1,3,2,0:T(8,128)(2,1)}, bf16[4,1500,2,64]{1,3,2,0:T(8,128)(2,1)}, bf16[4,1500,2,64]{1,3,2,0:T(8,128)(2,1)}, bf16[...) while((s32[]{:T(128)}, ...), condition=%wide.region_23.24_spmd, body=%wide.region_21.23_spmd.sunk | while | flops 2923706880 | bytes 156808192 | solution.py:207
  1424.7 139.9 %all_to_all.125 = bf16[8,2250,128]{2,1,0:T(8,128)(2,1)S(1)} all-to-all(bf16[8,2250,128]{2,1,0:T(8,128)(2,1)} %copy.138), channel_id=1, replica_groups=mesh['row'=8,'col'=4] {'row'}, dimensions={0} | all-to-all | bytes 9216000 | tf_op jit(solution)/shard_map/all_to_all | solution.py:143
  1609.8 36.9 %all-reduce.1 = bf16[8,768]{1,0:T(8,128)(2,1)S(1)} all-reduce(bf16[8,768]{1,0:T(8,128)(2,1)S(1)} %convert_element_type.273), channel_id=22, replica_groups=mesh['row'=8,'col'=4] {'row'}, use_global_device_ids=true, to_apply=%region_52.53.clone | all-reduce | flops 6144 | bytes 24576
  1649.0 57.5 %reduce-scatter.60.cloned.1.call-done = bf16[512,1024]{1,0:T(8,128)(2,1)} async-done(((bf16[4096,1024]{1,0:T(8,128)(2,1)}), bf16[512,1024]{1,0:T(8,128)(2,1)}) %reduce-scatter.60.cloned.1.call-update) | async-done | bytes 1048592 | tf_op jit(solution)/shard_map/reduce_scatter | solution.py:94
  1706.5 70.2 %reduce-scatter.32.cloned.1.call-done = bf16[128,1024]{1,0:T(8,128)(2,1)} async-done(((bf16[1024,1024]{1,0:T(8,128)(2,1)}), bf16[128,1024]{1,0:T(8,128)(2,1)}) %reduce-scatter.32.cloned.1.call-update) | async-done | bytes 262160 | tf_op jit(solution)/shard_map/reduce_scatter | solution.py:70
  1799.7 70.4 %reduce-scatter.36.cloned.1.call-done = bf16[128,1024]{1,0:T(8,128)(2,1)} async-done(((bf16[1024,1024]{1,0:T(8,128)(2,1)}), bf16[128,1024]{1,0:T(8,128)(2,1)}) %reduce-scatter.36.cloned.1.call-update) | async-done | bytes 262160 | tf_op jit(solution)/shard_map/reduce_scatter | solution.py:73
  1961.9 69.9 %reduce-scatter.28.cloned.1.call-done = bf16[128,1024]{1,0:T(8,128)(2,1)} async-done(((bf16[1024,1024]{1,0:T(8,128)(2,1)}), bf16[128,1024]{1,0:T(8,128)(2,1)}) %reduce-scatter.28.cloned.1.call-update) | async-done | bytes 262160 | tf_op jit(solution)/shard_map/reduce_scatter | solution.py:67
  2054.6 26.1 %reduce-scatter.58.cloned.1.call-done = bf16[128,1024]{1,0:T(8,128)(2,1)} async-done(((bf16[128,4096]{1,0:T(8,128)(2,1)}), bf16[128,1024]{1,0:T(8,128)(2,1)}) %reduce-scatter.58.cloned.1.call-update) | async-done | bytes 262160 | tf_op jit(solution)/shard_map/reduce_scatter | solution.py:126
  2082.5 25.5 %reduce-scatter.62.cloned.1.call-done = bf16[512,256]{1,0:T(8,128)(2,1)} async-done(((bf16[512,1024]{1,0:T(8,128)(2,1)}), bf16[512,256]{1,0:T(8,128)(2,1)}) %reduce-scatter.62.cloned.1.call-update) | async-done | bytes 262160 | tf_op jit(solution)/shard_map/reduce_scatter | solution.py:129
  (575 shorter events, 1016.6 us)
Async XLA Ops:
  46.4 522.7 %all-gather.34.cloned.1.call-start = ((), (), s32[]{:S(2)}) async-start(), calls=%async_computation.39 | async-start | bytes 1310720 | tf_op jit(solution)/shard_map/all_gather | solution.py:47
  47.1 588.8 %all-gather.24.cloned.1.call-start = ((), (), s32[]{:S(2)}) async-start(), calls=%async_computation.34 | async-start | bytes 2359296 | tf_op jit(solution)/shard_map/all_gather | solution.py:54
  307.9 334.8 %all-gather.26.cloned.1.call-start = ((), (), s32[]{:S(2)}) async-start(), calls=%async_computation.35 | async-start | bytes 2359296 | tf_op jit(solution)/shard_map/all_gather | solution.py:55
  314.3 492.0 %all-gather.28.cloned.1.call-start = ((), (), s32[]{:S(2)}) async-start(), calls=%async_computation.36 | async-start | bytes 2359296 | tf_op jit(solution)/shard_map/all_gather | solution.py:58
  320.7 491.0 %all-gather.32.cloned.1.call-start = ((), (), s32[]{:S(2)}) async-start(), calls=%async_computation.38 | async-start | bytes 9437184 | tf_op jit(solution)/shard_map/all_gather | solution.py:59
  906.5 668.3 %reduce-scatter.52.cloned.1.call-start = ((), (), s32[]{:S(2)}) async-start(), calls=%async_computation.53 | async-start | bytes 2359296 | tf_op jit(solution)/shard_map/reduce_scatter | solution.py:88
  911.1 672.3 %reduce-scatter.44.cloned.1.call-start = ((), (), s32[]{:S(2)}) async-start(), calls=%async_computation.49 | async-start | bytes 2359296 | tf_op jit(solution)/shard_map/reduce_scatter | solution.py:79
  1053.0 531.1 %reduce-scatter.40.cloned.1.call-start = ((), (), s32[]{:S(2)}) async-start(), calls=%async_computation.47 | async-start | bytes 2359296 | tf_op jit(solution)/shard_map/reduce_scatter | solution.py:76
  1065.7 519.0 %reduce-scatter.66.cloned.1.call-start = ((), (), s32[]{:S(2)}) async-start(), calls=%async_computation.60 | async-start | bytes 2359296
  1073.5 513.1 %reduce-scatter.64.cloned.1.call-start = ((), (), s32[]{:S(2)}) async-start(), calls=%async_computation.59 | async-start | bytes 2359296
  1080.3 568.0 %reduce-scatter.56.cloned.1.call-start = ((), (), s32[]{:S(2)}) async-start(), calls=%async_computation.55 | async-start | bytes 9437184 | tf_op jit(solution)/shard_map/reduce_scatter | solution.py:91
  1101.8 604.6 %reduce-scatter.60.cloned.1.call-start = ((), (), s32[]{:S(2)}) async-start(), calls=%async_computation.57 | async-start | bytes 9437184 | tf_op jit(solution)/shard_map/reduce_scatter | solution.py:94
  1122.9 653.8 %reduce-scatter.32.cloned.1.call-start = ((), (), s32[]{:S(2)}) async-start(), calls=%async_computation.43 | async-start | bytes 2359296 | tf_op jit(solution)/shard_map/reduce_scatter | solution.py:70
  1583.3 308.4 %reduce-scatter.46.cloned.1.call-start = ((), (), s32[]{:S(2)}) async-start(), calls=%async_computation.50 | async-start | bytes 327680 | tf_op jit(solution)/shard_map/reduce_scatter | solution.py:114
  1584.0 330.1 %reduce-scatter.42.cloned.1.call-start = ((), (), s32[]{:S(2)}) async-start(), calls=%async_computation.48 | async-start | bytes 327680 | tf_op jit(solution)/shard_map/reduce_scatter | solution.py:111
  1584.6 352.7 %reduce-scatter.50.cloned.1.call-start = ((), (), s32[]{:S(2)}) async-start(), calls=%async_computation.52 | async-start | bytes 327680 | tf_op jit(solution)/shard_map/reduce_scatter | solution.py:120
  1586.5 373.8 %reduce-scatter.48.cloned.1.call-start = ((), (), s32[]{:S(2)}) async-start(), calls=%async_computation.51 | async-start | bytes 327680 | tf_op jit(solution)/shard_map/reduce_scatter | solution.py:117
  1588.4 443.4 %reduce-scatter.28.cloned.1.call-start = ((), (), s32[]{:S(2)}) async-start(), calls=%async_computation.41 | async-start | bytes 2359296 | tf_op jit(solution)/shard_map/reduce_scatter | solution.py:67
  1595.1 458.0 %reduce-scatter.68.cloned.1.call-start = ((), (), s32[]{:S(2)}) async-start(), calls=%async_computation.61 | async-start | bytes 245760
  1648.2 432.5 %reduce-scatter.58.cloned.1.call-start = ((), (), s32[]{:S(2)}) async-start(), calls=%async_computation.56 | async-start | bytes 1310720 | tf_op jit(solution)/shard_map/reduce_scatter | solution.py:126
  1649.0 459.0 %reduce-scatter.62.cloned.1.call-start = ((), (), s32[]{:S(2)}) async-start(), calls=%async_computation.58 | async-start | bytes 1310720 | tf_op jit(solution)/shard_map/reduce_scatter | solution.py:129
  1706.5 424.2 %reduce-scatter.34.cloned.1.call-start = ((), (), s32[]{:S(2)}) async-start(), calls=%async_computation.44 | async-start | bytes 327680 | tf_op jit(solution)/shard_map/reduce_scatter | solution.py:105
  1776.7 376.5 %reduce-scatter.38.cloned.1.call-start = ((), (), s32[]{:S(2)}) async-start(), calls=%async_computation.46 | async-start | bytes 327680 | tf_op jit(solution)/shard_map/reduce_scatter | solution.py:108
  1870.1 305.7 %reduce-scatter.30.cloned.1.call-start = ((), (), s32[]{:S(2)}) async-start(), calls=%async_computation.42 | async-start | bytes 327680 | tf_op jit(solution)/shard_map/reduce_scatter | solution.py:102
  (110 other events, 4613.5 us)
Sparse Core Ops, SparseCore 0:
  16.5 49.6 all-gather.19
  68.3 47.8 all-gather.21
  118.3 47.7 all-gather.17
  168.1 47.7 all-gather.15
  217.9 47.7 all-gather.13
  302.9 119.0 all-gather.23
  424.1 49.7 all-gather.25
  475.9 47.9 all-gather.27
  526.0 174.2 all-gather.31
  702.3 147.2 all-gather.35
  911.2 84.4 reduce-scatter.51
  1053.1 73.1 reduce-scatter.43
  1129.7 73.8 reduce-scatter.39
  1207.0 66.7 reduce-scatter.65
  1277.2 66.5 reduce-scatter.63
  1347.3 206.8 reduce-scatter.55
  1558.2 148.1 reduce-scatter.59
  1709.8 66.7 reduce-scatter.31
  1802.1 67.9 reduce-scatter.35
  1964.0 67.6 reduce-scatter.27
  2055.8 24.8 reduce-scatter.57
  2083.1 24.8 reduce-scatter.61
  2110.6 20.0 reduce-scatter.33
  2155.7 20.0 reduce-scatter.29
  (9 shorter events, 168.3 us)
where the time goes:
time: 2190 us; the launch traced here: 2180 us
  waiting for transfers between devices  1050 us (48%)
  matrix products  411 us (19%)
  blocking collectives  315 us (14%)
  local copies, waits for them, and re-layouts  244 us (11%)
  other arithmetic  115 us (5%)
  starting transfers between devices  30.3 us (1%)
    all_to_all x4, waiting for transfers between devices, heads_layout(): lax.all_to_all(stacked, 'row', split_axis=1, concat_axis=0, tiled=True)  241 us
    all_to_all x2, blocking collectives, tokens_layout(): lax.all_to_all(stacked, 'row', split_axis=0, concat_axis=2, tiled=True)  184 us
    all_to_all x2, waiting for transfers between devices, tokens_layout(): lax.all_to_all(stacked, 'row', split_axis=0, concat_axis=2, tiled=True)  134 us
    dot_general x16, matrix products, causal_scores(): jnp.einsum('qhd,khd->hqk', query_clip, key_clip, preferred_element_type=j...  86.6 us
    dot_general x10, matrix products, by_transposed(): lax.dot_general(left, right, (((1,), (1,)), ((), ())), preferred_element_...  71.4 us
    reduce_scatter x1, waiting for transfers between devices, spread(): lax.psum_scatter(grads[2].astype(jnp.bfloat16), 'row', scatter_dimension=...  70.4 us
    reduce_scatter x1, waiting for transfers between devices, spread(): lax.psum_scatter(grads[1].astype(jnp.bfloat16), 'row', scatter_dimension=...  70.2 us
    reduce_scatter x1, waiting for transfers between devices, spread(): lax.psum_scatter(grads[0].astype(jnp.bfloat16), 'row', scatter_dimension=...  69.9 us
  transfers between devices with their start and end apart: 39, of which 26 were waited for; matrix products, arithmetic and copies ran while one was open for 32% of the time, Pallas kernels for 0%

commit v1 on v0

--- a/solution.py
+++ b/solution.py
@@ -1,8 +1,11 @@
+import functools
 from functools import partial
 
 import jax
 import jax.numpy as jnp
 from jax import lax
+from jax.experimental import pallas as pl
+from jax.experimental.pallas import tpu as pltpu
 from jax.sharding import PartitionSpec as P
 
 HEADS = 16
@@ -207,7 +210,7 @@
     return lax.map(one_clip, (query_clips, key_clips, value_clips, log_sums, grad_clips))
 
 
-def local(
+def general(
     frames_in,
     text_states,
     self_query,
@@ -433,6 +436,517 @@
     )
 
 
+NT=(((1,),(1,)),((),())); NN=(((1,),(0,)),((),())); TN=(((0,),(0,)),((),()))
+def dg(a,b,dims): return lax.dot_general(a,b,dims,preferred_element_type=jnp.float32)
+
+def attend_kernel(causal,tile,q_ref,k_ref,v_ref,o_ref,lse_ref):
+    pair=pl.program_id(0)
+    rows=q_ref.shape[0]
+    low=lax.broadcasted_iota(jnp.int32,(1,128),1)<HEAD_DIM
+    lane=lax.broadcasted_iota(jnp.int32,(1,128),1)
+    value=v_ref[...]
+    ones=jnp.ones_like(value)
+    @pl.when(pair==0)
+    def _(): lse_ref[...]=jnp.zeros_like(lse_ref)
+    for start in range(0,rows,tile):
+        n=min(tile,rows-start)
+        q=q_ref[start:start+n,:]*jnp.bfloat16(HEAD_DIM**-0.5)
+        mixed=[]; sums=[]
+        lse=lse_ref[start:start+n,:]
+        for h in range(2):
+            mine=low if h==0 else jnp.logical_not(low)
+            qh=jnp.where(mine,q,jnp.bfloat16(0))
+            vh=jnp.where(mine,value,ones)
+            if causal:
+                spans=([(0,start)] if start else [])+[(start,n)]
+            else: spans=[(0,k_ref.shape[0])]
+            scores=[]
+            for at,length in spans:
+                s=dg(qh,k_ref[at:at+length,:],NT)
+                if causal and at==start:
+                    ok=lax.broadcasted_iota(jnp.int32,s.shape,0)>=lax.broadcasted_iota(jnp.int32,s.shape,1)
+                    s=jnp.where(ok,s,-1e30)
+                scores.append(s)
+            top=functools.reduce(jnp.maximum,[jnp.max(s,axis=1,keepdims=True) for s in scores])
+            out=None
+            for (at,length),s in zip(spans,scores):
+                p=jnp.exp(s-top).astype(jnp.bfloat16)
+                part=dg(p,vh[at:at+length,:],NN)
+                out=part if out is None else out+part
+            total=out[:,HEAD_DIM:HEAD_DIM+1] if h==0 else out[:,0:1]
+            mixed.append(out/total)
+            lse=jnp.where(lane==2*pair+h,top+jnp.log(total),lse)
+        lse_ref[start:start+n,:]=lse
+        o_ref[start:start+n,:]=jnp.where(low,mixed[0],mixed[1]).astype(o_ref.dtype)
+
+def attend(q,k,v,causal,out_dtype,tile=256):
+    rows,width=q.shape; keys=k.shape[0]
+    return pl.pallas_call(functools.partial(attend_kernel,causal,tile),grid=(width//128,),
+        in_specs=[pl.BlockSpec((rows,128),lambda i:(0,i)),pl.BlockSpec((keys,128),lambda i:(0,i)),pl.BlockSpec((keys,128),lambda i:(0,i))],
+        out_specs=[pl.BlockSpec((rows,128),lambda i:(0,i)),pl.BlockSpec((rows,128),lambda i:(0,0))],
+        out_shape=[jax.ShapeDtypeStruct((rows,width),out_dtype),jax.ShapeDtypeStruct((rows,128),jnp.float32)],
+        compiler_params=pltpu.CompilerParams(vmem_limit_bytes=40<<20),
+        cost_estimate=pl.CostEstimate(flops=4*rows*keys*width,bytes_accessed=8*rows*width,transcendentals=rows*keys*width//64))(q,k,v)
+
+def attend_back_kernel(causal,tile,q_ref,k_ref,v_ref,do_ref,st_ref,dq_ref,dk_ref,dv_ref,acc):
+    rows=q_ref.shape[0]; keys=k_ref.shape[0]
+    low=lax.broadcasted_iota(jnp.int32,(1,128),1)<HEAD_DIM
+    acc[...]=jnp.zeros_like(acc)
+    for start in range(0,keys,tile):
+        n=min(tile,keys-start)
+        k=k_ref[start:start+n,:]*jnp.bfloat16(HEAD_DIM**-0.5)
+        v=v_ref[start:start+n,:]
+        spans=[(0,rows)]
+        if causal: spans=[(start,n)]+([(start+n,rows-start-n)] if start+n<rows else [])
+        dks=[];dvs=[]
+        for h in range(2):
+            mine=low if h==0 else jnp.logical_not(low)
+            kh=jnp.where(mine,k,jnp.bfloat16(0)); vh=jnp.where(mine,v,jnp.bfloat16(0))
+            dk=dv=None
+            for at,length in spans:
+                qs=q_ref[at:at+length,:]; do=do_ref[at:at+length,:]
+                s=dg(kh,qs,NT)
+                p=jnp.exp(s-st_ref[0,h:h+1,at:at+length])
+                if causal and at==start:
+                    ok=lax.broadcasted_iota(jnp.int32,s.shape,0)<=lax.broadcasted_iota(jnp.int32,s.shape,1)
+                    p=jnp.where(ok,p,0.0)
+                dp=dg(vh,do,NT)
+                ds=(p*(dp-st_ref[0,2+h:3+h,at:at+length])).astype(jnp.bfloat16)
+                a=dg(p.astype(jnp.bfloat16),do,NN); b=dg(ds,qs,NN)
+                dv=a if dv is None else dv+a
+                dk=b if dk is None else dk+b
+                acc[at:at+length,:]+=dg(ds,kh,TN)
+            dks.append(dk);dvs.append(dv)
+        dk_ref[start:start+n,:]=(jnp.where(low,dks[0],dks[1])*HEAD_DIM**-0.5).astype(dk_ref.dtype)
+        dv_ref[start:start+n,:]=jnp.where(low,dvs[0],dvs[1]).astype(dv_ref.dtype)
+    dq_ref[...]=acc[...].astype(dq_ref.dtype)
+
+def attend_back(q,k,v,do,stats,causal,out_dtype,tile=256):
+    rows,width=q.shape; keys=k.shape[0]
+    bq=pl.BlockSpec((rows,128),lambda i:(0,i)); bk=pl.BlockSpec((keys,128),lambda i:(0,i))
+    return pl.pallas_call(functools.partial(attend_back_kernel,causal,tile),grid=(width//128,),
+        in_specs=[bq,bk,bk,bq,pl.BlockSpec((1,4,rows),lambda i:(i,0,0))],out_specs=[bq,bk,bk],
+        out_shape=[jax.ShapeDtypeStruct((rows,width),out_dtype),jax.ShapeDtypeStruct((keys,width),out_dtype),jax.ShapeDtypeStruct((keys,width),out_dtype)],
+        scratch_shapes=[pltpu.VMEM((rows,128),jnp.float32)],
+        compiler_params=pltpu.CompilerParams(vmem_limit_bytes=40<<20),
+        cost_estimate=pl.CostEstimate(flops=10*rows*keys*width,bytes_accessed=16*rows*width,transcendentals=rows*keys*width//64))(q,k,v,do,stats)
+
+def feed_kernel(h_ref,cot_ref,res_ref,up_ref,down_ref,out_ref,g_ref,dup_ref,ddown_ref,acc):
+    i=pl.program_id(0)
+    @pl.when(i==0)
+    def _():
+        acc[...]=res_ref[...]
+        g_ref[...]=jnp.zeros_like(g_ref)
+    h=h_ref[...]; cot=cot_ref[...]
+    pre=dg(h,up_ref[...],NN)
+    cdf=0.5*(1.0+lax.erf(pre*0.7071067811865476))
+    inner=(pre*cdf).astype(jnp.bfloat16)
+    acc[...]+=dg(inner,down_ref[...],NN)
+    ddown_ref[...]=dg(inner,cot,TN).astype(ddown_ref.dtype)
+    slope=cdf+pre*(jnp.exp(-0.5*pre*pre)*0.3989422804014327)
+    gpre=(dg(cot,down_ref[...],NT)*slope).astype(jnp.bfloat16)
+    dup_ref[...]=dg(h,gpre,TN).astype(dup_ref.dtype)
+    g_ref[...]+=dg(gpre,up_ref[...],NT)
+    @pl.when(i==pl.num_programs(0)-1)
+    def _(): out_ref[...]=acc[...].astype(out_ref.dtype)
+
+def feed(h,cot,res,up,down,chunk=512):
+    rows,d=h.shape; ff=up.shape[1]
+    whole=pl.BlockSpec((rows,d),lambda i:(0,0))
+    return pl.pallas_call(feed_kernel,grid=(ff//chunk,),
+        in_specs=[whole,whole,whole,pl.BlockSpec((d,chunk),lambda i:(0,i)),pl.BlockSpec((chunk,d),lambda i:(i,0))],
+        out_specs=[whole,whole,pl.BlockSpec((d,chunk),lambda i:(0,i)),pl.BlockSpec((chunk,d),lambda i:(i,0))],
+        out_shape=[jax.ShapeDtypeStruct((rows,d),jnp.bfloat16),jax.ShapeDtypeStruct((rows,d),jnp.float32),jax.ShapeDtypeStruct((d,ff),jnp.bfloat16),jax.ShapeDtypeStruct((ff,d),jnp.bfloat16)],
+        scratch_shapes=[pltpu.VMEM((rows,d),jnp.float32)],
+        compiler_params=pltpu.CompilerParams(vmem_limit_bytes=56<<20),
+        cost_estimate=pl.CostEstimate(flops=12*rows*d*ff,bytes_accessed=8*d*ff+16*rows*d,transcendentals=2*rows*ff))(h,cot,res,up,down)
+
+
+MESH = pl.DeviceIdType.MESH
+ORDERS = ("xzy", "yzx", "xzy", "yzx", "zxy", "zyx")
+
+
+class Place:
+    def __init__(self):
+        row, col = lax.axis_index("row"), lax.axis_index("col")
+        self.z, self.y, self.x, self.k = row // 2, row % 2, col // 2, col % 2
+        self.along = lax.axis_size("row") // 2
+
+    def device(self, dz=0, y=False, x=False, k=False):
+        other_y = 1 - self.y if y else self.y
+        other_x = 1 - self.x if x else self.x
+        other_k = 1 - self.k if k else self.k
+        return ((self.z + dz) * 2 + other_y, other_x * 2 + other_k)
+
+    def across(self, axis):
+        return self.device(y=axis == "y", x=axis == "x", k=axis == "k")
+
+    def greet(self):
+        barrier = pltpu.get_barrier_semaphore()
+        for axis in "xyk":
+            pl.semaphore_signal(barrier, inc=1, device_id=self.across(axis), device_id_type=MESH)
+
+        @pl.when(self.z > 0)
+        def _():
+            pl.semaphore_signal(barrier, inc=1, device_id=self.device(dz=-1), device_id_type=MESH)
+
+        @pl.when(self.z + 1 < self.along)
+        def _():
+            pl.semaphore_signal(barrier, inc=1, device_id=self.device(dz=1), device_id_type=MESH)
+
+        below = jnp.where(self.z > 0, 1, 0)
+        above = jnp.where(self.z + 1 < self.along, 1, 0)
+        pl.semaphore_wait(barrier, 3 + below + above)
+
+
+def when(condition, run):
+    if condition is None:
+        run()
+    else:
+        pl.when(condition)(run)
+
+
+class Gather:
+    def __init__(self, place, block, full, strip, order, send, recv):
+        self.place, self.block, self.full, self.strip = place, block, full, strip
+        turn = order.index("z")
+        self.before, self.after = order[:turn], order[turn + 1 :]
+        self.send, self.recv, self.used, self.sent, self.started = send, recv, 0, 0, []
+
+    def region(self, z, y, x):
+        part, start, count = self.strip
+        column = (x * 2 + self.place.k) * self.block.shape[-1] + start
+        return self.full.at[z, y, part, :, pl.ds(pl.multiple_of(column, 128), count)]
+
+    def held(self, done, z):
+        y = slice(None) if "y" in done else self.place.y
+        return [self.region(z, y, x) for x in (range(2) if "x" in done else [self.place.x])]
+
+    def pairs(self, done, z, first):
+        if first:
+            part, start, count = self.strip
+            place = self.place
+            return [(self.block.at[part, :, pl.ds(start, count)], self.region(place.z, place.y, place.x))]
+        return [(region, region) for region in self.held(done, z)]
+
+    def semaphore(self):
+        self.used += 2
+        return self.used - 2
+
+    def copies(self, device, pairs, semaphore, send=0):
+        return [
+            pltpu.make_async_remote_copy(
+                src_ref=source, dst_ref=target, send_sem=self.send.at[send + at],
+                recv_sem=self.recv.at[semaphore + at], device_id=device, device_id_type=MESH)
+            for at, (source, target) in enumerate(pairs)
+        ]
+
+    def start(self, device, pairs, condition, semaphore):
+        copies = self.copies(device, pairs, semaphore, self.sent)
+        self.sent += len(copies)
+        when(condition, lambda: [copy.start() for copy in copies] and None)
+        self.started.append((condition, copies))
+        return condition, copies
+
+    def arrive(self, sent):
+        condition, copies = sent
+        when(condition, lambda: [copy.wait_recv() for copy in copies] and None)
+
+    def stages(self):
+        place, along = self.place, self.place.along
+        done = []
+        for axis in self.before:
+            sent = self.start(place.across(axis), self.pairs(done, place.z, not done), None, self.semaphore())
+            yield
+            self.arrive(sent)
+            done.append(axis)
+        first = not done
+        from_left = [self.semaphore() for _ in range(along - 1)]
+        from_right = [self.semaphore() for _ in range(along - 1)]
+
+        def pass_on(turn, step):
+            axes = done + list(self.after[:turn])
+            device = place.across(self.after[turn])
+            if step == 0:
+                return turn, step, [self.start(device, self.pairs(axes, place.z, not axes), None, self.semaphore())]
+            return turn, step, [
+                self.start(device, self.pairs(axes, z, False), (z >= 0) & (z < along), self.semaphore())
+                for z in (place.z - step, place.z + step)
+            ]
+
+        def step_out(step):
+            left, right = place.z - (step - 1), place.z + (step - 1)
+            self.start(place.device(dz=1), self.pairs(done, left, first and step == 1),
+                       (left >= 0) & (place.z + 1 < along), from_left[step - 1])
+            self.start(place.device(dz=-1), self.pairs(done, right, first and step == 1),
+                       (right < along) & (place.z > 0), from_right[step - 1])
+
+        def step_in(step):
+            for z, semaphore in ((place.z - step, from_left), (place.z + step, from_right)):
+                copies = self.copies(place.across("k"), self.pairs(done, z, False), semaphore[step - 1])
+                self.arrive(((z >= 0) & (z < along), copies))
+
+        step_out(1)
+        waiting = [pass_on(0, 0)] if self.after else []
+        for step in range(1, along + len(self.after)):
+            yield
+            if step < along:
+                step_in(step)
+                if step + 1 < along:
+                    step_out(step + 1)
+            following = []
+            for turn, at, sent in waiting:
+                for one in sent:
+                    self.arrive(one)
+                if turn + 1 < len(self.after):
+                    following.append(pass_on(turn + 1, at))
+            if self.after and step < along:
+                following.append(pass_on(0, step))
+            waiting = following
+        everything = [self.region(slice(None), slice(None), x) for x in range(2)]
+        sent = self.start(place.across("k"), [(r, r) for r in everything], None, self.semaphore())
+        yield
+        self.arrive(sent)
+
+    def finish(self):
+        for condition, copies in self.started:
+            when(condition, lambda copies=copies: [copy.wait_send() for copy in copies] and None)
+
+
+def gather_kernel(units, count, *refs):
+    blocks, fulls = refs[:count], refs[count : 2 * count]
+    send, recv, local_sem = refs[2 * count :]
+    place = Place()
+    place.greet()
+    own = []
+    for at, (block, full) in enumerate(zip(blocks, fulls)):
+        width = block.shape[-1]
+        columns = pl.ds(pl.multiple_of((place.x * 2 + place.k) * width, 128), width)
+        copy = pltpu.make_async_copy(block, full.at[place.z, place.y, :, :, columns], local_sem.at[at])
+        copy.start()
+        own.append(copy)
+    gathers = [
+        Gather(place, blocks[which], fulls[which], strip, order, send.at[at], recv.at[at])
+        for at, (which, strip, order) in enumerate(units)
+    ]
+    running = [gather.stages() for gather in gathers]
+    while running:
+        running = [stages for stages in running if next(stages, running) is not running]
+        while own:
+            own.pop().wait()
+    for gather in gathers:
+        gather.finish()
+
+
+def gather_units(blocks, least):
+    strips = []
+    for which, block in enumerate(blocks):
+        wide = min(least, block.shape[-1])
+        for part in range(block.shape[0]):
+            for start in range(0, block.shape[-1], wide):
+                strips.append((which, (part, start, wide)))
+    return [strip + (ORDERS[at % len(ORDERS)],) for at, strip in enumerate(strips)]
+
+
+def gather_blocks(blocks, collective_id, least):
+    along, cols = lax.axis_size("row") // 2, lax.axis_size("col")
+    units = gather_units(blocks, least)
+    count = len(blocks)
+    anywhere = pl.BlockSpec(memory_space=pl.ANY)
+    moved = sum(block.size for block in blocks) * 2 * along * 2 * cols
+    return pl.pallas_call(
+        functools.partial(gather_kernel, units, count),
+        out_shape=[
+            jax.ShapeDtypeStruct((along, 2) + b.shape[:2] + (cols * b.shape[2],), b.dtype) for b in blocks
+        ],
+        in_specs=[anywhere] * count,
+        out_specs=[anywhere] * count,
+        scratch_shapes=[
+            pltpu.SemaphoreType.DMA((len(units), 8 * along)),
+            pltpu.SemaphoreType.DMA((len(units), 12 * along)),
+            pltpu.SemaphoreType.DMA((count,)),
+        ],
+        compiler_params=pltpu.CompilerParams(collective_id=collective_id, has_side_effects=True),
+        cost_estimate=pl.CostEstimate(flops=0, bytes_accessed=2 * moved, transcendentals=0),
+    )(*blocks)
+
+
+class Scatter:
+    def __init__(self, place, grad, out, strip, width, order, slots, send, recv, local):
+        self.place, self.grad, self.out, self.strip, self.width = place, grad, out, strip, width
+        self.order = order[::-1]
+        self.slots, self.send, self.recv, self.local = slots, send, recv, local
+        self.sent, self.used, self.started = 0, 0, []
+
+    def columns(self, x, k):
+        return pl.ds(pl.multiple_of((x * 2 + k) * self.width + self.strip[1], 128), self.strip[2])
+
+
+def fast(
+    frames_in, text_states, self_query, self_key, self_value, self_output, cross_query, cross_key, cross_value, cross_output,
+    up_weight, down_weight, first_gain, first_bias, second_gain, second_bias, third_gain, third_bias, cotangent,
+):
+    row = lax.axis_index("row")
+    rows, width = frames_in.shape
+    half = width // 2
+    piece = first_gain.shape[0]
+    block_rows, block_cols = self_query.shape
+    back = row % 2
+    pairs = lax.axis_size("row") // 2
+    forth_perm = [(2 * i, 2 * i + 1) for i in range(pairs)]
+    back_perm = [(2 * i + 1, 2 * i) for i in range(pairs)]
+    swap = forth_perm + back_perm
+
+    def forth(array):
+        return lax.ppermute(array, "row", forth_perm)
+
+    def home(array):
+        return lax.ppermute(array, "row", back_perm)
+
+    def by_side(first, second):
+        return jnp.where(back == 0, first, second)
+
+    gains = jnp.zeros((1, 16, 128), jnp.bfloat16)
+    gains = gains.at[0, :6, :piece].set(
+        jnp.stack([first_gain, first_bias, second_gain, second_bias, third_gain, third_bias])
+    )
+
+    def small(block):
+        return block.reshape(1, block_rows, block_cols)
+
+    def flat(array):
+        return array.reshape(-1, array.shape[-1])
+
+    early = gather_blocks([small(self_query), small(self_key), small(self_value), gains], 1, 128)
+    query_self, key_self, value_self = [flat(w) for w in early[:3]]
+    late = gather_blocks(
+        [small(self_output), small(cross_query), small(cross_key), small(cross_value), small(cross_output),
+         up_weight.reshape(1, *up_weight.shape), down_weight.reshape(-1, block_rows, block_cols)], 2, 256)
+    out_self, query_cross, key_cross, value_cross, out_cross, up_full, down_full = [flat(w) for w in late]
+    norm_params = early[3].reshape(pairs * 2, 16, -1, 128)[:, :6, :, :piece].transpose(1, 0, 2, 3)
+    norm_params = norm_params.reshape(6, width).astype(jnp.float32)
+
+    frames = frames_in.astype(jnp.float32)
+    hidden_one = norm_forward(frames, norm_params[0], norm_params[1]).astype(jnp.bfloat16)
+    self_k = matmul(hidden_one, key_self).astype(jnp.bfloat16)
+    self_v = matmul(hidden_one, value_self).astype(jnp.bfloat16)
+    self_q = matmul(hidden_one, query_self).astype(jnp.bfloat16)
+    sent_k, sent_v, sent_q = forth(self_k[:, :half]), forth(self_v[:, :half]), home(self_q[:, half:])
+    near_mix, near_logs = attend(self_q, self_k, self_v, True, jnp.float32)
+    far_q = by_side(sent_q, self_q[:, :half])
+    far_k = by_side(self_k[:, half:], sent_k)
+    far_v = by_side(self_v[:, half:], sent_v)
+    far_mix, far_logs = attend(far_q, far_k, far_v, False, jnp.bfloat16)
+    half_heads = half // HEAD_DIM
+    far_logs = far_logs[:, :half_heads]
+    near_logs = near_logs[:, : 2 * half_heads]
+    far_mix = jnp.concatenate([far_mix, forth(far_mix)], axis=1)
+    far_logs = by_side(-1e30, jnp.concatenate([far_logs, forth(far_logs)], axis=1))
+    highest = jnp.maximum(near_logs, far_logs)
+    self_logs = highest + jnp.log(jnp.exp(near_logs - highest) + jnp.exp(far_logs - highest))
+
+    def per_feature(weights):
+        return jnp.repeat(weights, HEAD_DIM, axis=1)
+
+    self_mix = (
+        near_mix * per_feature(jnp.exp(near_logs - self_logs))
+        + by_side(0.0, far_mix.astype(jnp.float32)) * per_feature(jnp.exp(far_logs - self_logs))
+    ).astype(jnp.bfloat16)
+    resid_one = frames + matmul(self_mix, out_self)
+    hidden_two = norm_forward(resid_one, norm_params[2], norm_params[3]).astype(jnp.bfloat16)
+    cross_q = matmul(hidden_two, query_cross).astype(jnp.bfloat16)
+    other_text = lax.ppermute(text_states, "row", swap)
+    clip_text = by_side(
+        jnp.concatenate([text_states, other_text]), jnp.concatenate([other_text, text_states])
+    )
+    text_k = matmul(clip_text, key_cross).astype(jnp.bfloat16)
+    text_v = matmul(clip_text, value_cross).astype(jnp.bfloat16)
+    cross_mix, cross_logs = attend(cross_q, text_k, text_v, False, jnp.bfloat16)
+    cross_logs = cross_logs[:, : 2 * half_heads]
+    resid_two = resid_one + matmul(cross_mix, out_cross)
+    hidden_three = norm_forward(resid_two, norm_params[4], norm_params[5]).astype(jnp.bfloat16)
+    layer_out, grad_three, up_grad, down_grad = feed(hidden_three, cotangent, resid_two, up_full, down_full)
+
+    def stats_of(logs, mix, grad):
+        products = mix.astype(jnp.float32) * grad.astype(jnp.float32)
+        dots = jnp.sum(products.reshape(rows, -1, HEAD_DIM), axis=-1)
+        both = jnp.stack([logs.T.reshape(-1, 2, rows), dots.T.reshape(-1, 2, rows)], axis=1)
+        return both.reshape(-1, 4, rows)
+
+    cotan_full = cotangent.astype(jnp.float32)
+    unused_three, pull_three = jax.vjp(norm_forward, resid_two, norm_params[4], norm_params[5])
+    through_three, third_gain_part, third_bias_part = pull_three(grad_three)
+    grad_resid_two = cotan_full + through_three
+    grad_cross = grad_resid_two.astype(jnp.bfloat16)
+    cross_out_grad = over_tokens(cross_mix, grad_cross)
+    grad_cross_mix = by_transposed(grad_cross, out_cross).astype(jnp.bfloat16)
+    grad_cross_q, text_k_part, text_v_part = attend_back(
+        cross_q, text_k, text_v, grad_cross_mix, stats_of(cross_logs, cross_mix, grad_cross_mix), False, jnp.bfloat16)
+    text_rows = text_states.shape[0]
+    text_parts = jnp.concatenate([text_k_part, text_v_part], axis=1)
+    given = lax.ppermute(by_side(text_parts[text_rows:], text_parts[:text_rows]), "row", swap)
+    kept = by_side(text_parts[:text_rows], text_parts[text_rows:])
+    text_parts = (kept.astype(jnp.float32) + given.astype(jnp.float32)).astype(jnp.bfloat16)
+    grad_text_k, grad_text_v = text_parts[:, :width], text_parts[:, width:]
+    cross_query_part = over_tokens(hidden_two, grad_cross_q)
+    cross_key_part = over_tokens(text_states, grad_text_k)
+    cross_value_part = over_tokens(text_states, grad_text_v)
+    text_grad = by_transposed(grad_text_k, key_cross) + by_transposed(grad_text_v, value_cross)
+    grad_two = by_transposed(grad_cross_q, query_cross)
+    unused_two, pull_two = jax.vjp(norm_forward, resid_one, norm_params[2], norm_params[3])
+    through_two, second_gain_part, second_bias_part = pull_two(grad_two)
+    grad_resid_one = grad_resid_two + through_two
+    grad_self = grad_resid_one.astype(jnp.bfloat16)
+    self_out_grad = over_tokens(self_mix, grad_self)
+    grad_self_mix = by_transposed(grad_self, out_self).astype(jnp.bfloat16)
+    stats = stats_of(self_logs, self_mix, grad_self_mix)
+    far_pairs = half // 128
+    sent_grad, sent_stats = home(grad_self_mix[:, half:]), home(stats[far_pairs:])
+    near_dq, near_dk, near_dv = attend_back(self_q, self_k, self_v, grad_self_mix, stats, True, jnp.float32)
+    far_grad = by_side(sent_grad, grad_self_mix[:, :half])
+    far_stats = by_side(sent_stats, stats[:far_pairs])
+    far_dq, far_dk, far_dv = attend_back(far_q, far_k, far_v, far_grad, far_stats, False, jnp.bfloat16)
+    got_dq, got_dk, got_dv = forth(far_dq), home(far_dk), home(far_dv)
+
+    def with_far(near, lower, upper):
+        return (near + jnp.concatenate([lower, upper], axis=1).astype(jnp.float32)).astype(jnp.bfloat16)
+
+    none = jnp.zeros_like(far_dq)
+    grad_self_q = with_far(near_dq, by_side(none, far_dq), got_dq)
+    grad_self_k = with_far(near_dk, got_dk, by_side(far_dk, none))
+    grad_self_v = with_far(near_dv, got_dv, by_side(far_dv, none))
+    self_query_part = over_tokens(hidden_one, grad_self_q)
+    self_key_part = over_tokens(hidden_one, grad_self_k)
+    self_value_part = over_tokens(hidden_one, grad_self_v)
+    grad_one = (
+        by_transposed(grad_self_q, query_self)
+        + by_transposed(grad_self_k, key_self)
+        + by_transposed(grad_self_v, value_self)
+    )
+    unused_one, pull_one = jax.vjp(norm_forward, frames, norm_params[0], norm_params[1])
+    through_one, first_gain_part, first_bias_part = pull_one(grad_one)
+    input_grad = grad_resid_one + through_one
+    norm_grads = jnp.stack(
+        [first_gain_part, first_bias_part, second_gain_part, second_bias_part, third_gain_part, third_bias_part]
+    )
+    col_count = lax.axis_size("col")
+    norm_grads = norm_grads.reshape(6, 2 * pairs, col_count, piece).transpose(1, 2, 0, 3)
+    norm_grads = norm_grads.reshape(2 * pairs, col_count * 6 * piece)
+    summed = spread(
+        (self_query_part, self_key_part, self_value_part, self_out_grad, cross_query_part, cross_key_part,
+         cross_value_part, cross_out_grad, up_grad, down_grad, norm_grads))
+    norm_parts = summed[10].reshape(6, piece)
+    return (layer_out, input_grad, text_grad, *summed[:10], *norm_parts)
+
+
+def local(*arrays):
+    frames_in, self_query = arrays[0], arrays[2]
+    halves = 2 * frames_in.shape[0] == FRAMES and lax.axis_size("row") % 2 == 0
+    if halves and lax.axis_size("col") % 2 == 0 and self_query.shape[1] % 256 == 0 and self_query.shape[0] % 128 == 0:
+        return fast(*arrays)
+    return general(*arrays)
+
+
 def solution(mesh):
     placed = (
         P(("col", "row"), None),

time: 2190 us -> 1520 us (0.69)
  matrix products: 411 us -> 73 us
  Pallas kernels: 0 us -> 338 us
  blocking collectives: 315 us -> 35.8 us
  local copies, waits for them, and re-layouts: 244 us -> 68.7 us
  waiting for transfers between devices: 1050 us -> 907 us
  other arithmetic: 115 us -> 48.5 us
    all_to_all x6 -> x0, waiting for transfers between devices: 375 us -> none  [the longest x4 241 us: heads_layout(): lax.all_to_all(stacked, 'row', split_axis=1, concat_axis=0, tiled=True)]
    pallas_call x0 -> x9, Pallas kernels: none -> 338 us  [the longest x2 192 us: gather_blocks(): pl.pallas_call(functools.partial(gather_kernel, units, count), out_shape=...]
    dot_general x56 -> x0, matrix products: 231 us -> none  [the longest x16 86.6 us: causal_scores(): jnp.einsum('qhd,khd->hqk', query_clip, key_clip, preferred_element_type=j...]
    all_to_all x2 -> x0, blocking collectives: 184 us -> none  [tokens_layout(): lax.all_to_all(stacked, 'row', split_axis=0, concat_axis=2, tiled=True)]
    all_gather x12 -> x0, waiting for transfers between devices: 183 us -> none  [the longest x1 47.9 us: collect(): lax.all_gather(partly[2], 'row', axis=0, tiled=True)]
    reduce_scatter x1, waiting for transfers between devices: 0.02 us -> 152 us  [spread(): lax.psum_scatter(grads[8].astype(jnp.bfloat16), 'row', scatter_dimension=...]
    reduce_scatter x1, waiting for transfers between devices: 57.5 us -> 152 us  [spread(): lax.psum_scatter(grads[9].astype(jnp.bfloat16), 'row', scatter_dimension=...]
    all_gather x9 -> x0, blocking collectives: 88 us -> none  [the longest x1 31 us: collect(): lax.all_gather(partly[10], 'row', axis=0, tiled=True)]
  transfers between devices with their start and end apart: 39 -> 33, of which waited for: 26 -> 24; matrix products, arithmetic and copies ran while one was open for 32% -> 9% of each run, Pallas kernels for 0% -> 18%
where the time goes in v1:
time: 1520 us; the launch traced here: 1510 us
  waiting for transfers between devices  907 us (60%)
  Pallas kernels  338 us (22%)
  matrix products  73 us (5%)
  local copies, waits for them, and re-layouts  68.7 us (5%)
  other arithmetic  48.5 us (3%)
  blocking collectives  35.8 us (2%)
  starting transfers between devices  27.5 us (2%)
  between operations  16.4 us (1%)
    pallas_call x2, Pallas kernels, gather_blocks(): pl.pallas_call(functools.partial(gather_kernel, units, count), out_shape=...  192 us
    reduce_scatter x1, waiting for transfers between devices, spread(): lax.psum_scatter(grads[8].astype(jnp.bfloat16), 'row', scatter_dimension=...  152 us
    reduce_scatter x1, waiting for transfers between devices, spread(): lax.psum_scatter(grads[9].astype(jnp.bfloat16), 'row', scatter_dimension=...  152 us
    unnamed x24, waiting for transfers between devices  101 us
    reduce_scatter x1, waiting for transfers between devices, spread(): lax.psum_scatter(grads[1].astype(jnp.bfloat16), 'row', scatter_dimension=...  70.1 us
    reduce_scatter x1, waiting for transfers between devices, spread(): lax.psum_scatter(grads[2].astype(jnp.bfloat16), 'row', scatter_dimension=...  70.1 us
    reduce_scatter x1, waiting for transfers between devices, spread(): lax.psum_scatter(grads[0].astype(jnp.bfloat16), 'row', scatter_dimension=...  68.2 us
    ppermute x5, waiting for transfers between devices, home(): return lax.ppermute(array, 'row', back_perm)  62.5 us
  transfers between devices with their start and end apart: 33, of which 24 were waited for; matrix products, arithmetic and copies ran while one was open for 9% of the time, Pallas kernels for 18%

profile of v1, /device:TPU:0, one launch (start us, length us, event | category | flops | bytes accessed | tf_op | source)
XLA Modules:
  0.0 1514.7 jit_solution(5474640306905739277)
XLA Ops:
  14.7 44.2 %shard_map.330 = (bf16[4,2,1,128,1024]{4,3,2,1,0:T(8,128)(2,1)}, bf16[4,2,1,128,1024]{4,3,2,1,0:T(8,128)(2,1)}, bf16[4,2,1,128,1024]{4,3,2,1,0:T(8,128)(2,1)}, bf16[4,2,1,16,512]{4,3,2,1,0:T(8,128)(2,1)}) custom-call(bf16[1,128,256]{2,1,0:T(8,128)(2,1)} %bitcast.128, bf16[1,128,256]{2,1,0:T(8,128)(2,1)} %bitcast.129, bf16[1,128,256]{2,1,0:T(8,128)(2,1)} %bitcast.130, ...), custom_call_target="tpu_custom_call" | custom-call | bytes 12845056 | tf_op jit(solution)/shard_map/pallas_call | solution.py:757
  77.4 19.9 %shard_map.331 = (f32[750,1024]{1,0:T(8,128)S(1)}, f32[750,128]{1,0:T(8,128)S(1)}) custom-call(bf16[750,1024]{1,0:T(8,128)(2,1)S(1)} %convolution_convert_fusion.11.q_ref, bf16[750,1024]{1,0:T(8,128)(2,1)S(1)} %convolution_convert_fusion.10.k_ref, bf16[750,1024]{1,0:T(8,128)(2,1)S(1)} %convolution_convert_fusion.9.v_ref), custom_call_target="tpu_custom_call" | custom-call | flops 2304000000 | bytes 6144000 | tf_op jit(solution)/shard_map/pallas_call | solution.py:484
  98.4 147.7 %shard_map.333 = (bf16[4,2,1,128,1024]{4,3,2,1,0:T(8,128)(2,1)}, bf16[4,2,1,128,1024]{4,3,2,1,0:T(8,128)(2,1)}, bf16[4,2,1,128,1024]{4,3,2,1,0:T(8,128)(2,1)}, b...) custom-call(bf16[1,128,256]{2,1,0:T(8,128)(2,1)} %bitcast.131, ...), custom_call_target="tpu_custom_call" | custom-call | bytes 54525952 | tf_op jit(solution)/shard_map/pallas_call | solution.py:757
  320.0 49.1 %shard_map.335 = (bf16[750,1024]{1,0:T(8,128)(2,1)}, f32[750,1024]{1,0:T(8,128)}, bf16[1024,4096]{1,0:T(8,128)(2,1)}, bf16[4096,1024]{1,0:T(8,128)(2,1)}) custom-call(bf16[750,1024]{1,0:T(8,128)(2,1)} %add_convert_fusion.3.h_ref, bf16[750,1024]{1,0:T(8,128)(2,1)} %cot_ref.1, f32[750,1024]{1,0:T(8,128)} %copy-done.30, bf16[1024,4096]{1,0:T(8,128)(2,1)} %bitcast.145, ...), custom_call_target="tpu_custom_call" | custom-call | flops 37748736000 | bytes 45842432 | tf_op jit(solution)/shard_map/pallas_call | solution.py:556
  454.8 22.1 %collective-permute-done.7 = f32[4,4,750]{2,1,0:T(4,128)S(1)} collective-permute-done((f32[4,4,750]{2,1,0:T(4,128)S(1)}, f32[4,4,750]{2,1,0:T(4,128)S(1)}, u32[]{:S(2)}, u32[]{:S(2)}) %collective-permute-start.7) | collective-permute-done | bytes 48032 | tf_op jit(solution)/shard_map/ppermute | solution.py:804
  497.1 29.6 %shard_map.337 = (f32[750,1024]{1,0:T(8,128)S(1)}, f32[750,1024]{1,0:T(8,128)S(1)}, f32[750,1024]{1,0:T(8,128)}) custom-call(bf16[750,1024]{1,0:T(8,128)(2,1)S(1)} %copy-done.7, bf16[750,1024]{1,0:T(8,128)(2,1)S(1)} %copy-done.1, bf16[750,1024]{1,0:T(8,128)(2,1)S(1)} %copy-done.4, bf16[750,1024]{1,0:T(8,128)(2,1)S(1)} %get-tuple-element.224.do_ref, ...), custom_call_target="tpu_custom_call" | custom-call | flops 5760000000 | bytes 12288000 | tf_op jit(solution)/shard_map/pallas_call | solution.py:527
  535.2 21.1 %collective-permute-done.10 = bf16[750,512]{1,0:T(8,128)(2,1)S(1)} collective-permute-done((bf16[750,512]{1,0:T(8,128)(2,1)S(1)}, bf16[750,512]{1,0:T(8,128)(2,1)S(1)}, u32[]{:S(2)}, u32[]{:S(2)}) %collective-permute-start.10) | collective-permute-done | bytes 768032 | tf_op jit(solution)/shard_map/ppermute | solution.py:804
  607.1 35.8 %all-reduce.1 = bf16[8,768]{1,0:T(8,128)(2,1)S(1)} all-reduce(bf16[8,768]{1,0:T(8,128)(2,1)S(1)} %convert_element_type.242), channel_id=22, replica_groups=mesh['row'=8,'col'=4] {'row'}, use_global_device_ids=true, to_apply=%region_40.41.clone | all-reduce | flops 6144 | bytes 24576
  666.0 68.3 %reduce-scatter.66.cloned.1.call-done = bf16[128,1024]{1,0:T(8,128)(2,1)} async-done(((bf16[1024,1024]{1,0:T(8,128)(2,1)}), bf16[128,1024]{1,0:T(8,128)(2,1)}) %reduce-scatter.66.cloned.1.call-update) | async-done | bytes 262160
  736.2 68.2 %reduce-scatter.28.cloned.1.call-done = bf16[128,1024]{1,0:T(8,128)(2,1)} async-done(((bf16[1024,1024]{1,0:T(8,128)(2,1)}), bf16[128,1024]{1,0:T(8,128)(2,1)}) %reduce-scatter.28.cloned.1.call-update) | async-done | bytes 262160 | tf_op jit(solution)/shard_map/reduce_scatter | solution.py:70
  804.4 70.1 %reduce-scatter.36.cloned.1.call-done = bf16[128,1024]{1,0:T(8,128)(2,1)} async-done(((bf16[1024,1024]{1,0:T(8,128)(2,1)}), bf16[128,1024]{1,0:T(8,128)(2,1)}) %reduce-scatter.36.cloned.1.call-update) | async-done | bytes 262160 | tf_op jit(solution)/shard_map/reduce_scatter | solution.py:76
  874.6 70.1 %reduce-scatter.32.cloned.1.call-done = bf16[128,1024]{1,0:T(8,128)(2,1)} async-done(((bf16[1024,1024]{1,0:T(8,128)(2,1)}), bf16[128,1024]{1,0:T(8,128)(2,1)}) %reduce-scatter.32.cloned.1.call-update) | async-done | bytes 262160 | tf_op jit(solution)/shard_map/reduce_scatter | solution.py:73
  944.8 151.6 %reduce-scatter.60.cloned.1.call-done = bf16[512,1024]{1,0:T(8,128)(2,1)} async-done(((bf16[4096,1024]{1,0:T(8,128)(2,1)}), bf16[512,1024]{1,0:T(8,128)(2,1)}) %reduce-scatter.60.cloned.1.call-update) | async-done | bytes 1048592 | tf_op jit(solution)/shard_map/reduce_scatter | solution.py:97
  1096.4 151.9 %reduce-scatter.56.cloned.1.call-done = bf16[128,4096]{1,0:T(8,128)(2,1)} async-done(((bf16[1024,4096]{1,0:T(8,128)(2,1)}), bf16[128,4096]{1,0:T(8,128)(2,1)}) %reduce-scatter.56.cloned.1.call-update) | async-done | bytes 1048592 | tf_op jit(solution)/shard_map/reduce_scatter | solution.py:94
  1271.0 20.9 %reduce-scatter.54.cloned.1.call-done = bf16[128,256]{1,0:T(8,128)(2,1)} async-done(((bf16[128,1024]{1,0:T(8,128)(2,1)}), bf16[128,256]{1,0:T(8,128)(2,1)}) %reduce-scatter.54.cloned.1.call-update) | async-done | bytes 65552 | tf_op jit(solution)/shard_map/reduce_scatter | solution.py:126
  1293.4 21.2 %reduce-scatter.46.cloned.1.call-done = bf16[128,256]{1,0:T(8,128)(2,1)} async-done(((bf16[128,1024]{1,0:T(8,128)(2,1)}), bf16[128,256]{1,0:T(8,128)(2,1)}) %reduce-scatter.46.cloned.1.call-update) | async-done | bytes 65552 | tf_op jit(solution)/shard_map/reduce_scatter | solution.py:117
  1316.1 20.9 %reduce-scatter.42.cloned.1.call-done = bf16[128,256]{1,0:T(8,128)(2,1)} async-done(((bf16[128,1024]{1,0:T(8,128)(2,1)}), bf16[128,256]{1,0:T(8,128)(2,1)}) %reduce-scatter.42.cloned.1.call-update) | async-done | bytes 65552 | tf_op jit(solution)/shard_map/reduce_scatter | solution.py:114
  1338.5 21.6 %reduce-scatter.48.cloned.1.call-done = bf16[128,256]{0,1:T(8,128)(2,1)} async-done(((bf16[128,1024]{0,1:T(8,128)(2,1)}), bf16[128,256]{0,1:T(8,128)(2,1)}) %reduce-scatter.48.cloned.1.call-update) | async-done | bytes 65552 | tf_op jit(solution)/shard_map/reduce_scatter | solution.py:120
  1361.7 21.4 %reduce-scatter.50.cloned.1.call-done = bf16[128,256]{0,1:T(8,128)(2,1)} async-done(((bf16[128,1024]{0,1:T(8,128)(2,1)}), bf16[128,256]{0,1:T(8,128)(2,1)}) %reduce-scatter.50.cloned.1.call-update) | async-done | bytes 65552 | tf_op jit(solution)/shard_map/reduce_scatter | solution.py:123
  1384.7 20.9 %reduce-scatter.30.cloned.1.call-done = bf16[128,256]{1,0:T(8,128)(2,1)} async-done(((bf16[128,1024]{1,0:T(8,128)(2,1)}), bf16[128,256]{1,0:T(8,128)(2,1)}) %reduce-scatter.30.cloned.1.call-update) | async-done | bytes 65552 | tf_op jit(solution)/shard_map/reduce_scatter | solution.py:105
  1407.1 20.9 %reduce-scatter.38.cloned.1.call-done = bf16[128,256]{1,0:T(8,128)(2,1)} async-done(((bf16[128,1024]{1,0:T(8,128)(2,1)}), bf16[128,256]{1,0:T(8,128)(2,1)}) %reduce-scatter.38.cloned.1.call-update) | async-done | bytes 65552 | tf_op jit(solution)/shard_map/reduce_scatter | solution.py:111
  1429.5 21.2 %reduce-scatter.34.cloned.1.call-done = bf16[128,256]{1,0:T(8,128)(2,1)} async-done(((bf16[128,1024]{1,0:T(8,128)(2,1)}), bf16[128,256]{1,0:T(8,128)(2,1)}) %reduce-scatter.34.cloned.1.call-update) | async-done | bytes 65552 | tf_op jit(solution)/shard_map/reduce_scatter | solution.py:108
  1452.2 25.8 %reduce-scatter.62.cloned.1.call-done = bf16[512,256]{1,0:T(8,128)(2,1)} async-done(((bf16[512,1024]{1,0:T(8,128)(2,1)}), bf16[512,256]{1,0:T(8,128)(2,1)}) %reduce-scatter.62.cloned.1.call-update) | async-done | bytes 262160 | tf_op jit(solution)/shard_map/reduce_scatter | solution.py:132
  1479.8 25.9 %reduce-scatter.58.cloned.1.call-done = bf16[128,1024]{1,0:T(8,128)(2,1)} async-done(((bf16[128,4096]{1,0:T(8,128)(2,1)}), bf16[128,1024]{1,0:T(8,128)(2,1)}) %reduce-scatter.58.cloned.1.call-update) | async-done | bytes 262160 | tf_op jit(solution)/shard_map/reduce_scatter | solution.py:129
  (422 shorter events, 327.9 us)
Async XLA Ops:
  7.3 637.2 %reduce-scatter.52.cloned.1.call-start = ((), (), s32[]{:S(2)}) async-start(), calls=%async_computation.33 | async-start | bytes 2359296 | tf_op jit(solution)/shard_map/reduce_scatter | solution.py:91
  7.3 238.9 %collective-permute-start.5 = (bf16[32,1024]{1,0:T(8,128)(2,1)}, bf16[32,1024]{1,0:T(8,128)(2,1)S(1)}, u32[]{:S(2)}, u32[]{:S(2)}) collective-permute-start(bf16[32,1024]{1,0:T(8,128)(2,1)} %param.22), channel_id=1, source_target_pairs={{0,4},{8,12},{16,20},{24,28},{4,0},{12,8},{20,16},{28,24},{1,5},{9... | collective-permute-start | bytes 196616 | tf_op jit(solution)/shard_map/ppermute | solution.py:858
  64.7 183.8 %collective-permute-start.1 = (bf16[750,512]{1,0:T(8,128)(2,1)}, bf16[750,512]{1,0:T(8,128)(2,1)}, u32[]{:S(2)}, u32[]{:S(2)}) collective-permute-start(bf16[750,512]{1,0:T(8,128)(2,1)} %slice.152), channel_id=1, source_target_pairs={{0,4},{8,12},{16,20},{24,28},{1,5},{9,13},{17,21},{25,29},{2,6},{1... | collective-permute-start | bytes 2304008 | tf_op jit(solution)/shard_map/ppermute | solution.py:801
  70.9 178.8 %collective-permute-start.2 = (bf16[750,512]{1,0:T(8,128)(2,1)}, bf16[750,512]{1,0:T(8,128)(2,1)}, u32[]{:S(2)}, u32[]{:S(2)}) collective-permute-start(bf16[750,512]{1,0:T(8,128)(2,1)} %slice.154), channel_id=1, source_target_pairs={{0,4},{8,12},{16,20},{24,28},{1,5},{9,13},{17,21},{25,29},{2,6},{1... | collective-permute-start | bytes 2304008 | tf_op jit(solution)/shard_map/ppermute | solution.py:801
  379.8 265.3 %reduce-scatter.44.cloned.1.call-start = ((), (), s32[]{:S(2)}) async-start(), calls=%async_computation.29 | async-start | bytes 2359296 | tf_op jit(solution)/shard_map/reduce_scatter | solution.py:82
  412.3 233.5 %reduce-scatter.40.cloned.1.call-start = ((), (), s32[]{:S(2)}) async-start(), calls=%async_computation.27 | async-start | bytes 2359296 | tf_op jit(solution)/shard_map/reduce_scatter | solution.py:79
  424.7 239.4 %reduce-scatter.64.cloned.1.call-start = ((), (), s32[]{:S(2)}) async-start(), calls=%async_computation.39 | async-start | bytes 2359296
  434.2 300.1 %reduce-scatter.66.cloned.1.call-start = ((), (), s32[]{:S(2)}) async-start(), calls=%async_computation.40 | async-start | bytes 2359296
  437.7 366.7 %reduce-scatter.28.cloned.1.call-start = ((), (), s32[]{:S(2)}) async-start(), calls=%async_computation.21 | async-start | bytes 2359296 | tf_op jit(solution)/shard_map/reduce_scatter | solution.py:70
  533.8 340.7 %reduce-scatter.36.cloned.1.call-start = ((), (), s32[]{:S(2)}) async-start(), calls=%async_computation.25 | async-start | bytes 2359296 | tf_op jit(solution)/shard_map/reduce_scatter | solution.py:76
  562.6 382.0 %reduce-scatter.32.cloned.1.call-start = ((), (), s32[]{:S(2)}) async-start(), calls=%async_computation.23 | async-start | bytes 2359296 | tf_op jit(solution)/shard_map/reduce_scatter | solution.py:73
  589.5 506.8 %reduce-scatter.60.cloned.1.call-start = ((), (), s32[]{:S(2)}) async-start(), calls=%async_computation.37 | async-start | bytes 9437184 | tf_op jit(solution)/shard_map/reduce_scatter | solution.py:97
  590.2 658.1 %reduce-scatter.56.cloned.1.call-start = ((), (), s32[]{:S(2)}) async-start(), calls=%async_computation.35 | async-start | bytes 9437184 | tf_op jit(solution)/shard_map/reduce_scatter | solution.py:94
  590.8 678.7 %reduce-scatter.68.cloned.1.call-start = ((), (), s32[]{:S(2)}) async-start(), calls=%async_computation.41 | async-start | bytes 245760
  644.4 647.5 %reduce-scatter.54.cloned.1.call-start = ((), (), s32[]{:S(2)}) async-start(), calls=%async_computation.34 | async-start | bytes 327680 | tf_op jit(solution)/shard_map/reduce_scatter | solution.py:126
  645.0 669.6 %reduce-scatter.46.cloned.1.call-start = ((), (), s32[]{:S(2)}) async-start(), calls=%async_computation.30 | async-start | bytes 327680 | tf_op jit(solution)/shard_map/reduce_scatter | solution.py:117
  645.7 691.2 %reduce-scatter.42.cloned.1.call-start = ((), (), s32[]{:S(2)}) async-start(), calls=%async_computation.28 | async-start | bytes 327680 | tf_op jit(solution)/shard_map/reduce_scatter | solution.py:114
  646.3 713.8 %reduce-scatter.48.cloned.1.call-start = ((), (), s32[]{:S(2)}) async-start(), calls=%async_computation.31 | async-start | bytes 327680 | tf_op jit(solution)/shard_map/reduce_scatter | solution.py:120
  666.0 717.1 %reduce-scatter.50.cloned.1.call-start = ((), (), s32[]{:S(2)}) async-start(), calls=%async_computation.32 | async-start | bytes 327680 | tf_op jit(solution)/shard_map/reduce_scatter | solution.py:123
  736.1 669.5 %reduce-scatter.30.cloned.1.call-start = ((), (), s32[]{:S(2)}) async-start(), calls=%async_computation.22 | async-start | bytes 327680 | tf_op jit(solution)/shard_map/reduce_scatter | solution.py:105
  804.4 623.6 %reduce-scatter.38.cloned.1.call-start = ((), (), s32[]{:S(2)}) async-start(), calls=%async_computation.26 | async-start | bytes 327680 | tf_op jit(solution)/shard_map/reduce_scatter | solution.py:111
  874.5 576.1 %reduce-scatter.34.cloned.1.call-start = ((), (), s32[]{:S(2)}) async-start(), calls=%async_computation.24 | async-start | bytes 327680 | tf_op jit(solution)/shard_map/reduce_scatter | solution.py:108
  944.7 533.3 %reduce-scatter.62.cloned.1.call-start = ((), (), s32[]{:S(2)}) async-start(), calls=%async_computation.38 | async-start | bytes 1310720 | tf_op jit(solution)/shard_map/reduce_scatter | solution.py:132
  1096.4 409.3 %reduce-scatter.58.cloned.1.call-start = ((), (), s32[]{:S(2)}) async-start(), calls=%async_computation.36 | async-start | bytes 1310720 | tf_op jit(solution)/shard_map/reduce_scatter | solution.py:129
  (113 other events, 2640.8 us)
Sparse Core Ops, SparseCore 0:
  379.9 67.9 reduce-scatter.51
  451.4 68.6 reduce-scatter.43
  523.6 70.2 reduce-scatter.39
  597.3 66.7 reduce-scatter.63
  667.5 66.7 reduce-scatter.65
  737.7 66.6 reduce-scatter.27
  807.9 66.5 reduce-scatter.35
  878.0 66.5 reduce-scatter.31
  948.3 147.9 reduce-scatter.59
  1100.2 147.9 reduce-scatter.55
  1250.7 18.7 reduce-scatter.67
  1271.8 20.0 reduce-scatter.53
  1294.5 20.0 reduce-scatter.45
  1316.9 20.0 reduce-scatter.41
  1340.0 20.0 reduce-scatter.47
  1363.0 20.0 reduce-scatter.49
  1385.5 20.0 reduce-scatter.29
  1407.9 20.0 reduce-scatter.37
  1430.6 20.0 reduce-scatter.33
  1453.1 24.8 reduce-scatter.61
  1480.7 24.8 reduce-scatter.57

commit v2 on v1

--- a/solution.py
+++ b/solution.py
@@ -771,15 +771,181 @@
     )(*blocks)
 
 
+def add_blocks(total, extra, leading):
+    def one(at, unused):
+        place = []
+        for size in leading[::-1]:
+            place.append(at % size)
+            at = at // size
+        place = tuple(place[::-1])
+        total[place] = (total[place].astype(jnp.float32) + extra[place].astype(jnp.float32)).astype(total.dtype)
+        return unused
+
+    if not leading:
+        total[...] = (total[...].astype(jnp.float32) + extra[...].astype(jnp.float32)).astype(total.dtype)
+        return
+    count = 1
+    for size in leading:
+        count *= size
+    lax.fori_loop(0, count, one, 0)
+
+
 class Scatter:
     def __init__(self, place, grad, out, strip, width, order, slots, send, recv, local):
         self.place, self.grad, self.out, self.strip, self.width = place, grad, out, strip, width
         self.order = order[::-1]
-        self.slots, self.send, self.recv, self.local = slots, send, recv, local
-        self.sent, self.used, self.started = 0, 0, []
-
-    def columns(self, x, k):
-        return pl.ds(pl.multiple_of((x * 2 + k) * self.width + self.strip[1], 128), self.strip[2])
+        self.total, self.other_core, self.halves, self.steps = slots
+        self.send, self.recv, self.local = send, recv, local
+        self.used, self.started = 0, []
+
+    def region(self, x, k):
+        part, start, count = self.strip
+        column = (x * 2 + k) * self.width + start
+        return self.grad.at[:, :, part, :, pl.ds(pl.multiple_of(column, 128), count)]
+
+    def copy(self, device, source, target, semaphore=None):
+        if semaphore is None:
+            semaphore = self.used
+            self.used += 1
+        return pltpu.make_async_remote_copy(
+            src_ref=source, dst_ref=target, send_sem=self.send.at[semaphore], recv_sem=self.recv.at[semaphore],
+            device_id=device, device_id_type=MESH)
+
+    def start(self, copy, condition=None):
+        when(condition, lambda: copy.start())
+        self.started.append((condition, copy))
+
+    def stages(self):
+        place, along = self.place, self.place.along
+        rows, columns = self.total.shape[-2:]
+        own = [
+            pltpu.make_async_copy(self.region(x, place.k), self.total.at[:, :, x], self.local.at[x]) for x in range(2)
+        ]
+        swapped = [
+            self.copy(place.across("k"), self.region(x, 1 - place.k), self.other_core.at[:, :, x]) for x in range(2)
+        ]
+        for copy in own:
+            copy.start()
+        for copy in swapped:
+            self.start(copy)
+        yield
+        for copy in own:
+            copy.wait()
+        for copy in swapped:
+            copy.wait_recv()
+        add_blocks(self.total, self.other_core, (along, 2, 2))
+        left = {"z": slice(None), "y": slice(None), "x": slice(None)}
+        at = {"y": place.y, "x": place.x}
+
+        def view(ref, **places):
+            return ref.at[tuple({**left, **places}[axis] for axis in "zyx")]
+
+        def sizes():
+            return tuple(size for axis, size in zip("zyx", (along, 2, 2)) if isinstance(left[axis], slice))
+
+        exchanges = 0
+        for axis in self.order:
+            if axis == "z":
+                shape = tuple(2 for name in "yx" if isinstance(left[name], slice))
+                landing = self.steps.at[(slice(None),) * 2 + tuple(slice(None) if isinstance(left[name], slice) else 0 for name in "yx")]
+                right, leftward = [self.used + at for at in range(along)], [self.used + along + at for at in range(along)]
+                self.used += 2 * along
+                for step in range(along):
+                    if step:
+                        yield
+                    for way, names, first in ((1, right, place.z), (-1, leftward, along - 1 - place.z)):
+                        goal = along - 1 - step + place.z if way == 1 else step - along + 1 + place.z
+                        side = 0 if way == 1 else 1
+                        if step:
+                            arrived = self.copy(
+                                place.across("k"), landing.at[side, step - 1], landing.at[side, step - 1], names[step - 1])
+
+                            def take(arrived=arrived, goal=goal, side=side, step=step):
+                                arrived.wait_recv()
+                                add_blocks(view(self.total, z=goal), landing.at[side, step - 1], shape)
+
+                            pl.when((first >= 1) & (first <= step))(take)
+                        if step < along - 1:
+                            onward = self.copy(
+                                place.device(dz=way), view(self.total, z=jnp.clip(goal, 0, along - 1)), landing.at[side, step], names[step])
+                            self.start(onward, (first <= step) & (first < along - 1))
+                left["z"] = place.z
+            else:
+                landing = self.halves[exchanges]
+                exchanges += 1
+                target = landing.at[tuple(slice(None) if isinstance(left[name], slice) and name != axis else 0 for name in "zyx")]
+                swap = self.copy(place.across(axis), view(self.total, **{axis: 1 - at[axis]}), target)
+                self.start(swap)
+                yield
+                swap.wait_recv()
+                left[axis] = at[axis]
+                add_blocks(view(self.total), target, sizes())
+        part, start, count = self.strip
+        self.out[part, :, start : start + count] = view(self.total)[...].astype(jnp.float32)
+
+    def finish(self):
+        for condition, copy in self.started:
+            when(condition, lambda copy=copy: copy.wait_send())
+
+
+def scatter_slots(along, rows, columns, order):
+    left = {"z": along, "y": 2, "x": 2}
+    whole = (along, 2, 2, rows, columns)
+    shapes = [whole, whole]
+    steps = None
+    for axis in order[::-1]:
+        if axis == "z":
+            steps = (2, along - 1, left["y"], left["x"], rows, columns)
+        left[axis] = 1
+        if axis != "z":
+            shapes.append((left["z"], left["y"], left["x"], rows, columns))
+    return shapes + [steps]
+
+
+def scatter_kernel(units, count, *refs):
+    grads, outs = refs[:count], refs[count : 2 * count]
+    send, recv, local = refs[2 * count : 2 * count + 3]
+    slots = refs[2 * count + 3 :]
+    place = Place()
+    place.greet()
+    scatters = []
+    for at, (which, strip, order) in enumerate(units):
+        total, other_core, first, second, steps = slots[5 * at : 5 * at + 5]
+        scatters.append(
+            Scatter(place, grads[which], outs[which], strip, outs[which].shape[-1], order,
+                    (total, other_core, (first, second), steps), send.at[at], recv.at[at], local.at[at]))
+    running = [scatter.stages() for scatter in scatters]
+    while running:
+        running = [stages for stages in running if next(stages, running) is not running]
+    for scatter in scatters:
+        scatter.finish()
+
+
+def scatter_blocks(grads, collective_id, least):
+    along, cols = lax.axis_size("row") // 2, lax.axis_size("col")
+    blocks = [jax.ShapeDtypeStruct(g.shape[2:4] + (g.shape[4] // cols,), jnp.float32) for g in grads]
+    units = gather_units(blocks, least)
+    count = len(grads)
+    slots = []
+    for which, strip, order in units:
+        slots += [pltpu.VMEM(shape, jnp.bfloat16) for shape in scatter_slots(along, blocks[which].shape[1], strip[2], order)]
+    anywhere = pl.BlockSpec(memory_space=pl.ANY)
+    return pl.pallas_call(
+        functools.partial(scatter_kernel, units, count),
+        out_shape=blocks,
+        in_specs=[anywhere] * count,
+        out_specs=[pl.BlockSpec(memory_space=pltpu.VMEM)] * count,
+        scratch_shapes=[
+            pltpu.SemaphoreType.DMA((len(units), 2 * along + 4)),
+            pltpu.SemaphoreType.DMA((len(units), 2 * along + 4)),
+            pltpu.SemaphoreType.DMA((len(units), 2)),
+            *slots,
+        ],
+        compiler_params=pltpu.CompilerParams(
+            collective_id=collective_id, has_side_effects=True, vmem_limit_bytes=60 << 20),
+        cost_estimate=pl.CostEstimate(
+            flops=sum(g.size for g in grads), bytes_accessed=4 * sum(g.size for g in grads), transcendentals=0),
+    )(*grads)
 
 
 def fast(
@@ -929,14 +1095,22 @@
     norm_grads = jnp.stack(
         [first_gain_part, first_bias_part, second_gain_part, second_bias_part, third_gain_part, third_bias_part]
     )
-    col_count = lax.axis_size("col")
-    norm_grads = norm_grads.reshape(6, 2 * pairs, col_count, piece).transpose(1, 2, 0, 3)
-    norm_grads = norm_grads.reshape(2 * pairs, col_count * 6 * piece)
-    summed = spread(
-        (self_query_part, self_key_part, self_value_part, self_out_grad, cross_query_part, cross_key_part,
-         cross_value_part, cross_out_grad, up_grad, down_grad, norm_grads))
-    norm_parts = summed[10].reshape(6, piece)
-    return (layer_out, input_grad, text_grad, *summed[:10], *norm_parts)
+    norm_grads = norm_grads.reshape(6, 2 * pairs, -1, piece).transpose(1, 0, 2, 3)
+    norm_grads = jnp.pad(norm_grads, ((0, 0), (0, 10), (0, 0), (0, 128 - piece)))
+
+    def by_place(grad, parts):
+        return grad.astype(jnp.bfloat16).reshape(pairs, 2, parts, -1, grad.shape[-1])
+
+    early_sums = scatter_blocks(
+        [by_place(g, 1) for g in (self_out_grad, cross_query_part, cross_key_part, cross_value_part, cross_out_grad, up_grad)]
+        + [by_place(down_grad, down_weight.shape[0] // block_rows)], 4, 256)
+    late_sums = scatter_blocks(
+        [by_place(g, 1) for g in (self_query_part, self_key_part, self_value_part)]
+        + [by_place(norm_grads.reshape(2 * pairs * 16, -1), 1)], 3, 128)
+    norm_parts = late_sums[3][0, :6, :piece]
+    sums = late_sums[:3] + early_sums
+    sums = [total.reshape(-1, total.shape[-1]) for total in sums]
+    return (layer_out, input_grad, text_grad, *sums, *norm_parts)
 
 
 def local(*arrays):

time: 1520 us -> 795 us (0.52)
  waiting for transfers between devices: 907 us -> 32.8 us
  Pallas kernels: 338 us -> 551 us
  blocking collectives: 35.8 us -> 0 us
    reduce_scatter x18 -> x0, waiting for transfers between devices: 732 us -> none  [the longest x1 152 us: spread(): lax.psum_scatter(grads[8].astype(jnp.bfloat16), 'row', scatter_dimension=...]
    pallas_call x0 -> x2, Pallas kernels: none -> 212 us  [scatter_blocks(): pl.pallas_call(functools.partial(scatter_kernel, units, count), out_shape...]
    unnamed x24 -> x0, waiting for transfers between devices: 101 us -> none
    ppermute x5, waiting for transfers between devices: 62.5 us -> 18.3 us  [home(): return lax.ppermute(array, 'row', back_perm)]
    unnamed x1 -> x0, blocking collectives: 35.8 us -> none
    unnamed x225 -> x257, local copies, waits for them, and re-layouts: 37.7 us -> 23.5 us
  transfers between devices with their start and end apart: 33 -> 12, of which waited for: 24 -> 4; matrix products, arithmetic and copies ran while one was open for 9% -> 8% of each run, Pallas kernels for 18% -> 52%
where the time goes in v2:
time: 795 us; the launch traced here: 786 us
  Pallas kernels  551 us (69%)
  matrix products  68.8 us (9%)
  local copies, waits for them, and re-layouts  65.9 us (8%)
  other arithmetic  38.6 us (5%)
  waiting for transfers between devices  32.8 us (4%)
  starting transfers between devices  26.1 us (3%)
    pallas_call x2, Pallas kernels, scatter_blocks(): pl.pallas_call(functools.partial(scatter_kernel, units, count), out_shape...  212 us
    pallas_call x2, Pallas kernels, gather_blocks(): pl.pallas_call(functools.partial(gather_kernel, units, count), out_shape=...  192 us
    pallas_call x3, Pallas kernels, attend_back(): pl.pallas_call(functools.partial(attend_back_kernel, causal, tile), grid=...  54.5 us
    pallas_call x1, Pallas kernels, feed(): pl.pallas_call(feed_kernel, grid=(ff // chunk,), in_specs=[whole, whole,...  49.1 us
    pallas_call x3, Pallas kernels, attend(): pl.pallas_call(functools.partial(attend_kernel, causal, tile), grid=(widt...  43.1 us
    dot_general x8, matrix products, over_tokens(): lax.dot_general(left, right, (((0,), (0,)), ((), ())), preferred_element_...  27 us
    unnamed x257, local copies, waits for them, and re-layouts  23.5 us
    dot_general x8, matrix products, by_transposed(): lax.dot_general(left, right, (((1,), (1,)), ((), ())), preferred_element_...  23.4 us
  transfers between devices with their start and end apart: 12, of which 4 were waited for; matrix products, arithmetic and copies ran while one was open for 8% of the time, Pallas kernels for 52%

profile of v2, /device:TPU:0, one launch (start us, length us, event | category | flops | bytes accessed | tf_op | source)
XLA Modules:
  0.0 786.2 jit_solution(14710975025111211616)
XLA Ops:
  8.1 44.2 %shard_map.330 = (bf16[4,2,1,128,1024]{4,3,2,1,0:T(8,128)(2,1)}, bf16[4,2,1,128,1024]{4,3,2,1,0:T(8,128)(2,1)}, bf16[4,2,1,128,1024]{4,3,2,1,0:T(8,128)(2,1)}, bf16[4,2,1,16,512]{4,3,2,1,0:T(8,128)(2,1)}) custom-call(bf16[1,128,256]{2,1,0:T(8,128)(2,1)} %bitcast.162, bf16[1,128,256]{2,1,0:T(8,128)(2,1)} %bitcast.163, bf16[1,128,256]{2,1,0:T(8,128)(2,1)} %bitcast.164, ...), custom_call_target="tpu_custom_call" | custom-call | bytes 12845056 | tf_op jit(solution)/shard_map/pallas_call | solution.py:757
  53.5 3.5 convolution_convert_fusion.12.k_ref
  70.8 19.9 %shard_map.331 = (f32[750,1024]{1,0:T(8,128)S(1)}, f32[750,128]{1,0:T(8,128)S(1)}) custom-call(bf16[750,1024]{1,0:T(8,128)(2,1)S(1)} %convolution_convert_fusion.13.q_ref, bf16[750,1024]{1,0:T(8,128)(2,1)S(1)} %convolution_convert_fusion.12.k_ref, bf16[750,1024]{1,0:T(8,128)(2,1)S(1)} %convolution_convert_fusion.11.v_ref), custom_call_target="tpu_custom_call" | custom-call | flops 2304000000 | bytes 6144000 | tf_op jit(solution)/shard_map/pallas_call | solution.py:484
  94.2 147.8 %shard_map.333 = (bf16[4,2,1,128,1024]{4,3,2,1,0:T(8,128)(2,1)}, bf16[4,2,1,128,1024]{4,3,2,1,0:T(8,128)(2,1)}, bf16[4,2,1,128,1024]{4,3,2,1,0:T(8,128)(2,1)}, b...) custom-call(bf16[1,128,256]{2,1,0:T(8,128)(2,1)} %bitcast.165, ...), custom_call_target="tpu_custom_call" | custom-call | bytes 54525952 | tf_op jit(solution)/shard_map/pallas_call | solution.py:757
  247.3 11.7 %shard_map.332 = (bf16[750,512]{1,0:T(8,128)(2,1)}, f32[750,128]{1,0:T(8,128)S(1)}) custom-call(bf16[750,512]{1,0:T(8,128)(2,1)S(1)} %slice_select_fusion.3.q_ref, bf16[750,512]{1,0:T(8,128)(2,1)S(1)} %slice_select_fusion.2.k_ref, bf16[750,512]{1,0:T(8,128)(2,1)S(1)} %slice_select_fusion.1.v_ref), custom_call_target="tpu_custom_call" | custom-call | flops 1152000000 | bytes 3072000 | tf_op jit(solution)/shard_map/pallas_call | solution.py:484
  259.0 4.7 collective-permute-start.3
  266.5 6.4 collective-permute-done.3
  292.0 4.6 add_convert_fusion.5
  303.1 11.4 %shard_map.334 = (bf16[750,1024]{1,0:T(8,128)(2,1)S(1)}, f32[750,128]{1,0:T(8,128)S(1)}) custom-call(bf16[750,1024]{1,0:T(8,128)(2,1)S(1)} %convolution_convert_fusion.10.q_ref, bf16[64,1024]{1,0:T(8,128)(2,1)S(1)} %convolution_convert_fusion.15.k_ref, bf16[64,1024]{1,0:T(8,128)(2,1)S(1)} %convolution_convert_fusion.14.v_ref), custom_call_target="tpu_custom_call" | custom-call | flops 196608000 | bytes 6144000 | tf_op jit(solution)/shard_map/pallas_call | solution.py:484
  315.9 4.8 fusion.40
  323.2 49.1 %shard_map.335 = (bf16[750,1024]{1,0:T(8,128)(2,1)}, f32[750,1024]{1,0:T(8,128)}, bf16[1024,4096]{1,0:T(8,128)(2,1)}, bf16[4096,1024]{1,0:T(8,128)(2,1)}) custom-call(bf16[750,1024]{1,0:T(8,128)(2,1)} %add_convert_fusion.3.h_ref, bf16[750,1024]{1,0:T(8,128)(2,1)} %cot_ref.1, f32[750,1024]{1,0:T(8,128)} %copy-done.27, bf16[1024,4096]{1,0:T(8,128)(2,1)} %bitcast.177, ...), custom_call_target="tpu_custom_call" | custom-call | flops 37748736000 | bytes 45842432 | tf_op jit(solution)/shard_map/pallas_call | solution.py:556
  372.3 3.6 multiply_reduce_fusion
  392.5 10.6 %shard_map.336 = (bf16[750,1024]{1,0:T(8,128)(2,1)S(1)}, bf16[64,1024]{1,0:T(8,128)(2,1)S(1)}, bf16[64,1024]{1,0:T(8,128)(2,1)S(1)}) custom-call(bf16[750,1024]{1,0:T(8,128)(2,1)S(1)} %convolution_convert_fusion.10.q_ref, bf16[64,1024]{1,0:T(8,128)(2,1)S(1)} %convolution_convert_fusion.15.k_ref, bf16[64,1024]{1,0:T(8,128)(2,1)S(1)} %convolution_convert_fusion.14.v_ref, ...), custom_call_target="tpu_custom_call" | custom-call | flops 491520000 | bytes 12288000 | tf_op jit(solution)/shard_map/pallas_call | solution.py:527
  403.2 4.6 multiply_reduce_fusion.1
  440.1 29.8 %shard_map.337 = (f32[750,1024]{1,0:T(8,128)S(1)}, f32[750,1024]{1,0:T(8,128)S(1)}, f32[750,1024]{1,0:T(8,128)}) custom-call(bf16[750,1024]{1,0:T(8,128)(2,1)S(1)} %copy-done.7, bf16[750,1024]{1,0:T(8,128)(2,1)S(1)} %copy-done.1, bf16[750,1024]{1,0:T(8,128)(2,1)S(1)} %copy-done.4, bf16[750,1024]{1,0:T(8,128)(2,1)S(1)} %get-tuple-element.151.do_ref, ...), custom_call_target="tpu_custom_call" | custom-call | flops 5760000000 | bytes 12288000 | tf_op jit(solution)/shard_map/pallas_call | solution.py:527
  483.4 166.5 %shard_map.340 = (f32[1,128,256]{2,1,0:T(8,128)}, f32[1,128,256]{2,1,0:T(8,128)}, f32[1,128,256]{2,1,0:T(8,128)}, f32[1,128,256]{2,1,0:T(8,128)}, f32[1,128,256]...) custom-call(bf16[4,2,1,128,1024]{4,3,2,1,0:T(8,128)(2,1)} %bitcast.144, ...), custom_call_target="tpu_custom_call" | custom-call | flops 13631488 | bytes 54525952 | tf_op jit(solution)/shard_map/pallas_call | solution.py:933
  652.5 14.2 %shard_map.338 = (bf16[750,512]{1,0:T(8,128)(2,1)S(1)}, bf16[750,512]{1,0:T(8,128)(2,1)S(1)}, bf16[750,512]{1,0:T(8,128)(2,1)S(1)}) custom-call(bf16[750,512]{1,0:T(8,128)(2,1)S(1)} %copy-done.13, bf16[750,512]{1,0:T(8,128)(2,1)S(1)} %copy-done.9, bf16[750,512]{1,0:T(8,128)(2,1)S(1)} %copy-done.11, bf16[750,512]{1,0:T(8,128)(2,1)S(1)} %slice_select_fusion.do_ref, ...), custom_call_target="tpu_custom_call" | custom-call | flops 2880000000 | bytes 6144000 | tf_op jit(solution)/shard_map/pallas_call | solution.py:527
  672.5 8.0 %collective-permute-done.8 = bf16[750,512]{1,0:T(8,128)(2,1)S(1)} collective-permute-done((bf16[750,512]{1,0:T(8,128)(2,1)S(1)}, bf16[750,512]{1,0:T(8,128)(2,1)S(1)}, u32[]{:S(2)}, u32[]{:S(2)}) %collective-permute-start.8) | collective-permute-done | bytes 768032 | tf_op jit(solution)/shard_map/ppermute | solution.py:967
  682.4 9.3 %collective-permute-done.9 = bf16[750,512]{1,0:T(8,128)(2,1)S(1)} collective-permute-done((bf16[750,512]{1,0:T(8,128)(2,1)S(1)}, bf16[750,512]{1,0:T(8,128)(2,1)S(1)}, u32[]{:S(2)}, u32[]{:S(2)}) %collective-permute-start.9) | collective-permute-done | bytes 768032 | tf_op jit(solution)/shard_map/ppermute | solution.py:970
  693.6 9.0 %collective-permute-done.10 = bf16[750,512]{1,0:T(8,128)(2,1)S(1)} collective-permute-done((bf16[750,512]{1,0:T(8,128)(2,1)S(1)}, bf16[750,512]{1,0:T(8,128)(2,1)S(1)}, u32[]{:S(2)}, u32[]{:S(2)}) %collective-permute-start.10) | collective-permute-done | bytes 768032 | tf_op jit(solution)/shard_map/ppermute | solution.py:970
  702.7 4.3 fusion.34
  710.8 3.8 add_add_fusion.3
  715.7 6.2 convolution_convert_fusion.7
  728.7 46.0 %shard_map.339 = (f32[1,128,256]{2,1,0:T(8,128)}, f32[1,128,256]{2,1,0:T(8,128)}, f32[1,128,256]{2,1,0:T(8,128)}, f32[1,16,128]{2,1,0:T(8,128)}) custom-call(bf16[4,2,1,128,1024]{4,3,2,1,0:T(8,128)(2,1)} %bitcast.138, bf16[4,2,1,128,1024]{4,3,2,1,0:T(8,128)(2,1)} %bitcast.140, bf16[4,2,1,128,1024]{4,3,2,1,0:T(8,128)(2,1)} %bitcast.139, ...), custom_call_target="tpu_custom_call" | custom-call | flops 3211264 | bytes 12845056 | tf_op jit(solution)/shard_map/pallas_call | solution.py:933
  (382 shorter events, 159.3 us)
Async XLA Ops:
  0.7 52.8 %copy-start.29 = (bf16[750,1024]{1,0:T(8,128)(2,1)S(1)}, bf16[750,1024]{1,0:T(8,128)(2,1)}, u32[]{:S(2)}) copy-start(bf16[750,1024]{1,0:T(8,128)(2,1)} %param.21) | copy-start | bytes 4608004
  0.7 241.3 %collective-permute-start.5 = (bf16[32,1024]{1,0:T(8,128)(2,1)}, bf16[32,1024]{1,0:T(8,128)(2,1)S(1)}, u32[]{:S(2)}, u32[]{:S(2)}) collective-permute-start(bf16[32,1024]{1,0:T(8,128)(2,1)} %param.22), channel_id=1, source_target_pairs={{0,4},{8,12},{16,20},{24,28},{4,0},{12,8},{20,16},{28,24},{1,5},{9... | collective-permute-start | bytes 196616 | tf_op jit(solution)/shard_map/ppermute | solution.py:1024
  5.4 61.0 %copy-start.74 = (f32[750]{0:T(1024)}, f32[750]{0:T(1024)S(1)}, u32[]{:S(2)}) copy-start(f32[750]{0:T(1024)S(1)} %broadcast_multiply_fusion.2) | copy-start | bytes 9004
  7.4 49.6 %copy-start.83 = (f32[750]{0:T(1024)}, f32[750]{0:T(1024)S(1)}, u32[]{:S(2)}) copy-start(f32[750]{0:T(1024)S(1)} %fusion.9) | copy-start | bytes 9004
  7.4 59.0 %copy-start.79 = (f32[750]{0:T(1024)}, f32[750]{0:T(1024)S(1)}, u32[]{:S(2)}) copy-start(f32[750]{0:T(1024)S(1)} %fusion.20) | copy-start | bytes 9004
  58.1 186.2 %collective-permute-start.1 = (bf16[750,512]{1,0:T(8,128)(2,1)}, bf16[750,512]{1,0:T(8,128)(2,1)}, u32[]{:S(2)}, u32[]{:S(2)}) collective-permute-start(bf16[750,512]{1,0:T(8,128)(2,1)} %slice.159), channel_id=1, source_target_pairs={{0,4},{8,12},{16,20},{24,28},{1,5},{9,13},{17,21},{25,29},{2,6},{1... | collective-permute-start | bytes 2304008 | tf_op jit(solution)/shard_map/ppermute | solution.py:967
  64.2 181.3 %collective-permute-start.2 = (bf16[750,512]{1,0:T(8,128)(2,1)}, bf16[750,512]{1,0:T(8,128)(2,1)}, u32[]{:S(2)}, u32[]{:S(2)}) collective-permute-start(bf16[750,512]{1,0:T(8,128)(2,1)} %slice.161), channel_id=1, source_target_pairs={{0,4},{8,12},{16,20},{24,28},{1,5},{9,13},{17,21},{25,29},{2,6},{1... | collective-permute-start | bytes 2304008 | tf_op jit(solution)/shard_map/ppermute | solution.py:967
  69.3 172.7 %copy-start.60 = (bf16[32,1024]{1,0:T(8,128)(2,1)S(1)}, bf16[32,1024]{1,0:T(8,128)(2,1)}, u32[]{:S(2)}) copy-start(bf16[32,1024]{1,0:T(8,128)(2,1)} %param.22) | copy-start | bytes 196612
  69.3 176.3 %collective-permute-start = (bf16[750,512]{1,0:T(8,128)(2,1)}, bf16[750,512]{1,0:T(8,128)(2,1)}, u32[]{:S(2)}, u32[]{:S(2)}) collective-permute-start(bf16[750,512]{1,0:T(8,128)(2,1)} %slice.156), channel_id=1, source_target_pairs={{4,0},{12,8},{20,16},{28,24},{5,1},{13,9},{21,17},{29,25},{6,2},{1... | collective-permute-start | bytes 2304008 | tf_op jit(solution)/shard_map/ppermute | solution.py:970
  259.0 13.9 %collective-permute-start.3 = (f32[750,8]{1,0:T(8,128)S(1)}, f32[750,8]{1,0:T(8,128)S(1)}, u32[]{:S(2)}, u32[]{:S(2)}) collective-permute-start(f32[750,8]{1,0:T(8,128)S(1)} %bitcast.121), channel_id=1, source_target_pairs={{0,4},{8,12},{16,20},{24,28},{1,5},{9,13},{17,21},{25,29},{2,6},{1... | collective-permute-start | bytes 72008 | tf_op jit(solution)/shard_map/ppermute | solution.py:967
  263.7 28.3 %collective-permute-start.4 = (bf16[750,512]{1,0:T(8,128)(2,1)}, bf16[750,512]{1,0:T(8,128)(2,1)}, u32[]{:S(2)}, u32[]{:S(2)}) collective-permute-start(bf16[750,512]{1,0:T(8,128)(2,1)} %get-tuple-element.79), channel_id=1, source_target_pairs={{0,4},{8,12},{16,20},{24,28},{1,5},{9,13},{17,21},{25,29},{2,6},{1... | collective-permute-start | bytes 2304008 | tf_op jit(solution)/shard_map/ppermute | solution.py:967
  323.2 49.1 %copy-start.28 = (f32[750,1024]{1,0:T(8,128)S(1)}, f32[750,1024]{1,0:T(8,128)}, u32[]{:S(2)}) copy-start(f32[750,1024]{1,0:T(8,128)} %copy-done.27) | copy-start | bytes 9216004
  431.1 47.1 %collective-permute-start.11 = (bf16[32,2048]{1,0:T(8,128)(2,1)}, bf16[32,2048]{1,0:T(8,128)(2,1)}, u32[]{:S(2)}, u32[]{:S(2)}) collective-permute-start(bf16[32,2048]{1,0:T(8,128)(2,1)} %broadcast_select_fusion.3), channel_id=1, source_target_pairs={{0,4},{8,12},{16,20},{24,28},{4,0},{12,8},{20,16},{28,24},{1,5},{9... | collective-permute-start | bytes 393224 | tf_op jit(solution)/shard_map/ppermute | solution.py:1053
  436.0 41.4 %collective-permute-start.7 = (f32[4,4,750]{2,1,0:T(4,128)}, f32[4,4,750]{2,1,0:T(4,128)}, u32[]{:S(2)}, u32[]{:S(2)}) collective-permute-start(f32[4,4,750]{2,1,0:T(4,128)} %slice.146), channel_id=1, source_target_pairs={{4,0},{12,8},{20,16},{28,24},{5,1},{13,9},{21,17},{29,25},{6,2},{1... | collective-permute-start | bytes 144008 | tf_op jit(solution)/shard_map/ppermute | solution.py:970
  476.1 176.3 %collective-permute-start.6 = (bf16[750,512]{1,0:T(8,128)(2,1)S(1)}, bf16[750,512]{1,0:T(8,128)(2,1)S(1)}, u32[]{:S(2)}, u32[]{:S(2)}) collective-permute-start(bf16[750,512]{1,0:T(8,128)(2,1)S(1)} %slice.166), channel_id=1, source_target_pairs={{4,0},{12,8},{20,16},{28,24},{5,1},{13,9},{21,17},{29,25},{6,2},{1... | collective-permute-start | bytes 2304008 | tf_op jit(solution)/shard_map/ppermute | solution.py:970
  666.7 13.8 %collective-permute-start.8 = (bf16[750,512]{1,0:T(8,128)(2,1)S(1)}, bf16[750,512]{1,0:T(8,128)(2,1)S(1)}, u32[]{:S(2)}, u32[]{:S(2)}) collective-permute-start(bf16[750,512]{1,0:T(8,128)(2,1)S(1)} %get-tuple-element.93), channel_id=1, source_target_pairs={{0,4},{8,12},{16,20},{24,28},{1,5},{9,13},{17,21},{25,29},{2,6},{1... | collective-permute-start | bytes 2304008 | tf_op jit(solution)/shard_map/ppermute | solution.py:967
  669.7 22.0 %collective-permute-start.9 = (bf16[750,512]{1,0:T(8,128)(2,1)S(1)}, bf16[750,512]{1,0:T(8,128)(2,1)S(1)}, u32[]{:S(2)}, u32[]{:S(2)}) collective-permute-start(bf16[750,512]{1,0:T(8,128)(2,1)S(1)} %get-tuple-element.95), channel_id=1, source_target_pairs={{4,0},{12,8},{20,16},{28,24},{5,1},{13,9},{21,17},{29,25},{6,2},{1... | collective-permute-start | bytes 2304008 | tf_op jit(solution)/shard_map/ppermute | solution.py:970
  671.0 31.6 %collective-permute-start.10 = (bf16[750,512]{1,0:T(8,128)(2,1)S(1)}, bf16[750,512]{1,0:T(8,128)(2,1)S(1)}, u32[]{:S(2)}, u32[]{:S(2)}) collective-permute-start(bf16[750,512]{1,0:T(8,128)(2,1)S(1)} %get-tuple-element.97), channel_id=1, source_target_pairs={{4,0},{12,8},{20,16},{28,24},{5,1},{13,9},{21,17},{29,25},{6,2},{1... | collective-permute-start | bytes 2304008 | tf_op jit(solution)/shard_map/ppermute | solution.py:970
  728.7 52.1 %copy-start.73 = (f32[1,128,256]{2,1,0:T(8,128)S(1)}, f32[1,128,256]{2,1,0:T(8,128)}, u32[]{:S(2)}) copy-start(f32[1,128,256]{2,1,0:T(8,128)} %get-tuple-element.105) | copy-start | bytes 393220
  728.7 52.8 %copy-start.72 = (f32[1,128,256]{2,1,0:T(8,128)S(1)}, f32[1,128,256]{2,1,0:T(8,128)}, u32[]{:S(2)}) copy-start(f32[1,128,256]{2,1,0:T(8,128)} %get-tuple-element.106) | copy-start | bytes 393220
  728.7 53.5 %copy-start.71 = (f32[1,128,256]{2,1,0:T(8,128)S(1)}, f32[1,128,256]{2,1,0:T(8,128)}, u32[]{:S(2)}) copy-start(f32[1,128,256]{2,1,0:T(8,128)} %get-tuple-element.107) | copy-start | bytes 393220
  728.7 54.1 %copy-start.70 = (f32[1,128,256]{2,1,0:T(8,128)S(1)}, f32[1,128,256]{2,1,0:T(8,128)}, u32[]{:S(2)}) copy-start(f32[1,128,256]{2,1,0:T(8,128)} %get-tuple-element.108) | copy-start | bytes 393220
  728.7 54.8 %copy-start.69 = (f32[1,128,256]{2,1,0:T(8,128)S(1)}, f32[1,128,256]{2,1,0:T(8,128)}, u32[]{:S(2)}) copy-start(f32[1,128,256]{2,1,0:T(8,128)} %get-tuple-element.109) | copy-start | bytes 393220
  728.7 55.4 %copy-start.68 = (f32[1,128,1024]{2,1,0:T(8,128)S(1)}, f32[1,128,1024]{2,1,0:T(8,128)}, u32[]{:S(2)}) copy-start(f32[1,128,1024]{2,1,0:T(8,128)} %get-tuple-element.110) | copy-start | bytes 1572868
  (108 other events, 721.1 us)

commit v3 on v2

--- a/solution.py
+++ b/solution.py
@@ -537,26 +537,36 @@
     def _():
         acc[...]=res_ref[...]
         g_ref[...]=jnp.zeros_like(g_ref)
-    h=h_ref[...]; cot=cot_ref[...]
-    pre=dg(h,up_ref[...],NN)
+    h=h_ref[...]
+    up=up_ref[:,0].reshape(h.shape[1],-1)
+    blocks,wide=down_ref.shape[1],down_ref.shape[3]
+    pre=dg(h,up,NN)
     cdf=0.5*(1.0+lax.erf(pre*0.7071067811865476))
     inner=(pre*cdf).astype(jnp.bfloat16)
-    acc[...]+=dg(inner,down_ref[...],NN)
-    ddown_ref[...]=dg(inner,cot,TN).astype(ddown_ref.dtype)
     slope=cdf+pre*(jnp.exp(-0.5*pre*pre)*0.3989422804014327)
-    gpre=(dg(cot,down_ref[...],NT)*slope).astype(jnp.bfloat16)
-    dup_ref[...]=dg(h,gpre,TN).astype(dup_ref.dtype)
-    g_ref[...]+=dg(gpre,up_ref[...],NT)
+    grad=None
+    for at in range(blocks):
+        columns=slice(at*wide,(at+1)*wide)
+        cot=cot_ref[:,columns]
+        acc[:,columns]+=dg(inner,down_ref[0,at],NN)
+        ddown_ref[0,at]=dg(inner,cot,TN).astype(ddown_ref.dtype)
+        part=dg(cot,down_ref[0,at],NT)
+        grad=part if grad is None else grad+part
+    gpre=(grad*slope).astype(jnp.bfloat16)
+    dup_ref[:,0]=dg(h,gpre,TN).astype(dup_ref.dtype).reshape(dup_ref.shape[0],dup_ref.shape[2],dup_ref.shape[3])
+    g_ref[...]+=dg(gpre,up,NT)
     @pl.when(i==pl.num_programs(0)-1)
     def _(): out_ref[...]=acc[...].astype(out_ref.dtype)
 
-def feed(h,cot,res,up,down,chunk=512):
-    rows,d=h.shape; ff=up.shape[1]
+def feed(h,cot,res,up,down):
+    rows,d=h.shape; chunk=down.shape[2]; strips=up.shape[3]//chunk; ff=down.shape[0]*chunk
     whole=pl.BlockSpec((rows,d),lambda i:(0,0))
+    up_spec=pl.BlockSpec((up.shape[0],1,up.shape[2],chunk),lambda i:(0,i//strips,0,i%strips))
+    down_spec=pl.BlockSpec((1,)+down.shape[1:],lambda i:(i,0,0,0))
     return pl.pallas_call(feed_kernel,grid=(ff//chunk,),
-        in_specs=[whole,whole,whole,pl.BlockSpec((d,chunk),lambda i:(0,i)),pl.BlockSpec((chunk,d),lambda i:(i,0))],
-        out_specs=[whole,whole,pl.BlockSpec((d,chunk),lambda i:(0,i)),pl.BlockSpec((chunk,d),lambda i:(i,0))],
-        out_shape=[jax.ShapeDtypeStruct((rows,d),jnp.bfloat16),jax.ShapeDtypeStruct((rows,d),jnp.float32),jax.ShapeDtypeStruct((d,ff),jnp.bfloat16),jax.ShapeDtypeStruct((ff,d),jnp.bfloat16)],
+        in_specs=[whole,whole,whole,up_spec,down_spec],
+        out_specs=[whole,whole,up_spec,down_spec],
+        out_shape=[jax.ShapeDtypeStruct((rows,d),jnp.bfloat16),jax.ShapeDtypeStruct((rows,d),jnp.float32),jax.ShapeDtypeStruct(up.shape,jnp.bfloat16),jax.ShapeDtypeStruct(down.shape,jnp.bfloat16)],
         scratch_shapes=[pltpu.VMEM((rows,d),jnp.float32)],
         compiler_params=pltpu.CompilerParams(vmem_limit_bytes=56<<20),
         cost_estimate=pl.CostEstimate(flops=12*rows*d*ff,bytes_accessed=8*d*ff+16*rows*d,transcendentals=2*rows*ff))(h,cot,res,up,down)
@@ -604,6 +614,16 @@
         run()
     else:
         pl.when(condition)(run)
+
+
+def in_turn(units, lag):
+    ready = [(lag * at, at) for at in range(len(units))]
+    while ready:
+        turn, at = min(ready)
+        ready.remove((turn, at))
+        if next(units[at], units) is not units:
+            ready.append((turn + 1, at))
+        yield
 
 
 class Gather:
@@ -729,9 +749,7 @@
         Gather(place, blocks[which], fulls[which], strip, order, send.at[at], recv.at[at])
         for at, (which, strip, order) in enumerate(units)
     ]
-    running = [gather.stages() for gather in gathers]
-    while running:
-        running = [stages for stages in running if next(stages, running) is not running]
+    for unused in in_turn([gather.stages() for gather in gathers], 0.0):
         while own:
             own.pop().wait()
     for gather in gathers:
@@ -778,11 +796,11 @@
             place.append(at % size)
             at = at // size
         place = tuple(place[::-1])
-        total[place] = (total[place].astype(jnp.float32) + extra[place].astype(jnp.float32)).astype(total.dtype)
+        total[place] = total[place] + extra[place]
         return unused
 
     if not leading:
-        total[...] = (total[...].astype(jnp.float32) + extra[...].astype(jnp.float32)).astype(total.dtype)
+        total[...] = total[...] + extra[...]
         return
     count = 1
     for size in leading:
@@ -914,9 +932,8 @@
         scatters.append(
             Scatter(place, grads[which], outs[which], strip, outs[which].shape[-1], order,
                     (total, other_core, (first, second), steps), send.at[at], recv.at[at], local.at[at]))
-    running = [scatter.stages() for scatter in scatters]
-    while running:
-        running = [stages for stages in running if next(stages, running) is not running]
+    for unused in in_turn([scatter.stages() for scatter in scatters], 0.5):
+        pass
     for scatter in scatters:
         scatter.finish()
 
@@ -977,6 +994,11 @@
         jnp.stack([first_gain, first_bias, second_gain, second_bias, third_gain, third_bias])
     )
 
+    everyone = ("row", "col")
+    places = (lax.axis_size("row"), lax.axis_size("col"))
+    up_blocks = lax.all_gather(up_weight, everyone).reshape(*places, *up_weight.shape)
+    down_blocks = lax.all_gather(down_weight, everyone).reshape(*places, *down_weight.shape)
+
     def small(block):
         return block.reshape(1, block_rows, block_cols)
 
@@ -986,9 +1008,9 @@
     early = gather_blocks([small(self_query), small(self_key), small(self_value), gains], 1, 128)
     query_self, key_self, value_self = [flat(w) for w in early[:3]]
     late = gather_blocks(
-        [small(self_output), small(cross_query), small(cross_key), small(cross_value), small(cross_output),
-         up_weight.reshape(1, *up_weight.shape), down_weight.reshape(-1, block_rows, block_cols)], 2, 256)
-    out_self, query_cross, key_cross, value_cross, out_cross, up_full, down_full = [flat(w) for w in late]
+        [small(self_output), small(cross_query), small(cross_key), small(cross_value), small(cross_output)],
+        2, 128)
+    out_self, query_cross, key_cross, value_cross, out_cross = [flat(w) for w in late]
     norm_params = early[3].reshape(pairs * 2, 16, -1, 128)[:, :6, :, :piece].transpose(1, 0, 2, 3)
     norm_params = norm_params.reshape(6, width).astype(jnp.float32)
 
@@ -1031,7 +1053,11 @@
     cross_logs = cross_logs[:, : 2 * half_heads]
     resid_two = resid_one + matmul(cross_mix, out_cross)
     hidden_three = norm_forward(resid_two, norm_params[4], norm_params[5]).astype(jnp.bfloat16)
-    layer_out, grad_three, up_grad, down_grad = feed(hidden_three, cotangent, resid_two, up_full, down_full)
+    layer_out, grad_three, up_grad, down_grad = feed(hidden_three, cotangent, resid_two, up_blocks, down_blocks)
+    up_sum, down_sum = [
+        lax.psum_scatter(g.reshape(-1, *g.shape[2:]), everyone, scatter_dimension=0).astype(jnp.float32)
+        for g in (up_grad, down_grad)
+    ]
 
     def stats_of(logs, mix, grad):
         products = mix.astype(jnp.float32) * grad.astype(jnp.float32)
@@ -1102,15 +1128,14 @@
         return grad.astype(jnp.bfloat16).reshape(pairs, 2, parts, -1, grad.shape[-1])
 
     early_sums = scatter_blocks(
-        [by_place(g, 1) for g in (self_out_grad, cross_query_part, cross_key_part, cross_value_part, cross_out_grad, up_grad)]
-        + [by_place(down_grad, down_weight.shape[0] // block_rows)], 4, 256)
+        [by_place(g, 1) for g in (self_out_grad, cross_query_part, cross_key_part, cross_value_part, cross_out_grad)], 4, 128)
     late_sums = scatter_blocks(
         [by_place(g, 1) for g in (self_query_part, self_key_part, self_value_part)]
         + [by_place(norm_grads.reshape(2 * pairs * 16, -1), 1)], 3, 128)
     norm_parts = late_sums[3][0, :6, :piece]
     sums = late_sums[:3] + early_sums
     sums = [total.reshape(-1, total.shape[-1]) for total in sums]
-    return (layer_out, input_grad, text_grad, *sums, *norm_parts)
+    return (layer_out, input_grad, text_grad, *sums, up_sum, down_sum, *norm_parts)
 
 
 def local(*arrays):

time: 795 us -> 722 us (0.908)
  Pallas kernels: 551 us -> 459 us
  between operations: 2.7 us -> 15.6 us
  waiting for transfers between devices: 32.8 us -> 45.2 us
  local copies, waits for them, and re-layouts: 65.9 us -> 57.6 us
    pallas_call x2, Pallas kernels: 212 us -> 149 us  [scatter_blocks(): pl.pallas_call(functools.partial(scatter_kernel, units, count), out_shape...]
    pallas_call x2, Pallas kernels: 192 us -> 163 us  [gather_blocks(): pl.pallas_call(functools.partial(gather_kernel, units, count), out_shape=...]
    unnamed x257 -> x249, local copies, waits for them, and re-layouts: 23.5 us -> 18.8 us
  transfers between devices with their start and end apart: 12 -> 16, of which waited for: 4 -> 5; matrix products, arithmetic and copies ran while one was open for 8% -> 21% of each run, Pallas kernels for 52% -> 57%
where the time goes in v3:
time: 722 us; the launch traced here: 714 us
  Pallas kernels  459 us (64%)
  matrix products  65.4 us (9%)
  local copies, waits for them, and re-layouts  57.6 us (8%)
  waiting for transfers between devices  45.2 us (6%)
  other arithmetic  44.3 us (6%)
  starting transfers between devices  26.7 us (4%)
  between operations  15.6 us (2%)
    pallas_call x2, Pallas kernels, gather_blocks(): pl.pallas_call(functools.partial(gather_kernel, units, count), out_shape=...  163 us
    pallas_call x2, Pallas kernels, scatter_blocks(): pl.pallas_call(functools.partial(scatter_kernel, units, count), out_shape...  149 us
    pallas_call x3, Pallas kernels, attend_back(): pl.pallas_call(functools.partial(attend_back_kernel, causal, tile), grid=...  54.5 us
    pallas_call x1, Pallas kernels, feed(): pl.pallas_call(feed_kernel, grid=(ff // chunk,), in_specs=[whole, whole,...  49 us
    pallas_call x3, Pallas kernels, attend(): pl.pallas_call(functools.partial(attend_kernel, causal, tile), grid=(widt...  43.1 us
    dot_general x8, matrix products, over_tokens(): lax.dot_general(left, right, (((0,), (0,)), ((), ())), preferred_element_...  28.8 us
    ppermute x5, waiting for transfers between devices, home(): return lax.ppermute(array, 'row', back_perm)  25.3 us
    dot_general x8, matrix products, by_transposed(): lax.dot_general(left, right, (((1,), (1,)), ((), ())), preferred_element_...  22.9 us
  transfers between devices with their start and end apart: 16, of which 5 were waited for; matrix products, arithmetic and copies ran while one was open for 21% of the time, Pallas kernels for 57%

profile of v3, /device:TPU:0, one launch (start us, length us, event | category | flops | bytes accessed | tf_op | source)
XLA Modules:
  0.0 713.6 jit_solution(893290243349389111)
XLA Ops:
  13.1 58.6 %shard_map.330 = (bf16[4,2,1,128,1024]{4,3,2,1,0:T(8,128)(2,1)}, bf16[4,2,1,128,1024]{4,3,2,1,0:T(8,128)(2,1)}, bf16[4,2,1,128,1024]{4,3,2,1,0:T(8,128)(2,1)}, bf16[4,2,1,16,512]{4,3,2,1,0:T(8,128)(2,1)}) custom-call(bf16[1,128,256]{2,1,0:T(8,128)(2,1)} %bitcast.160, bf16[1,128,256]{2,1,0:T(8,128)(2,1)} %bitcast.161, bf16[1,128,256]{2,1,0:T(8,128)(2,1)} %bitcast.162, ...), custom_call_target="tpu_custom_call" | custom-call | bytes 12845056 | tf_op jit(solution)/shard_map/pallas_call | solution.py:775
  91.3 19.9 %shard_map.331 = (f32[750,1024]{1,0:T(8,128)S(1)}, f32[750,128]{1,0:T(8,128)S(1)}) custom-call(bf16[750,1024]{1,0:T(8,128)(2,1)S(1)} %convolution_convert_fusion.13.q_ref, bf16[750,1024]{1,0:T(8,128)(2,1)S(1)} %convolution_convert_fusion.12.k_ref, bf16[750,1024]{1,0:T(8,128)(2,1)S(1)} %convolution_convert_fusion.11.v_ref), custom_call_target="tpu_custom_call" | custom-call | flops 2304000000 | bytes 6144000 | tf_op jit(solution)/shard_map/pallas_call | solution.py:484
  112.3 104.5 %shard_map.333 = (bf16[4,2,1,128,1024]{4,3,2,1,0:T(8,128)(2,1)}, bf16[4,2,1,128,1024]{4,3,2,1,0:T(8,128)(2,1)}, bf16[4,2,1,128,1024]{4,3,2,1,0:T(8,128)(2,1)}, b...) custom-call(bf16[1,128,256]{2,1,0:T(8,128)(2,1)} %bitcast.163, bf16[1,128,256]{2,1,0:T(8,128)(2,1)} %bitcast.164, ...), custom_call_target="tpu_custom_call" | custom-call | bytes 20971520 | tf_op jit(solution)/shard_map/pallas_call | solution.py:775
  222.1 11.7 %shard_map.332 = (bf16[750,512]{1,0:T(8,128)(2,1)}, f32[750,128]{1,0:T(8,128)S(1)}) custom-call(bf16[750,512]{1,0:T(8,128)(2,1)S(1)} %slice_select_fusion.3.q_ref, bf16[750,512]{1,0:T(8,128)(2,1)S(1)} %slice_select_fusion.2.k_ref, bf16[750,512]{1,0:T(8,128)(2,1)S(1)} %slice_select_fusion.1.v_ref), custom_call_target="tpu_custom_call" | custom-call | flops 1152000000 | bytes 3072000 | tf_op jit(solution)/shard_map/pallas_call | solution.py:484
  233.8 3.8 collective-permute-start.3
  240.7 6.1 collective-permute-done.3
  263.2 4.6 add_convert_fusion.5
  274.2 11.4 %shard_map.334 = (bf16[750,1024]{1,0:T(8,128)(2,1)S(1)}, f32[750,128]{1,0:T(8,128)S(1)}) custom-call(bf16[750,1024]{1,0:T(8,128)(2,1)S(1)} %convolution_convert_fusion.10.q_ref, bf16[64,1024]{1,0:T(8,128)(2,1)S(1)} %convolution_convert_fusion.15.k_ref, bf16[64,1024]{1,0:T(8,128)(2,1)S(1)} %convolution_convert_fusion.14.v_ref), custom_call_target="tpu_custom_call" | custom-call | flops 196608000 | bytes 6144000 | tf_op jit(solution)/shard_map/pallas_call | solution.py:484
  290.9 49.0 %shard_map.335 = (bf16[750,1024]{1,0:T(8,128)(2,1)}, f32[750,1024]{1,0:T(8,128)}, bf16[8,4,128,1024]{3,2,1,0:T(8,128)(2,1)}, bf16[8,4,512,256]{3,2,1,0:T(8,128)(2,1)}) custom-call(bf16[750,1024]{1,0:T(8,128)(2,1)} %add_convert_fusion.3.h_ref, bf16[750,1024]{1,0:T(8,128)(2,1)} %cot_ref.1, f32[750,1024]{1,0:T(8,128)} %copy-done.25, ...), custom_call_target="tpu_custom_call" | custom-call | flops 37748736000 | bytes 45842432 | tf_op jit(solution)/shard_map/pallas_call | solution.py:566
  341.9 4.4 multiply_reduce_fusion
  346.4 4.0 fusion.36
  366.0 10.2 %shard_map.336 = (bf16[750,1024]{1,0:T(8,128)(2,1)S(1)}, bf16[64,1024]{1,0:T(8,128)(2,1)S(1)}, bf16[64,1024]{1,0:T(8,128)(2,1)S(1)}) custom-call(bf16[750,1024]{1,0:T(8,128)(2,1)S(1)} %convolution_convert_fusion.10.q_ref, bf16[64,1024]{1,0:T(8,128)(2,1)S(1)} %convolution_convert_fusion.15.k_ref, bf16[64,1024]{1,0:T(8,128)(2,1)S(1)} %convolution_convert_fusion.14.v_ref, ...), custom_call_target="tpu_custom_call" | custom-call | flops 491520000 | bytes 12288000 | tf_op jit(solution)/shard_map/pallas_call | solution.py:527
  379.5 4.6 multiply_reduce_fusion.1
  405.2 5.0 convolution_convert_fusion.4
  410.3 30.1 %shard_map.337 = (f32[750,1024]{1,0:T(8,128)S(1)}, f32[750,1024]{1,0:T(8,128)S(1)}, f32[750,1024]{1,0:T(8,128)}) custom-call(bf16[750,1024]{1,0:T(8,128)(2,1)S(1)} %copy-done.7, bf16[750,1024]{1,0:T(8,128)(2,1)S(1)} %copy-done.1, bf16[750,1024]{1,0:T(8,128)(2,1)S(1)} %copy-done.4, bf16[750,1024]{1,0:T(8,128)(2,1)S(1)} %get-tuple-element.143.do_ref, ...), custom_call_target="tpu_custom_call" | custom-call | flops 5760000000 | bytes 12288000 | tf_op jit(solution)/shard_map/pallas_call | solution.py:527
  457.1 99.1 %shard_map.340 = (f32[1,128,256]{2,1,0:T(8,128)}, f32[1,128,256]{2,1,0:T(8,128)}, f32[1,128,256]{2,1,0:T(8,128)}, f32[1,128,256]{2,1,0:T(8,128)}, f32[1,128,256]{2,1,0:T(8,128)}) custom-call(bf16[4,2,1,128,1024]{4,3,2,1,0:T(8,128)(2,1)} %bitcast.140, bf16[4,2,1,128,1024]{4,3,2,1,0:T(8,128)(2,1)} %bitcast.141, bf16[4,2,1,128,1024]{4,3,2,1,0:T(8,128)(2,1)} %bitcast.131, ...), custom_call_target="tpu_custom_call" | custom-call | flops 5242880 | bytes 20971520 | tf_op jit(solution)/shard_map/pallas_call | solution.py:950
  558.9 14.2 %shard_map.338 = (bf16[750,512]{1,0:T(8,128)(2,1)S(1)}, bf16[750,512]{1,0:T(8,128)(2,1)S(1)}, bf16[750,512]{1,0:T(8,128)(2,1)S(1)}) custom-call(bf16[750,512]{1,0:T(8,128)(2,1)S(1)} %copy-done.13, bf16[750,512]{1,0:T(8,128)(2,1)S(1)} %copy-done.9, bf16[750,512]{1,0:T(8,128)(2,1)S(1)} %copy-done.11, bf16[750,512]{1,0:T(8,128)(2,1)S(1)} %slice_select_fusion.do_ref, ...), custom_call_target="tpu_custom_call" | custom-call | flops 2880000000 | bytes 6144000 | tf_op jit(solution)/shard_map/pallas_call | solution.py:527
  579.3 11.8 %collective-permute-done.8 = bf16[750,512]{1,0:T(8,128)(2,1)S(1)} collective-permute-done((bf16[750,512]{1,0:T(8,128)(2,1)S(1)}, bf16[750,512]{1,0:T(8,128)(2,1)S(1)}, u32[]{:S(2)}, u32[]{:S(2)}) %collective-permute-start.8) | collective-permute-done | bytes 768032 | tf_op jit(solution)/shard_map/ppermute | solution.py:984
  593.0 12.8 %collective-permute-done.9 = bf16[750,512]{1,0:T(8,128)(2,1)S(1)} collective-permute-done((bf16[750,512]{1,0:T(8,128)(2,1)S(1)}, bf16[750,512]{1,0:T(8,128)(2,1)S(1)}, u32[]{:S(2)}, u32[]{:S(2)}) %collective-permute-start.9) | collective-permute-done | bytes 768032 | tf_op jit(solution)/shard_map/ppermute | solution.py:987
  607.7 12.5 %collective-permute-done.10 = bf16[750,512]{1,0:T(8,128)(2,1)S(1)} collective-permute-done((bf16[750,512]{1,0:T(8,128)(2,1)S(1)}, bf16[750,512]{1,0:T(8,128)(2,1)S(1)}, u32[]{:S(2)}, u32[]{:S(2)}) %collective-permute-start.10) | collective-permute-done | bytes 768032 | tf_op jit(solution)/shard_map/ppermute | solution.py:987
  620.2 4.0 fusion.34
  628.5 6.3 convolution_convert_fusion.7
  641.7 50.2 %shard_map.339 = (f32[1,128,256]{2,1,0:T(8,128)}, f32[1,128,256]{2,1,0:T(8,128)}, f32[1,128,256]{2,1,0:T(8,128)}, f32[1,16,128]{2,1,0:T(8,128)}) custom-call(bf16[4,2,1,128,1024]{4,3,2,1,0:T(8,128)(2,1)} %bitcast.143, bf16[4,2,1,128,1024]{4,3,2,1,0:T(8,128)(2,1)} %bitcast.145, bf16[4,2,1,128,1024]{4,3,2,1,0:T(8,128)(2,1)} %bitcast.144, ...), custom_call_target="tpu_custom_call" | custom-call | flops 3211264 | bytes 12845056 | tf_op jit(solution)/shard_map/pallas_call | solution.py:950
  693.3 4.6 add_add_fusion.3
  (388 shorter events, 154.5 us)
Async XLA Ops:
  7.2 67.6 %copy-start.26 = (bf16[750,1024]{1,0:T(8,128)(2,1)S(1)}, bf16[750,1024]{1,0:T(8,128)(2,1)}, u32[]{:S(2)}) copy-start(bf16[750,1024]{1,0:T(8,128)(2,1)} %param.21) | copy-start | bytes 4608004
  7.2 283.7 %all-gather.5.cloned.1.call-start = ((), (), s32[]{:S(2)}) async-start(), calls=%async_computation.4 | async-start | bytes 8650752 | tf_op jit(solution)/shard_map/all_gather | solution.py:999
  7.9 282.9 %all-gather.7.cloned.1.call-start = ((), (), s32[]{:S(2)}) async-start(), calls=%async_computation.5 | async-start | bytes 8650752 | tf_op jit(solution)/shard_map/all_gather | solution.py:1000
  8.7 689.3 %reduce-scatter.5.cloned.1.call-start = ((), (), s32[]{:S(2)}) async-start(), calls=%async_computation.3 | async-start | bytes 8650752 | tf_op jit(solution)/shard_map/reduce_scatter | solution.py:1058
  8.7 208.1 %collective-permute-start.5 = (bf16[32,1024]{1,0:T(8,128)(2,1)}, bf16[32,1024]{1,0:T(8,128)(2,1)S(1)}, u32[]{:S(2)}, u32[]{:S(2)}) collective-permute-start(bf16[32,1024]{1,0:T(8,128)(2,1)} %param.22), channel_id=1, source_target_pairs={{0,4},{8,12},{16,20},{24,28},{4,0},{12,8},{20,16},{28,24},{1,5},{9... | collective-permute-start | bytes 196616 | tf_op jit(solution)/shard_map/ppermute | solution.py:1046
  78.3 140.8 %collective-permute-start.1 = (bf16[750,512]{1,0:T(8,128)(2,1)}, bf16[750,512]{1,0:T(8,128)(2,1)}, u32[]{:S(2)}, u32[]{:S(2)}) collective-permute-start(bf16[750,512]{1,0:T(8,128)(2,1)} %slice.159), channel_id=1, source_target_pairs={{0,4},{8,12},{16,20},{24,28},{1,5},{9,13},{17,21},{25,29},{2,6},{1... | collective-permute-start | bytes 2304008 | tf_op jit(solution)/shard_map/ppermute | solution.py:984
  84.7 135.6 %collective-permute-start.2 = (bf16[750,512]{1,0:T(8,128)(2,1)}, bf16[750,512]{1,0:T(8,128)(2,1)}, u32[]{:S(2)}, u32[]{:S(2)}) collective-permute-start(bf16[750,512]{1,0:T(8,128)(2,1)} %slice.161), channel_id=1, source_target_pairs={{0,4},{8,12},{16,20},{24,28},{1,5},{9,13},{17,21},{25,29},{2,6},{1... | collective-permute-start | bytes 2304008 | tf_op jit(solution)/shard_map/ppermute | solution.py:984
  89.8 127.0 %copy-start.55 = (bf16[32,1024]{1,0:T(8,128)(2,1)S(1)}, bf16[32,1024]{1,0:T(8,128)(2,1)}, u32[]{:S(2)}) copy-start(bf16[32,1024]{1,0:T(8,128)(2,1)} %param.22) | copy-start | bytes 196612
  89.8 130.6 %collective-permute-start = (bf16[750,512]{1,0:T(8,128)(2,1)}, bf16[750,512]{1,0:T(8,128)(2,1)}, u32[]{:S(2)}, u32[]{:S(2)}) collective-permute-start(bf16[750,512]{1,0:T(8,128)(2,1)} %slice.156), channel_id=1, source_target_pairs={{4,0},{12,8},{20,16},{28,24},{5,1},{13,9},{21,17},{29,25},{6,2},{1... | collective-permute-start | bytes 2304008 | tf_op jit(solution)/shard_map/ppermute | solution.py:987
  112.1 176.0 %copy-start.76 = (f32[1024]{0:T(1024)}, f32[1024]{0:T(1024)S(1)}, u32[]{:S(2)}) copy-start(f32[1024]{0:T(1024)S(1)} %mul.209) | copy-start | bytes 12292
  112.1 158.1 %copy-start.93 = (f32[1024]{0:T(1024)}, f32[1024]{0:T(1024)S(1)}, u32[]{:S(2)}) copy-start(f32[1024]{0:T(1024)S(1)} %mul.203) | copy-start | bytes 12292
  112.2 158.0 %copy-start.103 = (f32[1024]{0:T(1024)}, f32[1024]{0:T(1024)S(1)}, u32[]{:S(2)}) copy-start(f32[1024]{0:T(1024)S(1)} %add.132) | copy-start | bytes 12292
  233.8 13.0 %collective-permute-start.3 = (f32[750,8]{1,0:T(8,128)S(1)}, f32[750,8]{1,0:T(8,128)S(1)}, u32[]{:S(2)}, u32[]{:S(2)}) collective-permute-start(f32[750,8]{1,0:T(8,128)S(1)} %bitcast.123), channel_id=1, source_target_pairs={{0,4},{8,12},{16,20},{24,28},{1,5},{9,13},{17,21},{25,29},{2,6},{1... | collective-permute-start | bytes 72008 | tf_op jit(solution)/shard_map/ppermute | solution.py:984
  237.6 25.5 %collective-permute-start.4 = (bf16[750,512]{1,0:T(8,128)(2,1)}, bf16[750,512]{1,0:T(8,128)(2,1)}, u32[]{:S(2)}, u32[]{:S(2)}) collective-permute-start(bf16[750,512]{1,0:T(8,128)(2,1)} %get-tuple-element.75), channel_id=1, source_target_pairs={{0,4},{8,12},{16,20},{24,28},{1,5},{9,13},{17,21},{25,29},{2,6},{1... | collective-permute-start | bytes 2304008 | tf_op jit(solution)/shard_map/ppermute | solution.py:984
  339.9 359.9 %reduce-scatter.3.cloned.1.call-start = ((), (), s32[]{:S(2)}) async-start(), calls=%async_computation.2 | async-start | bytes 8650752 | tf_op jit(solution)/shard_map/reduce_scatter | solution.py:1058
  377.1 74.9 %collective-permute-start.11 = (bf16[32,2048]{1,0:T(8,128)(2,1)}, bf16[32,2048]{1,0:T(8,128)(2,1)}, u32[]{:S(2)}, u32[]{:S(2)}) collective-permute-start(bf16[32,2048]{1,0:T(8,128)(2,1)} %broadcast_select_fusion.3), channel_id=1, source_target_pairs={{0,4},{8,12},{16,20},{24,28},{4,0},{12,8},{20,16},{28,24},{1,5},{9... | collective-permute-start | bytes 393224 | tf_op jit(solution)/shard_map/ppermute | solution.py:1079
  403.7 48.2 %collective-permute-start.7 = (f32[4,4,750]{2,1,0:T(4,128)}, f32[4,4,750]{2,1,0:T(4,128)S(1)}, u32[]{:S(2)}, u32[]{:S(2)}) collective-permute-start(f32[4,4,750]{2,1,0:T(4,128)} %slice.146), channel_id=1, source_target_pairs={{4,0},{12,8},{20,16},{28,24},{5,1},{13,9},{21,17},{29,25},{6,2},{1... | collective-permute-start | bytes 144008 | tf_op jit(solution)/shard_map/ppermute | solution.py:987
  410.3 30.1 %copy-start.20 = (bf16[750,1024]{1,0:T(8,128)(2,1)S(1)}, bf16[750,1024]{1,0:T(8,128)(2,1)}, u32[]{:S(2)}) copy-start(bf16[750,1024]{1,0:T(8,128)(2,1)} %copy-done.19) | copy-start | bytes 4608004
  450.6 108.1 %collective-permute-start.6 = (bf16[750,512]{1,0:T(8,128)(2,1)S(1)}, bf16[750,512]{1,0:T(8,128)(2,1)S(1)}, u32[]{:S(2)}, u32[]{:S(2)}) collective-permute-start(bf16[750,512]{1,0:T(8,128)(2,1)S(1)} %slice.166), channel_id=1, source_target_pairs={{4,0},{12,8},{20,16},{28,24},{5,1},{13,9},{21,17},{29,25},{6,2},{1... | collective-permute-start | bytes 2304008 | tf_op jit(solution)/shard_map/ppermute | solution.py:987
  573.1 18.1 %collective-permute-start.8 = (bf16[750,512]{1,0:T(8,128)(2,1)S(1)}, bf16[750,512]{1,0:T(8,128)(2,1)S(1)}, u32[]{:S(2)}, u32[]{:S(2)}) collective-permute-start(bf16[750,512]{1,0:T(8,128)(2,1)S(1)} %get-tuple-element.87), channel_id=1, source_target_pairs={{0,4},{8,12},{16,20},{24,28},{1,5},{9,13},{17,21},{25,29},{2,6},{1... | collective-permute-start | bytes 2304008 | tf_op jit(solution)/shard_map/ppermute | solution.py:984
  576.4 29.4 %collective-permute-start.9 = (bf16[750,512]{1,0:T(8,128)(2,1)S(1)}, bf16[750,512]{1,0:T(8,128)(2,1)S(1)}, u32[]{:S(2)}, u32[]{:S(2)}) collective-permute-start(bf16[750,512]{1,0:T(8,128)(2,1)S(1)} %get-tuple-element.89), channel_id=1, source_target_pairs={{4,0},{12,8},{20,16},{28,24},{5,1},{13,9},{21,17},{29,25},{6,2},{1... | collective-permute-start | bytes 2304008 | tf_op jit(solution)/shard_map/ppermute | solution.py:987
  577.7 42.5 %collective-permute-start.10 = (bf16[750,512]{1,0:T(8,128)(2,1)S(1)}, bf16[750,512]{1,0:T(8,128)(2,1)S(1)}, u32[]{:S(2)}, u32[]{:S(2)}) collective-permute-start(bf16[750,512]{1,0:T(8,128)(2,1)S(1)} %get-tuple-element.91), channel_id=1, source_target_pairs={{4,0},{12,8},{20,16},{28,24},{5,1},{13,9},{21,17},{29,25},{6,2},{1... | collective-permute-start | bytes 2304008 | tf_op jit(solution)/shard_map/ppermute | solution.py:987
  579.3 40.9 %copy-start.45 = (bf16[750,512]{1,0:T(8,128)(2,1)}, bf16[750,512]{1,0:T(8,128)(2,1)S(1)}, u32[]{:S(2)}) copy-start(bf16[750,512]{1,0:T(8,128)(2,1)S(1)} %get-tuple-element.145) | copy-start | bytes 2304004
  641.6 51.6 %copy-start.30 = (bf16[750,1024]{1,0:T(8,128)(2,1)S(1)}, bf16[750,1024]{1,0:T(8,128)(2,1)}, u32[]{:S(2)}) copy-start(bf16[750,1024]{1,0:T(8,128)(2,1)} %param.21) | copy-start | bytes 4608004
  (109 other events, 888.3 us)
Sparse Core Ops, SparseCore 0:
  10.9 86.3 all-gather.4
  100.2 102.7 all-gather.6
  340.0 151.5 reduce-scatter.4
  493.8 152.8 reduce-scatter.2

commit v4 on v3

--- a/solution.py
+++ b/solution.py
@@ -965,6 +965,227 @@
     )(*grads)
 
 
+def attend_rows(q, key_ref, value_ref, spans, diagonal, put):
+    low = lax.broadcasted_iota(jnp.int32, (1, 128), 1) < HEAD_DIM
+    mixed, logs = [], []
+    for h in range(2):
+        mine = low if h == 0 else jnp.logical_not(low)
+        qh = jnp.where(mine, q, jnp.bfloat16(0))
+        scores = []
+        for at, length in spans:
+            s = dg(qh, key_ref[at : at + length, :], NT)
+            if at == diagonal:
+                allowed = lax.broadcasted_iota(jnp.int32, s.shape, 0) >= lax.broadcasted_iota(jnp.int32, s.shape, 1)
+                s = jnp.where(allowed, s, -1e30)
+            scores.append(s)
+        top = functools.reduce(jnp.maximum, [jnp.max(s, axis=1, keepdims=True) for s in scores])
+        out = None
+        for (at, length), s in zip(spans, scores):
+            p = jnp.exp(s - top).astype(jnp.bfloat16)
+            value = value_ref[at : at + length, :]
+            part = dg(p, jnp.where(mine, value, jnp.ones_like(value)), NN)
+            out = part if out is None else out + part
+        total = out[:, HEAD_DIM : HEAD_DIM + 1] if h == 0 else out[:, 0:1]
+        mixed.append(out / total)
+        logs.append(top + jnp.log(total))
+    put(logs)
+    return jnp.where(low, mixed[0], mixed[1])
+
+
+def rows_of(lanes_ref, first):
+    picked = lax.broadcasted_iota(jnp.int32, (8, 128), 0) + first == lax.broadcasted_iota(jnp.int32, (8, 128), 1)
+    return lax.dot_general(
+        picked.astype(jnp.float32), lanes_ref[...], NT, precision=lax.Precision.HIGHEST,
+        preferred_element_type=jnp.float32)
+
+
+def pair_attend_kernel(tile, q_ref, k_ref, v_ref, q_any, k_any, v_any, mix_ref, logs_ref, fq_out, fk_out, fv_out,
+                       near, near_logs, far_q, far_k, far_v, far, far_logs, got, far_rows, got_rows,
+                       send, recv, local, keep):
+    step = pl.program_id(0)
+    place = Place()
+    pairs = near.shape[0]
+    fars = pairs // 2
+    rows = q_ref.shape[0]
+    first, second = place.y == 0, place.y == 1
+    partner = place.across("y")
+    lane = lax.broadcasted_iota(jnp.int32, (1, 128), 1)
+    scale = jnp.bfloat16(HEAD_DIM**-0.5)
+    plan = ((q_any, far_q, False), (k_any, far_k, True), (v_any, far_v, True))
+
+    def columns(pair):
+        return pl.ds(pl.multiple_of(pair * 128, 128), 128)
+
+    def sending(which, j):
+        array, landing, by_first = plan[which]
+        return pltpu.make_async_remote_copy(
+            src_ref=array.at[:, columns(j if by_first else fars + j)], dst_ref=landing.at[j],
+            send_sem=send.at[which, j], recv_sem=recv.at[which, j], device_id=partner, device_id_type=MESH)
+
+    def keeping(which, j):
+        array, landing, by_first = plan[which]
+        return pltpu.make_async_copy(
+            array.at[:, columns(fars + j if by_first else j)], landing.at[j], local.at[which, j])
+
+    def mixture_out(j):
+        return pltpu.make_async_remote_copy(
+            src_ref=far.at[j], dst_ref=got.at[j], send_sem=send.at[3, j], recv_sem=recv.at[3, j],
+            device_id=partner, device_id_type=MESH)
+
+    def logs_out():
+        return pltpu.make_async_remote_copy(
+            src_ref=far_rows, dst_ref=got_rows, send_sem=send.at[4, 0], recv_sem=recv.at[4, 0],
+            device_id=partner, device_id_type=MESH)
+
+    def saving(which):
+        return pltpu.make_async_copy(plan[which][1], (fq_out, fk_out, fv_out)[which], keep.at[which])
+
+    @pl.when(step == 0)
+    def _():
+        barrier = pltpu.get_barrier_semaphore()
+        pl.semaphore_signal(barrier, inc=1, device_id=partner, device_id_type=MESH)
+        pl.semaphore_wait(barrier, 1)
+        near_logs[...] = jnp.zeros_like(near_logs)
+        far_logs[...] = jnp.zeros_like(far_logs)
+        for j in range(fars):
+            for which in range(3):
+
+                @pl.when(first if plan[which][2] else second)
+                def _(which=which, j=j):
+                    keeping(which, j).start()
+
+    @pl.when((step % 3 == 0) & (step < 3 * fars))
+    def _():
+        j = step // 3
+        for which in range(3):
+
+            @pl.when(first if plan[which][2] else second)
+            def _(which=which):
+                @pl.when(j > 0)
+                def _():
+                    sending(which, j - 1).wait_send()
+
+                sending(which, j).start()
+
+    @pl.when(step < pairs)
+    def _():
+        for start in range(0, rows, tile):
+            n = min(tile, rows - start)
+
+            def put(logs, start=start, n=n):
+                kept = near_logs[start : start + n, :]
+                for h in range(2):
+                    kept = jnp.where(lane == 2 * step + h, logs[h], kept)
+                near_logs[start : start + n, :] = kept
+
+            spans = ([(0, start)] if start else []) + [(start, n)]
+            near[step, start : start + n, :] = attend_rows(
+                q_ref[start : start + n, :] * scale, k_ref, v_ref, spans, start, put)
+
+    @pl.when((step >= pairs) & (step < pairs + fars))
+    def _():
+        j = step - pairs
+        for which in range(3):
+            by_first = plan[which][2]
+
+            @pl.when(first if by_first else second)
+            def _(which=which):
+                keeping(which, j).wait()
+
+            @pl.when(second if by_first else first)
+            def _(which=which):
+                sending(which, j).wait_recv()
+
+        base = jnp.where(first, 2 * fars, 0)
+        for start in range(0, rows, tile):
+            n = min(tile, rows - start)
+
+            def put(logs, start=start, n=n):
+                kept = far_logs[start : start + n, :]
+                for h in range(2):
+                    kept = jnp.where(lane == base + 2 * j + h, logs[h], kept)
+                far_logs[start : start + n, :] = kept
+
+            far[j, start : start + n, :] = attend_rows(
+                far_q[j, start : start + n, :] * scale, far_k.at[j], far_v.at[j], [(0, rows)], None, put
+            ).astype(far.dtype)
+
+        @pl.when(first)
+        def _():
+            mixture_out(j).start()
+
+    @pl.when(step == pairs + fars)
+    def _():
+        for which in range(3):
+            saving(which).start()
+
+        @pl.when(first)
+        def _():
+            far_rows[...] = rows_of(far_logs, 2 * fars)
+            logs_out().start()
+            for pair in range(pairs):
+                mix_ref[:, pair * 128 : (pair + 1) * 128] = near[pair].astype(mix_ref.dtype)
+            logs_ref[...] = near_logs[...]
+            logs_out().wait_send()
+            for j in range(fars):
+                mixture_out(j).wait_send()
+            for which in (1, 2):
+                sending(which, fars - 1).wait_send()
+
+        @pl.when(second)
+        def _():
+            logs_out().wait_recv()
+            for j in range(fars):
+                mixture_out(j).wait_recv()
+            sending(0, fars - 1).wait_send()
+            spread_out = (lax.broadcasted_iota(jnp.int32, (8, 128), 0) + 2 * fars == lane).astype(jnp.float32)
+            theirs = lax.dot_general(
+                got_rows[...], spread_out, TN, precision=lax.Precision.HIGHEST, preferred_element_type=jnp.float32)
+            logs_far = far_logs[...] + theirs
+            logs_near = near_logs[...]
+            top = jnp.maximum(logs_near, logs_far)
+            total = top + jnp.log(jnp.exp(logs_near - top) + jnp.exp(logs_far - top))
+            logs_ref[...] = total
+            share = jnp.exp(logs_near - total)
+            low = lane < HEAD_DIM
+            for pair in range(pairs):
+                part = jnp.where(low, share[:, 2 * pair : 2 * pair + 1], share[:, 2 * pair + 1 : 2 * pair + 2])
+                other = (far[pair] if pair < fars else got[pair - fars]).astype(jnp.float32)
+                mix_ref[:, pair * 128 : (pair + 1) * 128] = (other + (near[pair] - other) * part).astype(mix_ref.dtype)
+
+        for which in range(3):
+            saving(which).wait()
+
+
+def pair_attend(q, k, v, collective_id, tile=384):
+    rows, width = q.shape
+    pairs = width // 128
+    fars = pairs // 2
+    block = pl.BlockSpec((rows, 128), lambda i: (0, jnp.minimum(i, pairs - 1)))
+    anywhere = pl.BlockSpec(memory_space=pl.ANY)
+    kept = jax.ShapeDtypeStruct((fars, rows, 128), jnp.bfloat16)
+    half = pltpu.VMEM((fars, rows, 128), jnp.bfloat16)
+    return pl.pallas_call(
+        functools.partial(pair_attend_kernel, tile),
+        grid=(pairs + fars + 1,),
+        in_specs=[block] * 3 + [anywhere] * 3,
+        out_specs=[pl.BlockSpec((rows, width), lambda i: (0, 0)), pl.BlockSpec((rows, 128), lambda i: (0, 0))] + [anywhere] * 3,
+        out_shape=[
+            jax.ShapeDtypeStruct((rows, width), jnp.bfloat16), jax.ShapeDtypeStruct((rows, 128), jnp.float32), kept, kept, kept],
+        scratch_shapes=[
+            pltpu.VMEM((pairs, rows, 128), jnp.float32), pltpu.VMEM((rows, 128), jnp.float32),
+            half, half, half, half, pltpu.VMEM((rows, 128), jnp.float32), half,
+            pltpu.VMEM((8, rows), jnp.float32), pltpu.VMEM((8, rows), jnp.float32),
+            pltpu.SemaphoreType.DMA((5, fars)), pltpu.SemaphoreType.DMA((5, fars)),
+            pltpu.SemaphoreType.DMA((3, fars)), pltpu.SemaphoreType.DMA((3,)),
+        ],
+        compiler_params=pltpu.CompilerParams(
+            collective_id=collective_id, has_side_effects=True, vmem_limit_bytes=48 << 20),
+        cost_estimate=pl.CostEstimate(
+            flops=4 * rows * rows * width, bytes_accessed=16 * rows * width, transcendentals=rows * rows * pairs * 2),
+    )(q, k, v, q, k, v)
+
+
 def fast(
     frames_in, text_states, self_query, self_key, self_value, self_output, cross_query, cross_key, cross_value, cross_output,
     up_weight, down_weight, first_gain, first_bias, second_gain, second_bias, third_gain, third_bias, cotangent,
@@ -1007,10 +1228,9 @@
 
     early = gather_blocks([small(self_query), small(self_key), small(self_value), gains], 1, 128)
     query_self, key_self, value_self = [flat(w) for w in early[:3]]
-    late = gather_blocks(
-        [small(self_output), small(cross_query), small(cross_key), small(cross_value), small(cross_output)],
-        2, 128)
-    out_self, query_cross, key_cross, value_cross, out_cross = [flat(w) for w in late]
+    between = jnp.stack([self_output, cross_query, cross_key, cross_value, cross_output])
+    between = lax.all_gather(between, everyone).reshape(*places, *between.shape).transpose(2, 0, 3, 1, 4)
+    out_self, query_cross, key_cross, value_cross, out_cross = between.reshape(-1, width, width)
     norm_params = early[3].reshape(pairs * 2, 16, -1, 128)[:, :6, :, :piece].transpose(1, 0, 2, 3)
     norm_params = norm_params.reshape(6, width).astype(jnp.float32)
 
@@ -1019,27 +1239,10 @@
     self_k = matmul(hidden_one, key_self).astype(jnp.bfloat16)
     self_v = matmul(hidden_one, value_self).astype(jnp.bfloat16)
     self_q = matmul(hidden_one, query_self).astype(jnp.bfloat16)
-    sent_k, sent_v, sent_q = forth(self_k[:, :half]), forth(self_v[:, :half]), home(self_q[:, half:])
-    near_mix, near_logs = attend(self_q, self_k, self_v, True, jnp.float32)
-    far_q = by_side(sent_q, self_q[:, :half])
-    far_k = by_side(self_k[:, half:], sent_k)
-    far_v = by_side(self_v[:, half:], sent_v)
-    far_mix, far_logs = attend(far_q, far_k, far_v, False, jnp.bfloat16)
+    self_mix, log_lanes, far_q, far_k, far_v = pair_attend(self_q, self_k, self_v, 5)
     half_heads = half // HEAD_DIM
-    far_logs = far_logs[:, :half_heads]
-    near_logs = near_logs[:, : 2 * half_heads]
-    far_mix = jnp.concatenate([far_mix, forth(far_mix)], axis=1)
-    far_logs = by_side(-1e30, jnp.concatenate([far_logs, forth(far_logs)], axis=1))
-    highest = jnp.maximum(near_logs, far_logs)
-    self_logs = highest + jnp.log(jnp.exp(near_logs - highest) + jnp.exp(far_logs - highest))
-
-    def per_feature(weights):
-        return jnp.repeat(weights, HEAD_DIM, axis=1)
-
-    self_mix = (
-        near_mix * per_feature(jnp.exp(near_logs - self_logs))
-        + by_side(0.0, far_mix.astype(jnp.float32)) * per_feature(jnp.exp(far_logs - self_logs))
-    ).astype(jnp.bfloat16)
+    self_logs = log_lanes[:, : 2 * half_heads]
+    far_q, far_k, far_v = [a.transpose(1, 0, 2).reshape(rows, half) for a in (far_q, far_k, far_v)]
     resid_one = frames + matmul(self_mix, out_self)
     hidden_two = norm_forward(resid_one, norm_params[2], norm_params[3]).astype(jnp.bfloat16)
     cross_q = matmul(hidden_two, query_cross).astype(jnp.bfloat16)

time: 722 us -> 702 us (0.972)
  Pallas kernels: 459 us -> 370 us
  waiting for transfers between devices: 45.2 us -> 123 us
  local copies, waits for them, and re-layouts: 57.6 us -> 71.9 us
  starting transfers between devices: 26.7 us -> 13.8 us
  other arithmetic: 44.3 us -> 33.6 us
    pallas_call x2 -> x1, Pallas kernels: 163 us -> 58.8 us  [gather_blocks(): pl.pallas_call(functools.partial(gather_kernel, units, count), out_shape=...]
    all_gather x1, waiting for transfers between devices: 0.01 us -> 79 us  [fast(): lax.all_gather(down_weight, everyone).reshape(*places, *down_weight.shape)]
    pallas_call x0 -> x1, Pallas kernels: none -> 58.3 us  [pair_attend(): pl.pallas_call(functools.partial(pair_attend_kernel, tile), grid=(pairs +...]
    pallas_call x3 -> x1, Pallas kernels: 43.1 us -> 11.4 us  [attend(): pl.pallas_call(functools.partial(attend_kernel, causal, tile), grid=(widt...]
    pallas_call x2, Pallas kernels: 149 us -> 139 us  [scatter_blocks(): pl.pallas_call(functools.partial(scatter_kernel, units, count), out_shape...]
    ppermute x5 -> x1, starting transfers between devices: 14.1 us -> 3.6 us  [forth(): return lax.ppermute(array, 'row', forth_perm)]
    reshape x2 -> x1, local copies, waits for them, and re-layouts: 7.06 us -> 16.4 us  [fast(): lax.all_gather(between, everyone).reshape(*places, *between.shape)]
    unnamed x249 -> x227, local copies, waits for them, and re-layouts: 18.8 us -> 25 us
  transfers between devices with their start and end apart: 16 -> 12, of which waited for: 5 -> 5; matrix products, arithmetic and copies ran while one was open for 21% -> 21% of each run, Pallas kernels for 57% -> 46%
where the time goes in v4:
time: 702 us; the launch traced here: 695 us
  Pallas kernels  370 us (53%)
  waiting for transfers between devices  123 us (18%)
  local copies, waits for them, and re-layouts  71.9 us (10%)
  matrix products  66.3 us (9%)
  other arithmetic  33.6 us (5%)
  between operations  15.6 us (2%)
  starting transfers between devices  13.8 us (2%)
    pallas_call x2, Pallas kernels, scatter_blocks(): pl.pallas_call(functools.partial(scatter_kernel, units, count), out_shape...  139 us
    all_gather x1, waiting for transfers between devices, fast(): lax.all_gather(down_weight, everyone).reshape(*places, *down_weight.shape)  79 us
    pallas_call x1, Pallas kernels, gather_blocks(): pl.pallas_call(functools.partial(gather_kernel, units, count), out_shape=...  58.8 us
    pallas_call x1, Pallas kernels, pair_attend(): pl.pallas_call(functools.partial(pair_attend_kernel, tile), grid=(pairs +...  58.3 us
    pallas_call x3, Pallas kernels, attend_back(): pl.pallas_call(functools.partial(attend_back_kernel, causal, tile), grid=...  54.4 us
    pallas_call x1, Pallas kernels, feed(): pl.pallas_call(feed_kernel, grid=(ff // chunk,), in_specs=[whole, whole,...  49 us
    dot_general x8, matrix products, over_tokens(): lax.dot_general(left, right, (((0,), (0,)), ((), ())), preferred_element_...  28.9 us
    ppermute x4, waiting for transfers between devices, home(): return lax.ppermute(array, 'row', back_perm)  25.4 us
  transfers between devices with their start and end apart: 12, of which 5 were waited for; matrix products, arithmetic and copies ran while one was open for 21% of the time, Pallas kernels for 46%

profile of v4, /device:TPU:0, one launch (start us, length us, event | category | flops | bytes accessed | tf_op | source)
XLA Modules:
  0.0 694.9 jit_solution(10524718173700601855)
XLA Ops:
  18.3 58.8 %shard_map.330 = (bf16[4,2,1,128,1024]{4,3,2,1,0:T(8,128)(2,1)}, bf16[4,2,1,128,1024]{4,3,2,1,0:T(8,128)(2,1)}, bf16[4,2,1,128,1024]{4,3,2,1,0:T(8,128)(2,1)}, bf16[4,2,1,16,512]{4,3,2,1,0:T(8,128)(2,1)}) custom-call(bf16[1,128,256]{2,1,0:T(8,128)(2,1)} %bitcast.242, bf16[1,128,256]{2,1,0:T(8,128)(2,1)} %bitcast.243, bf16[1,128,256]{2,1,0:T(8,128)(2,1)} %bitcast.244, ...), custom_call_target="tpu_custom_call" | custom-call | bytes 12845056 | tf_op jit(solution)/shard_map/pallas_call | solution.py:775
  88.0 58.3 %shard_map.331 = (bf16[750,1024]{1,0:T(8,128)(2,1)S(1)}, f32[750,128]{1,0:T(8,128)S(1)}, bf16[4,750,128]{2,1,0:T(8,128)(2,1)S(1)}, bf16[4,750,128]{2,1,0:T(8,128)(2,1)S(1)}, bf16[4,750,128]{2,1,0:T(8,128)(2,1)S(1)}) custom-call(bf16[750,1024]{1,0:T(8,128)(2,1)S(1)} %convolution_convert_fusion.10.q_ref.q_any, ...), custom_call_target="tpu_custom_call" | custom-call | flops 2304000000 | bytes 12288000 | tf_op jit(solution)/shard_map/pallas_call | solution.py:1168
  149.1 16.4 %copy.55 = bf16[8,4,5,128,256]{3,0,4,1,2:T(8,128)(2,1)} copy(bf16[8,4,5,128,256]{4,3,2,1,0:T(8,128)(2,1)} %bitcast.204) | data formatting | bytes 20971520 | tf_op jit(solution)/shard_map/reshape | solution.py:1232
  165.5 5.3 fusion.88
  177.2 11.4 %shard_map.332 = (bf16[750,1024]{1,0:T(8,128)(2,1)S(1)}, f32[750,128]{1,0:T(8,128)S(1)}) custom-call(bf16[750,1024]{1,0:T(8,128)(2,1)S(1)} %fusion.50.q_ref, bf16[64,1024]{1,0:T(8,128)(2,1)S(1)} %fusion.56.k_ref, bf16[64,1024]{1,0:T(8,128)(2,1)S(1)} %fusion.59.v_ref), custom_call_target="tpu_custom_call" | custom-call | flops 196608000 | bytes 6144000 | tf_op jit(solution)/shard_map/pallas_call | solution.py:484
  193.9 4.9 all-gather.9.cloned.1.call-done
  198.8 79.0 %all-gather.11.cloned.1.call-done = bf16[16384,256]{1,0:T(8,128)(2,1)} async-done(((bf16[512,256]{1,0:T(8,128)(2,1)}), bf16[16384,256]{1,0:T(8,128)(2,1)}) %all-gather.11.cloned.1.call-update) | async-done | bytes 8388624 | tf_op jit(solution)/shard_map/all_gather | solution.py:1221
  277.8 49.0 %shard_map.333 = (bf16[750,1024]{1,0:T(8,128)(2,1)}, f32[750,1024]{1,0:T(8,128)}, bf16[8,4,128,1024]{3,2,1,0:T(8,128)(2,1)}, bf16[8,4,512,256]{3,2,1,0:T(8,128)(2,1)}) custom-call(bf16[750,1024]{1,0:T(8,128)(2,1)} %add_convert_fusion.3.h_ref, bf16[750,1024]{1,0:T(8,128)(2,1)} %cot_ref.1, f32[750,1024]{1,0:T(8,128)} %copy-done.22, ...), custom_call_target="tpu_custom_call" | custom-call | flops 37748736000 | bytes 45842432 | tf_op jit(solution)/shard_map/pallas_call | solution.py:566
  336.7 4.5 multiply_reduce_fusion
  341.2 3.8 fusion.87
  351.7 3.9 copy.57
  361.0 10.2 %shard_map.334 = (bf16[750,1024]{1,0:T(8,128)(2,1)S(1)}, bf16[64,1024]{1,0:T(8,128)(2,1)S(1)}, bf16[64,1024]{1,0:T(8,128)(2,1)S(1)}) custom-call(bf16[750,1024]{1,0:T(8,128)(2,1)S(1)} %fusion.50.q_ref, bf16[64,1024]{1,0:T(8,128)(2,1)S(1)} %fusion.56.k_ref, bf16[64,1024]{1,0:T(8,128)(2,1)S(1)} %fusion.59.v_ref, ...), custom_call_target="tpu_custom_call" | custom-call | flops 491520000 | bytes 12288000 | tf_op jit(solution)/shard_map/pallas_call | solution.py:527
  373.5 4.5 multiply_reduce_fusion.1
  397.8 5.0 convolution_convert_fusion.4
  402.9 29.8 %shard_map.335 = (f32[750,1024]{1,0:T(8,128)S(1)}, f32[750,1024]{1,0:T(8,128)S(1)}, f32[750,1024]{1,0:T(8,128)}) custom-call(bf16[750,1024]{1,0:T(8,128)(2,1)S(1)} %copy-done.21, bf16[750,1024]{1,0:T(8,128)(2,1)S(1)} %copy-done.18, bf16[750,1024]{1,0:T(8,128)(2,1)S(1)} %copy-done.19, bf16[750,1024]{1,0:T(8,128)(2,1)S(1)} %get-tuple-element.138.do_ref, ...), custom_call_target="tpu_custom_call" | custom-call | flops 5760000000 | bytes 12288000 | tf_op jit(solution)/shard_map/pallas_call | solution.py:527
  445.6 89.3 %shard_map.338 = (f32[1,128,256]{2,1,0:T(8,128)}, f32[1,128,256]{2,1,0:T(8,128)}, f32[1,128,256]{2,1,0:T(8,128)}, f32[1,128,256]{2,1,0:T(8,128)}, f32[1,128,256]{2,1,0:T(8,128)}) custom-call(bf16[4,2,1,128,1024]{4,3,2,1,0:T(8,128)(2,1)} %bitcast.224, bf16[4,2,1,128,1024]{4,3,2,1,0:T(8,128)(2,1)} %bitcast.225, bf16[4,2,1,128,1024]{4,3,2,1,0:T(8,128)(2,1)} %bitcast.209, ...), custom_call_target="tpu_custom_call" | custom-call | flops 5242880 | bytes 20971520 | tf_op jit(solution)/shard_map/pallas_call | solution.py:950
  538.5 14.4 %shard_map.336 = (bf16[750,512]{1,0:T(8,128)(2,1)S(1)}, bf16[750,512]{1,0:T(8,128)(2,1)S(1)}, bf16[750,512]{1,0:T(8,128)(2,1)S(1)}) custom-call(bf16[750,512]{1,0:T(8,128)(2,1)S(1)} %bitcast.196, bf16[750,512]{1,0:T(8,128)(2,1)S(1)} %bitcast.197, bf16[750,512]{1,0:T(8,128)(2,1)S(1)} %bitcast.198, bf16[750,512]{1,0:T(8,128)(2,1)S(1)} %slice_select_fusion.do_ref, ...), custom_call_target="tpu_custom_call" | custom-call | flops 2880000000 | bytes 6144000 | tf_op jit(solution)/shard_map/pallas_call | solution.py:527
  560.4 12.5 %collective-permute-done.3 = bf16[750,512]{1,0:T(8,128)(2,1)S(1)} collective-permute-done((bf16[750,512]{1,0:T(8,128)(2,1)S(1)}, bf16[750,512]{1,0:T(8,128)(2,1)S(1)}, u32[]{:S(2)}, u32[]{:S(2)}) %collective-permute-start.3) | collective-permute-done | bytes 768032 | tf_op jit(solution)/shard_map/ppermute | solution.py:1205
  574.8 12.3 %collective-permute-done.4 = bf16[750,512]{1,0:T(8,128)(2,1)S(1)} collective-permute-done((bf16[750,512]{1,0:T(8,128)(2,1)S(1)}, bf16[750,512]{1,0:T(8,128)(2,1)S(1)}, u32[]{:S(2)}, u32[]{:S(2)}) %collective-permute-start.4) | collective-permute-done | bytes 768032 | tf_op jit(solution)/shard_map/ppermute | solution.py:1208
  589.0 13.1 %collective-permute-done.5 = bf16[750,512]{1,0:T(8,128)(2,1)S(1)} collective-permute-done((bf16[750,512]{1,0:T(8,128)(2,1)S(1)}, bf16[750,512]{1,0:T(8,128)(2,1)S(1)}, u32[]{:S(2)}, u32[]{:S(2)}) %collective-permute-start.5) | collective-permute-done | bytes 768032 | tf_op jit(solution)/shard_map/ppermute | solution.py:1208
  602.1 4.2 fusion.85
  610.5 6.3 convolution_convert_fusion.7
  623.7 49.2 %shard_map.337 = (f32[1,128,256]{2,1,0:T(8,128)}, f32[1,128,256]{2,1,0:T(8,128)}, f32[1,128,256]{2,1,0:T(8,128)}, f32[1,16,128]{2,1,0:T(8,128)}) custom-call(bf16[4,2,1,128,1024]{4,3,2,1,0:T(8,128)(2,1)} %bitcast.227, bf16[4,2,1,128,1024]{4,3,2,1,0:T(8,128)(2,1)} %bitcast.229, bf16[4,2,1,128,1024]{4,3,2,1,0:T(8,128)(2,1)} %bitcast.228, ...), custom_call_target="tpu_custom_call" | custom-call | flops 3211264 | bytes 12845056 | tf_op jit(solution)/shard_map/pallas_call | solution.py:950
  674.4 4.6 add_add_fusion.3
  (349 shorter events, 128.4 us)
Async XLA Ops:
  7.2 71.4 %copy-start.23 = (bf16[750,1024]{1,0:T(8,128)(2,1)S(1)}, bf16[750,1024]{1,0:T(8,128)(2,1)}, u32[]{:S(2)}) copy-start(bf16[750,1024]{1,0:T(8,128)(2,1)} %param.21) | copy-start | bytes 4608004
  7.2 141.9 %all-gather.7.cloned.1.call-start = ((), (), s32[]{:S(2)}) async-start(), calls=%async_computation.4 | async-start | bytes 10813440 | tf_op jit(solution)/shard_map/all_gather | solution.py:1232
  12.3 186.5 %all-gather.9.cloned.1.call-start = ((), (), s32[]{:S(2)}) async-start(), calls=%async_computation.5 | async-start | bytes 8650752 | tf_op jit(solution)/shard_map/all_gather | solution.py:1220
  13.1 264.7 %all-gather.11.cloned.1.call-start = ((), (), s32[]{:S(2)}) async-start(), calls=%async_computation.6 | async-start | bytes 8650752 | tf_op jit(solution)/shard_map/all_gather | solution.py:1221
  13.8 665.2 %reduce-scatter.5.cloned.1.call-start = ((), (), s32[]{:S(2)}) async-start(), calls=%async_computation.3 | async-start | bytes 8650752 | tf_op jit(solution)/shard_map/reduce_scatter | solution.py:1261
  13.9 159.5 %collective-permute-start = (bf16[32,1024]{1,0:T(8,128)(2,1)}, bf16[32,1024]{1,0:T(8,128)(2,1)S(1)}, u32[]{:S(2)}, u32[]{:S(2)}) collective-permute-start(bf16[32,1024]{1,0:T(8,128)(2,1)} %param.22), channel_id=1, source_target_pairs={{0,4},{8,12},{16,20},{24,28},{4,0},{12,8},{20,16},{28,24},{1,5},{9... | collective-permute-start | bytes 196616 | tf_op jit(solution)/shard_map/ppermute | solution.py:1249
  78.4 96.9 %copy-start.81 = (f32[1024]{0:T(1024)}, f32[1024]{0:T(1024)S(1)}, u32[]{:S(2)}) copy-start(f32[1024]{0:T(1024)S(1)} %mul.195) | copy-start | bytes 12292
  78.5 96.8 %copy-start.90 = (f32[1024]{0:T(1024)}, f32[1024]{0:T(1024)S(1)}, u32[]{:S(2)}) copy-start(f32[1024]{0:T(1024)S(1)} %add.119) | copy-start | bytes 12292
  149.1 21.8 %copy-start = (bf16[750,1024]{1,0:T(8,128)(2,1)}, bf16[750,1024]{1,0:T(8,128)(2,1)S(1)}, u32[]{:S(2)}) copy-start(bf16[750,1024]{1,0:T(8,128)(2,1)S(1)} %get-tuple-element.68) | copy-start | bytes 4608004
  191.0 135.8 %copy-start.79 = (f32[750]{0:T(1024)}, f32[750]{0:T(1024)S(1)}, u32[]{:S(2)}) copy-start(f32[750]{0:T(1024)S(1)} %multiply_reduce_fusion.4) | copy-start | bytes 9004
  326.8 354.0 %reduce-scatter.3.cloned.1.call-start = ((), (), s32[]{:S(2)}) async-start(), calls=%async_computation.2 | async-start | bytes 8650752 | tf_op jit(solution)/shard_map/reduce_scatter | solution.py:1261
  372.0 68.4 %collective-permute-start.6 = (bf16[32,2048]{1,0:T(8,128)(2,1)}, bf16[32,2048]{1,0:T(8,128)(2,1)}, u32[]{:S(2)}, u32[]{:S(2)}) collective-permute-start(bf16[32,2048]{1,0:T(8,128)(2,1)} %broadcast_select_fusion.3), channel_id=1, source_target_pairs={{0,4},{8,12},{16,20},{24,28},{4,0},{12,8},{20,16},{28,24},{1,5},{9... | collective-permute-start | bytes 393224 | tf_op jit(solution)/shard_map/ppermute | solution.py:1282
  394.0 46.4 %collective-permute-start.2 = (f32[4,4,750]{2,1,0:T(4,128)S(1)}, f32[4,4,750]{2,1,0:T(4,128)S(1)}, u32[]{:S(2)}, u32[]{:S(2)}) collective-permute-start(f32[4,4,750]{2,1,0:T(4,128)S(1)} %slice.123), channel_id=1, source_target_pairs={{4,0},{12,8},{20,16},{28,24},{5,1},{13,9},{21,17},{29,25},{6,2},{1... | collective-permute-start | bytes 144008 | tf_op jit(solution)/shard_map/ppermute | solution.py:1208
  396.2 141.0 %collective-permute-start.1 = (bf16[750,512]{1,0:T(8,128)(2,1)}, bf16[750,512]{1,0:T(8,128)(2,1)}, u32[]{:S(2)}, u32[]{:S(2)}) collective-permute-start(bf16[750,512]{1,0:T(8,128)(2,1)} %slice.137), channel_id=1, source_target_pairs={{4,0},{12,8},{20,16},{28,24},{5,1},{13,9},{21,17},{29,25},{6,2},{1... | collective-permute-start | bytes 2304008 | tf_op jit(solution)/shard_map/ppermute | solution.py:1208
  402.8 29.8 %copy-start.13 = (bf16[750,1024]{1,0:T(8,128)(2,1)S(1)}, bf16[750,1024]{1,0:T(8,128)(2,1)}, u32[]{:S(2)}) copy-start(bf16[750,1024]{1,0:T(8,128)(2,1)} %copy-done.12) | copy-start | bytes 4608004
  402.8 29.8 %copy-start.33 = (f32[750,1024]{1,0:T(8,128)S(1)}, f32[750,1024]{1,0:T(8,128)}, u32[]{:S(2)}) copy-start(f32[750,1024]{1,0:T(8,128)} %copy-done.31) | copy-start | bytes 9216004
  402.8 29.8 %copy-start.85 = (f32[750]{0:T(1024)S(1)}, f32[750]{0:T(1024)}, u32[]{:S(2)}) copy-start(f32[750]{0:T(1024)} %copy-done.83) | copy-start | bytes 9004
  402.9 29.8 %copy-start.91 = (f32[1024]{0:T(1024)S(1)}, f32[1024]{0:T(1024)}, u32[]{:S(2)}) copy-start(f32[1024]{0:T(1024)} %copy-done.90) | copy-start | bytes 12292
  552.9 20.0 %collective-permute-start.3 = (bf16[750,512]{1,0:T(8,128)(2,1)S(1)}, bf16[750,512]{1,0:T(8,128)(2,1)S(1)}, u32[]{:S(2)}, u32[]{:S(2)}) collective-permute-start(bf16[750,512]{1,0:T(8,128)(2,1)S(1)} %get-tuple-element.79), channel_id=1, source_target_pairs={{0,4},{8,12},{16,20},{24,28},{1,5},{9,13},{17,21},{25,29},{2,6},{1... | collective-permute-start | bytes 2304008 | tf_op jit(solution)/shard_map/ppermute | solution.py:1205
  557.6 29.4 %collective-permute-start.4 = (bf16[750,512]{1,0:T(8,128)(2,1)S(1)}, bf16[750,512]{1,0:T(8,128)(2,1)S(1)}, u32[]{:S(2)}, u32[]{:S(2)}) collective-permute-start(bf16[750,512]{1,0:T(8,128)(2,1)S(1)} %get-tuple-element.81), channel_id=1, source_target_pairs={{4,0},{12,8},{20,16},{28,24},{5,1},{13,9},{21,17},{29,25},{6,2},{1... | collective-permute-start | bytes 2304008 | tf_op jit(solution)/shard_map/ppermute | solution.py:1208
  558.9 43.1 %collective-permute-start.5 = (bf16[750,512]{1,0:T(8,128)(2,1)S(1)}, bf16[750,512]{1,0:T(8,128)(2,1)S(1)}, u32[]{:S(2)}, u32[]{:S(2)}) collective-permute-start(bf16[750,512]{1,0:T(8,128)(2,1)S(1)} %get-tuple-element.83), channel_id=1, source_target_pairs={{4,0},{12,8},{20,16},{28,24},{5,1},{13,9},{21,17},{29,25},{6,2},{1... | collective-permute-start | bytes 2304008 | tf_op jit(solution)/shard_map/ppermute | solution.py:1208
  560.3 26.7 %copy-start.54 = (bf16[750,512]{1,0:T(8,128)(2,1)}, bf16[750,512]{1,0:T(8,128)(2,1)S(1)}, u32[]{:S(2)}) copy-start(bf16[750,512]{1,0:T(8,128)(2,1)S(1)} %get-tuple-element.141) | copy-start | bytes 2304004
  560.4 41.7 %copy-start.41 = (bf16[750,512]{1,0:T(8,128)(2,1)}, bf16[750,512]{1,0:T(8,128)(2,1)S(1)}, u32[]{:S(2)}) copy-start(bf16[750,512]{1,0:T(8,128)(2,1)S(1)} %get-tuple-element.140) | copy-start | bytes 2304004
  623.7 50.7 %copy-start.27 = (bf16[750,1024]{1,0:T(8,128)(2,1)S(1)}, bf16[750,1024]{1,0:T(8,128)(2,1)}, u32[]{:S(2)}) copy-start(bf16[750,1024]{1,0:T(8,128)(2,1)} %param.21) | copy-start | bytes 4608004
  (89 other events, 558.0 us)
Sparse Core Ops, SparseCore 0:
  12.4 104.5 all-gather.6
  119.9 78.8 all-gather.8
  201.7 76.0 all-gather.10
  327.0 150.2 reduce-scatter.4
  479.4 150.2 reduce-scatter.2

commit v5 on v4

--- a/solution.py
+++ b/solution.py
@@ -549,7 +549,7 @@
         columns=slice(at*wide,(at+1)*wide)
         cot=cot_ref[:,columns]
         acc[:,columns]+=dg(inner,down_ref[0,at],NN)
-        ddown_ref[0,at]=dg(inner,cot,TN).astype(ddown_ref.dtype)
+        ddown_ref[:,columns]=dg(inner,cot,TN).astype(ddown_ref.dtype)
         part=dg(cot,down_ref[0,at],NT)
         grad=part if grad is None else grad+part
     gpre=(grad*slope).astype(jnp.bfloat16)
@@ -565,8 +565,8 @@
     down_spec=pl.BlockSpec((1,)+down.shape[1:],lambda i:(i,0,0,0))
     return pl.pallas_call(feed_kernel,grid=(ff//chunk,),
         in_specs=[whole,whole,whole,up_spec,down_spec],
-        out_specs=[whole,whole,up_spec,down_spec],
-        out_shape=[jax.ShapeDtypeStruct((rows,d),jnp.bfloat16),jax.ShapeDtypeStruct((rows,d),jnp.float32),jax.ShapeDtypeStruct(up.shape,jnp.bfloat16),jax.ShapeDtypeStruct(down.shape,jnp.bfloat16)],
+        out_specs=[whole,whole,up_spec,pl.BlockSpec((chunk,d),lambda i:(i,0))],
+        out_shape=[jax.ShapeDtypeStruct((rows,d),jnp.bfloat16),jax.ShapeDtypeStruct((rows,d),jnp.float32),jax.ShapeDtypeStruct(up.shape,jnp.bfloat16),jax.ShapeDtypeStruct((ff,d),jnp.bfloat16)],
         scratch_shapes=[pltpu.VMEM((rows,d),jnp.float32)],
         compiler_params=pltpu.CompilerParams(vmem_limit_bytes=56<<20),
         cost_estimate=pl.CostEstimate(flops=12*rows*d*ff,bytes_accessed=8*d*ff+16*rows*d,transcendentals=2*rows*ff))(h,cot,res,up,down)
@@ -756,19 +756,19 @@
         gather.finish()
 
 
-def gather_units(blocks, least):
+def gather_units(blocks, least, orders):
     strips = []
     for which, block in enumerate(blocks):
         wide = min(least, block.shape[-1])
         for part in range(block.shape[0]):
             for start in range(0, block.shape[-1], wide):
                 strips.append((which, (part, start, wide)))
-    return [strip + (ORDERS[at % len(ORDERS)],) for at, strip in enumerate(strips)]
+    return [strip + (orders[at % len(orders)],) for at, strip in enumerate(strips)]
 
 
 def gather_blocks(blocks, collective_id, least):
     along, cols = lax.axis_size("row") // 2, lax.axis_size("col")
-    units = gather_units(blocks, least)
+    units = gather_units(blocks, least, ORDERS)
     count = len(blocks)
     anywhere = pl.BlockSpec(memory_space=pl.ANY)
     moved = sum(block.size for block in blocks) * 2 * along * 2 * cols
@@ -821,42 +821,44 @@
         column = (x * 2 + k) * self.width + start
         return self.grad.at[:, :, part, :, pl.ds(pl.multiple_of(column, 128), count)]
 
-    def copy(self, device, source, target, semaphore=None):
-        if semaphore is None:
-            semaphore = self.used
-            self.used += 1
+    def copy(self, device, source, target, semaphore):
         return pltpu.make_async_remote_copy(
             src_ref=source, dst_ref=target, send_sem=self.send.at[semaphore], recv_sem=self.recv.at[semaphore],
             device_id=device, device_id_type=MESH)
 
-    def start(self, copy, condition=None):
-        when(condition, lambda: copy.start())
-        self.started.append((condition, copy))
+    def reserve(self, count):
+        self.used += count
+        return self.used - count
+
+    def start(self, make, condition=lambda: None):
+        when(condition(), lambda: make().start())
+        self.started.append((condition, make))
 
     def stages(self):
         place, along = self.place, self.place.along
         rows, columns = self.total.shape[-2:]
-        own = [
-            pltpu.make_async_copy(self.region(x, place.k), self.total.at[:, :, x], self.local.at[x]) for x in range(2)
-        ]
-        swapped = [
-            self.copy(place.across("k"), self.region(x, 1 - place.k), self.other_core.at[:, :, x]) for x in range(2)
-        ]
-        for copy in own:
-            copy.start()
-        for copy in swapped:
-            self.start(copy)
+        core = self.reserve(2)
+
+        def own(x):
+            return pltpu.make_async_copy(self.region(x, place.k), self.total.at[:, :, x], self.local.at[x])
+
+        def swapped(x):
+            return self.copy(
+                place.across("k"), self.region(x, 1 - place.k), self.other_core.at[:, :, x], core + x)
+
+        for x in range(2):
+            own(x).start()
+            self.start(functools.partial(swapped, x))
         yield
-        for copy in own:
-            copy.wait()
-        for copy in swapped:
-            copy.wait_recv()
+        for x in range(2):
+            own(x).wait()
+            swapped(x).wait_recv()
         add_blocks(self.total, self.other_core, (along, 2, 2))
         left = {"z": slice(None), "y": slice(None), "x": slice(None)}
         at = {"y": place.y, "x": place.x}
 
-        def view(ref, **places):
-            return ref.at[tuple({**left, **places}[axis] for axis in "zyx")]
+        def view(ref, kept=None, **places):
+            return ref.at[tuple({**(left if kept is None else kept), **places}[axis] for axis in "zyx")]
 
         def sizes():
             return tuple(size for axis, size in zip("zyx", (along, 2, 2)) if isinstance(left[axis], slice))
@@ -865,9 +867,13 @@
         for axis in self.order:
             if axis == "z":
                 shape = tuple(2 for name in "yx" if isinstance(left[name], slice))
-                landing = self.steps.at[(slice(None),) * 2 + tuple(slice(None) if isinstance(left[name], slice) else 0 for name in "yx")]
-                right, leftward = [self.used + at for at in range(along)], [self.used + along + at for at in range(along)]
-                self.used += 2 * along
+                inner = tuple(slice(None) if isinstance(left[name], slice) else 0 for name in "yx")
+
+                def landing(side, step, inner=inner):
+                    return self.steps.at[(side, step) + inner]
+
+                base = self.reserve(2 * along)
+                right, leftward = range(base, base + along), range(base + along, base + 2 * along)
                 for step in range(along):
                     if step:
                         yield
@@ -875,35 +881,48 @@
                         goal = along - 1 - step + place.z if way == 1 else step - along + 1 + place.z
                         side = 0 if way == 1 else 1
                         if step:
-                            arrived = self.copy(
-                                place.across("k"), landing.at[side, step - 1], landing.at[side, step - 1], names[step - 1])
-
-                            def take(arrived=arrived, goal=goal, side=side, step=step):
-                                arrived.wait_recv()
-                                add_blocks(view(self.total, z=goal), landing.at[side, step - 1], shape)
+                            arrived = landing(side, step - 1)
+
+                            def take(arrived=arrived, goal=goal, side=side, step=step, names=names):
+                                self.copy(place.across("k"), arrived, arrived, names[step - 1]).wait_recv()
+                                add_blocks(view(self.total, z=goal), arrived, shape)
 
                             pl.when((first >= 1) & (first <= step))(take)
                         if step < along - 1:
-                            onward = self.copy(
-                                place.device(dz=way), view(self.total, z=jnp.clip(goal, 0, along - 1)), landing.at[side, step], names[step])
-                            self.start(onward, (first <= step) & (first < along - 1))
+                            kept = dict(left)
+
+                            def onward(way=way, step=step, kept=kept, landing=landing, side=side, names=names):
+                                goal = along - 1 - step + place.z if way == 1 else step - along + 1 + place.z
+                                source = view(self.total, kept, z=jnp.clip(goal, 0, along - 1))
+                                return self.copy(place.device(dz=way), source, landing(side, step), names[step])
+
+                            def reached(way=way, step=step):
+                                first = place.z if way == 1 else along - 1 - place.z
+                                return (first <= step) & (first < along - 1)
+
+                            self.start(onward, reached)
                 left["z"] = place.z
             else:
                 landing = self.halves[exchanges]
                 exchanges += 1
-                target = landing.at[tuple(slice(None) if isinstance(left[name], slice) and name != axis else 0 for name in "zyx")]
-                swap = self.copy(place.across(axis), view(self.total, **{axis: 1 - at[axis]}), target)
+                inner = tuple(slice(None) if isinstance(left[name], slice) and name != axis else 0 for name in "zyx")
+                semaphore, kept = self.reserve(1), dict(left)
+
+                def swap(axis=axis, kept=kept, landing=landing, inner=inner, semaphore=semaphore):
+                    source = view(self.total, kept, **{axis: 1 - at[axis]})
+                    return self.copy(place.across(axis), source, landing.at[inner], semaphore)
+
                 self.start(swap)
                 yield
-                swap.wait_recv()
+                swap().wait_recv()
                 left[axis] = at[axis]
-                add_blocks(view(self.total), target, sizes())
+                add_blocks(view(self.total), landing.at[inner], sizes())
         part, start, count = self.strip
         self.out[part, :, start : start + count] = view(self.total)[...].astype(jnp.float32)
 
     def finish(self):
-        for condition, copy in self.started:
-            when(condition, lambda copy=copy: copy.wait_send())
+        for condition, make in self.started:
+            when(condition(), lambda make=make: make().wait_send())
 
 
 def scatter_slots(along, rows, columns, order):
@@ -920,44 +939,48 @@
     return shapes + [steps]
 
 
-def scatter_kernel(units, count, *refs):
-    grads, outs = refs[:count], refs[count : 2 * count]
-    send, recv, local = refs[2 * count : 2 * count + 3]
-    slots = refs[2 * count + 3 :]
-    place = Place()
-    place.greet()
+def scatters_of(place, units, grads, outs, send, recv, local, slots):
     scatters = []
     for at, (which, strip, order) in enumerate(units):
         total, other_core, first, second, steps = slots[5 * at : 5 * at + 5]
         scatters.append(
             Scatter(place, grads[which], outs[which], strip, outs[which].shape[-1], order,
                     (total, other_core, (first, second), steps), send.at[at], recv.at[at], local.at[at]))
+    return scatters
+
+
+def scatter_kernel(units, count, *refs):
+    grads, outs = refs[:count], refs[count : 2 * count]
+    place = Place()
+    place.greet()
+    scatters = scatters_of(place, units, grads, outs, *refs[2 * count : 2 * count + 3], refs[2 * count + 3 :])
     for unused in in_turn([scatter.stages() for scatter in scatters], 0.5):
         pass
     for scatter in scatters:
         scatter.finish()
 
 
-def scatter_blocks(grads, collective_id, least):
+def scatter_plan(grads, least, orders):
     along, cols = lax.axis_size("row") // 2, lax.axis_size("col")
     blocks = [jax.ShapeDtypeStruct(g.shape[2:4] + (g.shape[4] // cols,), jnp.float32) for g in grads]
-    units = gather_units(blocks, least)
+    units = gather_units(blocks, least, orders)
+    scratch = [pltpu.SemaphoreType.DMA((len(units), 2 * along + 4))] * 2 + [pltpu.SemaphoreType.DMA((len(units), 2))]
+    for which, strip, order in units:
+        shapes = scatter_slots(along, blocks[which].shape[1], strip[2], order)
+        scratch += [pltpu.VMEM(shape, jnp.bfloat16) for shape in shapes]
+    return blocks, units, scratch
+
+
+def scatter_blocks(grads, collective_id, least):
+    blocks, units, scratch = scatter_plan(grads, least, ORDERS)
     count = len(grads)
-    slots = []
-    for which, strip, order in units:
-        slots += [pltpu.VMEM(shape, jnp.bfloat16) for shape in scatter_slots(along, blocks[which].shape[1], strip[2], order)]
     anywhere = pl.BlockSpec(memory_space=pl.ANY)
     return pl.pallas_call(
         functools.partial(scatter_kernel, units, count),
         out_shape=blocks,
         in_specs=[anywhere] * count,
         out_specs=[pl.BlockSpec(memory_space=pltpu.VMEM)] * count,
-        scratch_shapes=[
-            pltpu.SemaphoreType.DMA((len(units), 2 * along + 4)),
-            pltpu.SemaphoreType.DMA((len(units), 2 * along + 4)),
-            pltpu.SemaphoreType.DMA((len(units), 2)),
-            *slots,
-        ],
+        scratch_shapes=scratch,
         compiler_params=pltpu.CompilerParams(
             collective_id=collective_id, has_side_effects=True, vmem_limit_bytes=60 << 20),
         cost_estimate=pl.CostEstimate(
@@ -1186,6 +1209,261 @@
     )(q, k, v, q, k, v)
 
 
+def back_pair(tile, causal, q_ref, k_ref, v_ref, do_ref, stats, acc, put):
+    rows, keys = q_ref.shape[0], k_ref.shape[0]
+    low = lax.broadcasted_iota(jnp.int32, (1, 128), 1) < HEAD_DIM
+    acc[...] = jnp.zeros_like(acc)
+    for start in range(0, keys, tile):
+        n = min(tile, keys - start)
+        k = k_ref[start : start + n, :] * jnp.bfloat16(HEAD_DIM**-0.5)
+        v = v_ref[start : start + n, :]
+        spans = [(0, rows)]
+        if causal:
+            spans = [(start, n)] + ([(start + n, rows - start - n)] if start + n < rows else [])
+        dks, dvs = [], []
+        for h in range(2):
+            mine = low if h == 0 else jnp.logical_not(low)
+            kh, vh = jnp.where(mine, k, jnp.bfloat16(0)), jnp.where(mine, v, jnp.bfloat16(0))
+            dk = dv = None
+            for at, length in spans:
+                qs, do = q_ref[at : at + length, :], do_ref[at : at + length, :]
+                p = jnp.exp(dg(kh, qs, NT) - stats[h : h + 1, at : at + length])
+                if causal and at == start:
+                    allowed = lax.broadcasted_iota(jnp.int32, p.shape, 0) <= lax.broadcasted_iota(jnp.int32, p.shape, 1)
+                    p = jnp.where(allowed, p, 0.0)
+                ds = (p * (dg(vh, do, NT) - stats[2 + h : 3 + h, at : at + length])).astype(jnp.bfloat16)
+                a, b = dg(p.astype(jnp.bfloat16), do, NN), dg(ds, qs, NN)
+                dv = a if dv is None else dv + a
+                dk = b if dk is None else dk + b
+                acc[at : at + length, :] += dg(ds, kh, TN)
+            dks.append(dk)
+            dvs.append(dv)
+        put(start, n, jnp.where(low, dks[0], dks[1]) * HEAD_DIM**-0.5, jnp.where(low, dvs[0], dvs[1]))
+
+
+def pair_back_kernel(tile, far_tile, units, count, events, *refs):
+    q_ref, k_ref, v_ref, do_ref, mix_ref, logs_ref, do_any, fq_any, fk_any, fv_any = refs[:10]
+    grads, (dq_ref, dk_ref, dv_ref) = refs[10 : 10 + count], refs[10 + count : 13 + count]
+    sums = refs[13 + count : 13 + 2 * count]
+    (near, acc, stats, far_stats, used_stats, far_q, far_k, far_v, far_do, far_dq, far_dk, far_dv, got_q, got_k, got_v,
+     send, recv, local, do_local) = refs[13 + 2 * count : 32 + 2 * count]
+    scatter_refs = refs[32 + 2 * count :]
+    step = pl.program_id(0)
+    place = Place()
+    pairs = near.shape[1]
+    fars = pairs // 2
+    first, second = place.y == 0, place.y == 1
+    partner = place.across("y")
+    lane = lax.broadcasted_iota(jnp.int32, (8, 128), 1)
+    line = lax.broadcasted_iota(jnp.int32, (8, 128), 0)
+
+    def columns(pair):
+        return pl.ds(pl.multiple_of(pair * 128, 128), 128)
+
+    def remote(source, target, which, j):
+        return pltpu.make_async_remote_copy(
+            src_ref=source, dst_ref=target, send_sem=send.at[which, j], recv_sem=recv.at[which, j],
+            device_id=partner, device_id_type=MESH)
+
+    def grad_over(j):
+        return remote(do_any.at[:, columns(fars + j)], far_do.at[j], 0, j)
+
+    def grad_kept(j):
+        return pltpu.make_async_copy(do_any.at[:, columns(j)], far_do.at[j], do_local.at[j])
+
+    def stats_over():
+        return remote(stats.at[pl.ds(fars, fars)], far_stats, 4, 0)
+
+    def back_over(which, j):
+        source, target = ((far_dq, got_q), (far_dk, got_k), (far_dv, got_v))[which]
+        return remote(source.at[j], target.at[j], 1 + which, j)
+
+    def far_in(which):
+        source, target = ((fq_any, far_q), (fk_any, far_k), (fv_any, far_v))[which]
+        return pltpu.make_async_copy(source, target, local.at[which])
+
+    scatters = scatters_of(place, units, grads, sums, *scatter_refs[:3], scatter_refs[3:])
+    turns = in_turn([scatter.stages() for scatter in scatters], 0.5)
+
+    @pl.when(step == 0)
+    def _():
+        place.greet()
+        for which in range(3):
+            far_in(which).start()
+        for j in range(fars):
+
+            @pl.when(second)
+            def _(j=j):
+                grad_over(j).start()
+
+            @pl.when(second)
+            def _(j=j):
+                grad_kept(j).start()
+
+    for at, number in enumerate(events):
+
+        @pl.when(step == at)
+        def _(number=number):
+            for unused in range(number):
+                next(turns, None)
+
+    @pl.when((step == fars) & second)
+    def _():
+        stats_over().start()
+
+    @pl.when(step < pairs)
+    def _():
+        pair = lax.rem(step + fars, pairs)
+        picked = ((line < 2) & (line + 2 * pair == lane)).astype(jnp.float32)
+        halves = (((line == 2) & (lane < HEAD_DIM)) | ((line == 3) & (lane >= HEAD_DIM))).astype(jnp.float32)
+        products = mix_ref[...].astype(jnp.float32) * do_ref[...].astype(jnp.float32)
+        both = lax.dot_general(
+            picked, logs_ref[...], NT, precision=lax.Precision.HIGHEST, preferred_element_type=jnp.float32)
+        both += lax.dot_general(
+            halves, products, NT, precision=lax.Precision.HIGHEST, preferred_element_type=jnp.float32)
+        stats[pair] = both
+
+        def put(start, n, dk, dv):
+            near[1, pair, start : start + n, :] = dk
+            near[2, pair, start : start + n, :] = dv
+
+        back_pair(tile, True, q_ref, k_ref, v_ref, do_ref, stats.at[pair], acc, put)
+        near[0, pair] = acc[...]
+
+    @pl.when((step >= pairs) & (step < pairs + fars))
+    def _():
+        j = step - pairs
+
+        @pl.when(j == 0)
+        def _():
+            for which in range(3):
+                far_in(which).wait()
+
+            @pl.when(first)
+            def _():
+                stats_over().wait_recv()
+
+        @pl.when(first)
+        def _():
+            grad_over(j).wait_recv()
+            used_stats[...] = far_stats[j]
+
+        @pl.when(second)
+        def _():
+            grad_kept(j).wait()
+            used_stats[...] = stats[j]
+
+        def put(start, n, dk, dv):
+            far_dk[j, start : start + n, :] = dk.astype(far_dk.dtype)
+            far_dv[j, start : start + n, :] = dv.astype(far_dv.dtype)
+
+        back_pair(far_tile, False, far_q.at[j], far_k.at[j], far_v.at[j], far_do.at[j], used_stats, acc, put)
+        far_dq[j] = acc[...].astype(far_dq.dtype)
+
+        @pl.when(first)
+        def _():
+            back_over(0, j).start()
+
+        @pl.when(second)
+        def _():
+            back_over(1, j).start()
+            back_over(2, j).start()
+
+    @pl.when(step >= pairs + fars)
+    def _():
+        pair = step - pairs - fars
+        lower = pair < fars
+        j = lax.rem(pair, fars)
+
+        def write(ref, which, other):
+            total = near[which, pair]
+            if other is not None:
+                total = total + other[j].astype(jnp.float32)
+            ref[...] = total.astype(ref.dtype)
+
+        @pl.when(first & lower)
+        def _():
+            for which in (1, 2):
+                back_over(which, j).wait_recv()
+            write(dq_ref, 0, None)
+            write(dk_ref, 1, got_k)
+            write(dv_ref, 2, got_v)
+
+        @pl.when(first & jnp.logical_not(lower))
+        def _():
+            write(dq_ref, 0, None)
+            write(dk_ref, 1, far_dk)
+            write(dv_ref, 2, far_dv)
+
+        @pl.when(second & lower)
+        def _():
+            write(dq_ref, 0, far_dq)
+            write(dk_ref, 1, None)
+            write(dv_ref, 2, None)
+
+        @pl.when(second & jnp.logical_not(lower))
+        def _():
+            back_over(0, j).wait_recv()
+            write(dq_ref, 0, got_q)
+            write(dk_ref, 1, None)
+            write(dv_ref, 2, None)
+
+    @pl.when(step == 2 * pairs + fars - 1)
+    def _():
+        for unused in turns:
+            pass
+        for scatter in scatters:
+            scatter.finish()
+
+        @pl.when(first)
+        def _():
+            for j in range(fars):
+                back_over(0, j).wait_send()
+
+        @pl.when(second)
+        def _():
+            stats_over().wait_send()
+            for j in range(fars):
+                grad_over(j).wait_send()
+                for which in (1, 2):
+                    back_over(which, j).wait_send()
+
+
+BACK_ORDERS = ("yzx", "yzx", "xzy", "yzx", "yzx", "zyx", "yzx", "yxz", "yzx")
+
+
+def pair_back(q, k, v, do, mix, logs, far, grads, collective_id, events, tile=384, far_tile=256):
+    rows, width = q.shape
+    pairs = width // 128
+    fars = pairs // 2
+    blocks, units, scratch = scatter_plan(grads, 256, BACK_ORDERS)
+    count = len(grads)
+    block = pl.BlockSpec((rows, 128), lambda i: (0, lax.rem(jnp.minimum(i, pairs - 1) + fars, pairs)))
+    joined = pl.BlockSpec((rows, 128), lambda i: (0, jnp.maximum(i - pairs - fars, 0)))
+    anywhere = pl.BlockSpec(memory_space=pl.ANY)
+    half = pltpu.VMEM((fars, rows, 128), jnp.bfloat16)
+    out = jax.ShapeDtypeStruct((rows, width), jnp.bfloat16)
+    result = pl.pallas_call(
+        functools.partial(pair_back_kernel, tile, far_tile, units, count, events),
+        grid=(2 * pairs + fars,),
+        in_specs=[block] * 5 + [pl.BlockSpec((rows, 128), lambda i: (0, 0))] + [anywhere] * (4 + count),
+        out_specs=[joined] * 3 + [pl.BlockSpec(memory_space=pltpu.VMEM)] * count,
+        out_shape=[out] * 3 + blocks,
+        scratch_shapes=[
+            pltpu.VMEM((3, pairs, rows, 128), jnp.float32), pltpu.VMEM((rows, 128), jnp.float32),
+            pltpu.VMEM((pairs, 8, rows), jnp.float32), pltpu.VMEM((fars, 8, rows), jnp.float32),
+            pltpu.VMEM((8, rows), jnp.float32), *[half] * 10,
+            pltpu.SemaphoreType.DMA((5, fars)), pltpu.SemaphoreType.DMA((5, fars)),
+            pltpu.SemaphoreType.DMA((3,)), pltpu.SemaphoreType.DMA((fars,)), *scratch,
+        ],
+        compiler_params=pltpu.CompilerParams(
+            collective_id=collective_id, has_side_effects=True, vmem_limit_bytes=62 << 20),
+        cost_estimate=pl.CostEstimate(
+            flops=10 * rows * rows * width, bytes_accessed=16 * rows * width, transcendentals=rows * rows * pairs * 2),
+    )(q, k, v, do, mix, logs, do, *far, *grads)
+    return result[:3], result[3:]
+
+
 def fast(
     frames_in, text_states, self_query, self_key, self_value, self_output, cross_query, cross_key, cross_value, cross_output,
     up_weight, down_weight, first_gain, first_bias, second_gain, second_bias, third_gain, third_bias, cotangent,
@@ -1241,8 +1519,6 @@
     self_q = matmul(hidden_one, query_self).astype(jnp.bfloat16)
     self_mix, log_lanes, far_q, far_k, far_v = pair_attend(self_q, self_k, self_v, 5)
     half_heads = half // HEAD_DIM
-    self_logs = log_lanes[:, : 2 * half_heads]
-    far_q, far_k, far_v = [a.transpose(1, 0, 2).reshape(rows, half) for a in (far_q, far_k, far_v)]
     resid_one = frames + matmul(self_mix, out_self)
     hidden_two = norm_forward(resid_one, norm_params[2], norm_params[3]).astype(jnp.bfloat16)
     cross_q = matmul(hidden_two, query_cross).astype(jnp.bfloat16)
@@ -1257,10 +1533,7 @@
     resid_two = resid_one + matmul(cross_mix, out_cross)
     hidden_three = norm_forward(resid_two, norm_params[4], norm_params[5]).astype(jnp.bfloat16)
     layer_out, grad_three, up_grad, down_grad = feed(hidden_three, cotangent, resid_two, up_blocks, down_blocks)
-    up_sum, down_sum = [
-        lax.psum_scatter(g.reshape(-1, *g.shape[2:]), everyone, scatter_dimension=0).astype(jnp.float32)
-        for g in (up_grad, down_grad)
-    ]
+    up_sum = lax.psum_scatter(up_grad.reshape(-1, *up_weight.shape), everyone, scatter_dimension=0).astype(jnp.float32)
 
     def stats_of(logs, mix, grad):
         products = mix.astype(jnp.float32) * grad.astype(jnp.float32)
@@ -1294,22 +1567,14 @@
     grad_self = grad_resid_one.astype(jnp.bfloat16)
     self_out_grad = over_tokens(self_mix, grad_self)
     grad_self_mix = by_transposed(grad_self, out_self).astype(jnp.bfloat16)
-    stats = stats_of(self_logs, self_mix, grad_self_mix)
-    far_pairs = half // 128
-    sent_grad, sent_stats = home(grad_self_mix[:, half:]), home(stats[far_pairs:])
-    near_dq, near_dk, near_dv = attend_back(self_q, self_k, self_v, grad_self_mix, stats, True, jnp.float32)
-    far_grad = by_side(sent_grad, grad_self_mix[:, :half])
-    far_stats = by_side(sent_stats, stats[:far_pairs])
-    far_dq, far_dk, far_dv = attend_back(far_q, far_k, far_v, far_grad, far_stats, False, jnp.bfloat16)
-    got_dq, got_dk, got_dv = forth(far_dq), home(far_dk), home(far_dv)
-
-    def with_far(near, lower, upper):
-        return (near + jnp.concatenate([lower, upper], axis=1).astype(jnp.float32)).astype(jnp.bfloat16)
-
-    none = jnp.zeros_like(far_dq)
-    grad_self_q = with_far(near_dq, by_side(none, far_dq), got_dq)
-    grad_self_k = with_far(near_dk, got_dk, by_side(far_dk, none))
-    grad_self_v = with_far(near_dv, got_dv, by_side(far_dv, none))
+
+    def by_place(grad, parts):
+        return grad.astype(jnp.bfloat16).reshape(pairs, 2, parts, -1, grad.shape[-1])
+
+    (grad_self_q, grad_self_k, grad_self_v), early_sums = pair_back(
+        self_q, self_k, self_v, grad_self_mix, self_mix, log_lanes, (far_q, far_k, far_v),
+        [by_place(g, 1) for g in (self_out_grad, cross_query_part, cross_key_part, cross_value_part, cross_out_grad)]
+        + [by_place(down_grad, down_weight.shape[0] // block_rows)], 4, [4] * 12)
     self_query_part = over_tokens(hidden_one, grad_self_q)
     self_key_part = over_tokens(hidden_one, grad_self_k)
     self_value_part = over_tokens(hidden_one, grad_self_v)
@@ -1327,18 +1592,13 @@
     norm_grads = norm_grads.reshape(6, 2 * pairs, -1, piece).transpose(1, 0, 2, 3)
     norm_grads = jnp.pad(norm_grads, ((0, 0), (0, 10), (0, 0), (0, 128 - piece)))
 
-    def by_place(grad, parts):
-        return grad.astype(jnp.bfloat16).reshape(pairs, 2, parts, -1, grad.shape[-1])
-
-    early_sums = scatter_blocks(
-        [by_place(g, 1) for g in (self_out_grad, cross_query_part, cross_key_part, cross_value_part, cross_out_grad)], 4, 128)
     late_sums = scatter_blocks(
         [by_place(g, 1) for g in (self_query_part, self_key_part, self_value_part)]
         + [by_place(norm_grads.reshape(2 * pairs * 16, -1), 1)], 3, 128)
     norm_parts = late_sums[3][0, :6, :piece]
-    sums = late_sums[:3] + early_sums
+    sums = [*late_sums[:3], *early_sums]
     sums = [total.reshape(-1, total.shape[-1]) for total in sums]
-    return (layer_out, input_grad, text_grad, *sums, up_sum, down_sum, *norm_parts)
+    return (layer_out, input_grad, text_grad, *sums[:-1], up_sum, sums[-1], *norm_parts)
 
 
 def local(*arrays):

time: 702 us -> 675 us (0.962)
  Pallas kernels: 370 us -> 422 us
  waiting for transfers between devices: 123 us -> 83.1 us
  local copies, waits for them, and re-layouts: 71.9 us -> 55.3 us
  other arithmetic: 33.6 us -> 22.4 us
  starting transfers between devices: 13.8 us -> 4.71 us
    pallas_call x0 -> x1, Pallas kernels: none -> 186 us  [pair_back(): pl.pallas_call(functools.partial(pair_back_kernel, tile, far_tile, units,...]
    pallas_call x2 -> x1, Pallas kernels: 139 us -> 47.8 us  [scatter_blocks(): pl.pallas_call(functools.partial(scatter_kernel, units, count), out_shape...]
    pallas_call x3 -> x1, Pallas kernels: 54.4 us -> 10.6 us  [attend_back(): pl.pallas_call(functools.partial(attend_back_kernel, causal, tile), grid=...]
    ppermute x5 -> x0, waiting for transfers between devices: 37.9 us -> none  [the longest x4 25.4 us: home(): return lax.ppermute(array, 'row', back_perm)]
    ppermute x5 -> x0, starting transfers between devices: 9.01 us -> none  [the longest x4 5.41 us: home(): return lax.ppermute(array, 'row', back_perm)]
    unnamed x227 -> x157, local copies, waits for them, and re-layouts: 25 us -> 22.8 us
  transfers between devices with their start and end apart: 12 -> 6, of which waited for: 5 -> 2; matrix products, arithmetic and copies ran while one was open for 21% -> 18% of each run, Pallas kernels for 46% -> 56%
where the time goes in v5:
time: 675 us; the launch traced here: 668 us
  Pallas kernels  422 us (63%)
  waiting for transfers between devices  83.1 us (12%)
  matrix products  65.5 us (10%)
  local copies, waits for them, and re-layouts  55.3 us (8%)
  other arithmetic  22.4 us (3%)
  between operations  14.9 us (2%)
    pallas_call x1, Pallas kernels, pair_back(): pl.pallas_call(functools.partial(pair_back_kernel, tile, far_tile, units,...  186 us
    all_gather x1, waiting for transfers between devices, fast(): lax.all_gather(down_weight, everyone).reshape(*places, *down_weight.shape)  78.9 us
    pallas_call x1, Pallas kernels, gather_blocks(): pl.pallas_call(functools.partial(gather_kernel, units, count), out_shape=...  58.8 us
    pallas_call x1, Pallas kernels, pair_attend(): pl.pallas_call(functools.partial(pair_attend_kernel, tile), grid=(pairs +...  58.3 us
    pallas_call x1, Pallas kernels, feed(): pl.pallas_call(feed_kernel, grid=(ff // chunk,), in_specs=[whole, whole,...  49 us
    pallas_call x1, Pallas kernels, scatter_blocks(): pl.pallas_call(functools.partial(scatter_kernel, units, count), out_shape...  47.8 us
    dot_general x8, matrix products, over_tokens(): lax.dot_general(left, right, (((0,), (0,)), ((), ())), preferred_element_...  26 us
    dot_general x8, matrix products, by_transposed(): lax.dot_general(left, right, (((1,), (1,)), ((), ())), preferred_element_...  24.6 us
  transfers between devices with their start and end apart: 6, of which 2 were waited for; matrix products, arithmetic and copies ran while one was open for 18% of the time, Pallas kernels for 56%

profile of v5, /device:TPU:0, one launch (start us, length us, event | category | flops | bytes accessed | tf_op | source)
XLA Modules:
  0.0 667.7 jit_solution(11524857007136232967)
XLA Ops:
  18.3 58.8 %shard_map.330 = (bf16[4,2,1,128,1024]{4,3,2,1,0:T(8,128)(2,1)}, bf16[4,2,1,128,1024]{4,3,2,1,0:T(8,128)(2,1)}, bf16[4,2,1,128,1024]{4,3,2,1,0:T(8,128)(2,1)}, bf16[4,2,1,16,512]{4,3,2,1,0:T(8,128)(2,1)}) custom-call(bf16[1,128,256]{2,1,0:T(8,128)(2,1)} %bitcast.211, bf16[1,128,256]{2,1,0:T(8,128)(2,1)} %bitcast.212, bf16[1,128,256]{2,1,0:T(8,128)(2,1)} %bitcast.213, ...), custom_call_target="tpu_custom_call" | custom-call | bytes 12845056 | tf_op jit(solution)/shard_map/pallas_call | solution.py:775
  88.0 58.3 %shard_map.331 = (bf16[750,1024]{1,0:T(8,128)(2,1)S(1)}, f32[750,128]{1,0:T(8,128)S(1)}, bf16[4,750,128]{2,1,0:T(8,128)(2,1)S(1)}, bf16[4,750,128]{2,1,0:T(8,128)(2,1)S(1)}, bf16[4,750,128]{2,1,0:T(8,128)(2,1)S(1)}) custom-call(bf16[750,1024]{1,0:T(8,128)(2,1)S(1)} %convolution_convert_fusion.10.q_ref.q_any.refs_0_, ...), custom_call_target="tpu_custom_call" | custom-call | flops 2304000000 | bytes 12288000 | tf_op jit(solution)/shard_map/pallas_call | solution.py:1191
  150.9 16.5 %copy.43 = bf16[8,4,5,128,256]{3,0,4,1,2:T(8,128)(2,1)} copy(bf16[8,4,5,128,256]{4,3,2,1,0:T(8,128)(2,1)} %bitcast.179) | data formatting | bytes 20971520 | tf_op jit(solution)/shard_map/reshape | solution.py:1510
  167.4 5.7 fusion.86
  179.4 11.4 %shard_map.332 = (bf16[750,1024]{1,0:T(8,128)(2,1)S(1)}, f32[750,128]{1,0:T(8,128)S(1)}) custom-call(bf16[750,1024]{1,0:T(8,128)(2,1)S(1)} %fusion.50.q_ref, bf16[64,1024]{1,0:T(8,128)(2,1)S(1)} %fusion.56.k_ref, bf16[64,1024]{1,0:T(8,128)(2,1)S(1)} %fusion.59.v_ref), custom_call_target="tpu_custom_call" | custom-call | flops 196608000 | bytes 6144000 | tf_op jit(solution)/shard_map/pallas_call | solution.py:484
  198.8 78.9 %all-gather.11.cloned.1.call-done = bf16[16384,256]{1,0:T(8,128)(2,1)} async-done(((bf16[512,256]{1,0:T(8,128)(2,1)}), bf16[16384,256]{1,0:T(8,128)(2,1)}) %all-gather.11.cloned.1.call-update) | async-done | bytes 8388624 | tf_op jit(solution)/shard_map/all_gather | solution.py:1499
  277.7 49.0 %shard_map.333 = (bf16[750,1024]{1,0:T(8,128)(2,1)}, f32[750,1024]{1,0:T(8,128)}, bf16[8,4,128,1024]{3,2,1,0:T(8,128)(2,1)}, bf16[4096,1024]{1,0:T(8,128)(2,1)}) custom-call(bf16[750,1024]{1,0:T(8,128)(2,1)} %add_convert_fusion.h_ref, bf16[750,1024]{1,0:T(8,128)(2,1)} %cot_ref.1, f32[750,1024]{1,0:T(8,128)} %copy-done.10, ...), custom_call_target="tpu_custom_call" | custom-call | flops 37748736000 | bytes 45842432 | tf_op jit(solution)/shard_map/pallas_call | solution.py:566
  327.0 4.6 multiply_reduce_fusion
  335.8 3.4 convert_multiply_fusion
  339.2 3.6 copy.45
  345.2 10.6 %shard_map.334 = (bf16[750,1024]{1,0:T(8,128)(2,1)S(1)}, bf16[64,1024]{1,0:T(8,128)(2,1)S(1)}, bf16[64,1024]{1,0:T(8,128)(2,1)S(1)}) custom-call(bf16[750,1024]{1,0:T(8,128)(2,1)S(1)} %fusion.50.q_ref, bf16[64,1024]{1,0:T(8,128)(2,1)S(1)} %fusion.56.k_ref, bf16[64,1024]{1,0:T(8,128)(2,1)S(1)} %fusion.59.v_ref, ...), custom_call_target="tpu_custom_call" | custom-call | flops 491520000 | bytes 12288000 | tf_op jit(solution)/shard_map/pallas_call | solution.py:527
  357.4 3.9 multiply_reduce_fusion.1
  365.1 3.2 convolution_convert_fusion.7
  371.2 3.4 convolution_convert_fusion.6
  374.6 3.2 convolution_convert_fusion.5
  382.5 185.7 %shard_map.335 = (bf16[750,1024]{1,0:T(8,128)(2,1)}, bf16[750,1024]{1,0:T(8,128)(2,1)}, bf16[750,1024]{1,0:T(8,128)(2,1)}, f32[1,128,256]{2,1,0:T(8,128)}, f32[1...) custom-call(bf16[750,1024]{1,0:T(8,128)(2,1)} %copy-done, ...), custom_call_target="tpu_custom_call" | custom-call | flops 5760000000 | bytes 12288000 | tf_op jit(solution)/shard_map/pallas_call | solution.py:1446
  568.3 4.0 fusion.90
  574.8 3.8 fusion.83
  578.7 3.3 fusion.8
  583.0 5.0 convolution_convert_fusion.4
  588.0 3.5 convolution_convert_fusion.2
  591.5 3.5 convolution_convert_fusion.3
  595.0 47.8 %shard_map.336 = (f32[1,128,256]{2,1,0:T(8,128)}, f32[1,128,256]{2,1,0:T(8,128)}, f32[1,128,256]{2,1,0:T(8,128)}, f32[1,16,128]{2,1,0:T(8,128)}) custom-call(bf16[4,2,1,128,1024]{4,3,2,1,0:T(8,128)(2,1)} %bitcast.197, bf16[4,2,1,128,1024]{4,3,2,1,0:T(8,128)(2,1)} %bitcast.199, bf16[4,2,1,128,1024]{4,3,2,1,0:T(8,128)(2,1)} %bitcast.198, ...), custom_call_target="tpu_custom_call" | custom-call | flops 3211264 | bytes 12845056 | tf_op jit(solution)/shard_map/pallas_call | solution.py:978
  649.0 3.9 add_add_fusion.3
  (241 shorter events, 77.7 us)
Async XLA Ops:
  7.2 71.4 %copy-start.14 = (bf16[750,1024]{1,0:T(8,128)(2,1)S(1)}, bf16[750,1024]{1,0:T(8,128)(2,1)}, u32[]{:S(2)}) copy-start(bf16[750,1024]{1,0:T(8,128)(2,1)} %param.21) | copy-start | bytes 4608004
  7.2 143.7 %all-gather.7.cloned.1.call-start = ((), (), s32[]{:S(2)}) async-start(), calls=%async_computation.2 | async-start | bytes 10813440 | tf_op jit(solution)/shard_map/all_gather | solution.py:1510
  12.3 186.5 %all-gather.9.cloned.1.call-start = ((), (), s32[]{:S(2)}) async-start(), calls=%async_computation.3 | async-start | bytes 8650752 | tf_op jit(solution)/shard_map/all_gather | solution.py:1498
  13.1 264.6 %all-gather.11.cloned.1.call-start = ((), (), s32[]{:S(2)}) async-start(), calls=%async_computation.4 | async-start | bytes 8650752 | tf_op jit(solution)/shard_map/all_gather | solution.py:1499
  13.8 639.2 %reduce-scatter.2.cloned.1.call-start = ((), (), s32[]{:S(2)}) async-start(), calls=%async_computation.1 | async-start | bytes 8650752 | tf_op jit(solution)/shard_map/reduce_scatter | solution.py:1536
  13.9 161.7 %collective-permute-start = (bf16[32,1024]{1,0:T(8,128)(2,1)}, bf16[32,1024]{1,0:T(8,128)(2,1)S(1)}, u32[]{:S(2)}, u32[]{:S(2)}) collective-permute-start(bf16[32,1024]{1,0:T(8,128)(2,1)} %param.22), channel_id=1, source_target_pairs={{0,4},{8,12},{16,20},{24,28},{4,0},{12,8},{20,16},{28,24},{1,5},{9... | collective-permute-start | bytes 196616 | tf_op jit(solution)/shard_map/ppermute | solution.py:1525
  78.3 7.9 %copy-start.56 = (f32[1024]{0:T(1024)}, f32[1024]{0:T(1024)S(1)}, u32[]{:S(2)}) copy-start(f32[1024]{0:T(1024)S(1)} %add.103) | copy-start | bytes 12292
  78.4 99.1 %copy-start.50 = (f32[1024]{0:T(1024)}, f32[1024]{0:T(1024)S(1)}, u32[]{:S(2)}) copy-start(f32[1024]{0:T(1024)S(1)} %mul.192) | copy-start | bytes 12292
  78.5 99.0 %copy-start.58 = (f32[1024]{0:T(1024)}, f32[1024]{0:T(1024)S(1)}, u32[]{:S(2)}) copy-start(f32[1024]{0:T(1024)S(1)} %add.108) | copy-start | bytes 12292
  150.9 22.3 %copy-start.1 = (bf16[750,1024]{1,0:T(8,128)(2,1)}, bf16[750,1024]{1,0:T(8,128)(2,1)S(1)}, u32[]{:S(2)}) copy-start(bf16[750,1024]{1,0:T(8,128)(2,1)S(1)} %get-tuple-element.66.refs_4_) | copy-start | bytes 4608004
  173.1 17.7 %copy-start.28 = (bf16[1,8,128,4,256]{2,1,4,3,0:T(8,128)(2,1)}, bf16[1,8,128,4,256]{2,1,4,3,0:T(8,128)(2,1)S(1)}, u32[]{:S(2)}) copy-start(bf16[1,8,128,4,256]{2,1,4,3,0:T(8,128)(2,1)S(1)} %get-tuple-element.107) | copy-start | bytes 6291460
  175.0 15.8 %copy-start.18 = (f32[750,1024]{1,0:T(8,128)}, f32[750,1024]{1,0:T(8,128)S(1)}, u32[]{:S(2)}) copy-start(f32[750,1024]{1,0:T(8,128)S(1)} %get-tuple-element.125) | copy-start | bytes 9216004
  345.2 12.2 %copy-start.19 = (f32[750,1024]{1,0:T(8,128)S(1)}, f32[750,1024]{1,0:T(8,128)}, u32[]{:S(2)}) copy-start(f32[750,1024]{1,0:T(8,128)} %copy-done.18) | copy-start | bytes 9216004
  345.2 12.2 %copy-start.51 = (f32[1024]{0:T(1024)S(1)}, f32[1024]{0:T(1024)}, u32[]{:S(2)}) copy-start(f32[1024]{0:T(1024)} %copy-done.50) | copy-start | bytes 12292
  345.2 12.2 %copy-start.53 = (f32[750]{0:T(1024)S(1)}, f32[750]{0:T(1024)}, u32[]{:S(2)}) copy-start(f32[750]{0:T(1024)} %copy-done.52) | copy-start | bytes 9004
  355.9 22.3 %collective-permute-start.1 = (bf16[32,2048]{1,0:T(8,128)(2,1)S(1)}, bf16[32,2048]{1,0:T(8,128)(2,1)S(1)}, u32[]{:S(2)}, u32[]{:S(2)}) collective-permute-start(bf16[32,2048]{1,0:T(8,128)(2,1)S(1)} %broadcast_select_fusion), channel_id=1, source_target_pairs={{0,4},{8,12},{16,20},{24,28},{4,0},{12,8},{20,16},{28,24},{1,5},{9... | collective-permute-start | bytes 393224 | tf_op jit(solution)/shard_map/ppermute | solution.py:1555
  649.0 6.5 copy-start.42
  649.0 7.1 %copy-start.41 = (f32[1,128,256]{2,1,0:T(8,128)S(1)}, f32[1,128,256]{2,1,0:T(8,128)}, u32[]{:S(2)}) copy-start(f32[1,128,256]{2,1,0:T(8,128)} %get-tuple-element.84) | copy-start | bytes 393220
  649.0 7.8 %copy-start.40 = (f32[1,128,256]{2,1,0:T(8,128)S(1)}, f32[1,128,256]{2,1,0:T(8,128)}, u32[]{:S(2)}) copy-start(f32[1,128,256]{2,1,0:T(8,128)} %get-tuple-element.85) | copy-start | bytes 393220
  649.0 8.4 %copy-start.39 = (f32[1,128,256]{2,1,0:T(8,128)S(1)}, f32[1,128,256]{2,1,0:T(8,128)}, u32[]{:S(2)}) copy-start(f32[1,128,256]{2,1,0:T(8,128)} %get-tuple-element.86) | copy-start | bytes 393220
  649.0 9.1 %copy-start.38 = (f32[1,128,256]{2,1,0:T(8,128)S(1)}, f32[1,128,256]{2,1,0:T(8,128)}, u32[]{:S(2)}) copy-start(f32[1,128,256]{2,1,0:T(8,128)} %get-tuple-element.87) | copy-start | bytes 393220
  649.0 9.7 %copy-start.37 = (f32[1,128,256]{2,1,0:T(8,128)S(1)}, f32[1,128,256]{2,1,0:T(8,128)}, u32[]{:S(2)}) copy-start(f32[1,128,256]{2,1,0:T(8,128)} %get-tuple-element.88) | copy-start | bytes 393220
  649.0 10.4 %copy-start.36 = (f32[1,128,256]{2,1,0:T(8,128)S(1)}, f32[1,128,256]{2,1,0:T(8,128)}, u32[]{:S(2)}) copy-start(f32[1,128,256]{2,1,0:T(8,128)} %get-tuple-element.89) | copy-start | bytes 393220
  653.0 7.1 %copy-start.32 = (f32[4,128,256]{2,1,0:T(8,128)S(1)}, f32[4,128,256]{2,1,0:T(8,128)}, u32[]{:S(2)}) copy-start(f32[4,128,256]{2,1,0:T(8,128)} %get-tuple-element.91) | copy-start | bytes 1572868
  (51 other events, 144.7 us)
Sparse Core Ops, SparseCore 0:
  12.4 104.4 all-gather.6
  119.8 78.8 all-gather.8
  201.6 76.0 all-gather.10
  326.9 160.1 reduce-scatter.1

commit v6 on v5

--- a/solution.py
+++ b/solution.py
@@ -488,49 +488,6 @@
         compiler_params=pltpu.CompilerParams(vmem_limit_bytes=40<<20),
         cost_estimate=pl.CostEstimate(flops=4*rows*keys*width,bytes_accessed=8*rows*width,transcendentals=rows*keys*width//64))(q,k,v)
 
-def attend_back_kernel(causal,tile,q_ref,k_ref,v_ref,do_ref,st_ref,dq_ref,dk_ref,dv_ref,acc):
-    rows=q_ref.shape[0]; keys=k_ref.shape[0]
-    low=lax.broadcasted_iota(jnp.int32,(1,128),1)<HEAD_DIM
-    acc[...]=jnp.zeros_like(acc)
-    for start in range(0,keys,tile):
-        n=min(tile,keys-start)
-        k=k_ref[start:start+n,:]*jnp.bfloat16(HEAD_DIM**-0.5)
-        v=v_ref[start:start+n,:]
-        spans=[(0,rows)]
-        if causal: spans=[(start,n)]+([(start+n,rows-start-n)] if start+n<rows else [])
-        dks=[];dvs=[]
-        for h in range(2):
-            mine=low if h==0 else jnp.logical_not(low)
-            kh=jnp.where(mine,k,jnp.bfloat16(0)); vh=jnp.where(mine,v,jnp.bfloat16(0))
-            dk=dv=None
-            for at,length in spans:
-                qs=q_ref[at:at+length,:]; do=do_ref[at:at+length,:]
-                s=dg(kh,qs,NT)
-                p=jnp.exp(s-st_ref[0,h:h+1,at:at+length])
-                if causal and at==start:
-                    ok=lax.broadcasted_iota(jnp.int32,s.shape,0)<=lax.broadcasted_iota(jnp.int32,s.shape,1)
-                    p=jnp.where(ok,p,0.0)
-                dp=dg(vh,do,NT)
-                ds=(p*(dp-st_ref[0,2+h:3+h,at:at+length])).astype(jnp.bfloat16)
-                a=dg(p.astype(jnp.bfloat16),do,NN); b=dg(ds,qs,NN)
-                dv=a if dv is None else dv+a
-                dk=b if dk is None else dk+b
-                acc[at:at+length,:]+=dg(ds,kh,TN)
-            dks.append(dk);dvs.append(dv)
-        dk_ref[start:start+n,:]=(jnp.where(low,dks[0],dks[1])*HEAD_DIM**-0.5).astype(dk_ref.dtype)
-        dv_ref[start:start+n,:]=jnp.where(low,dvs[0],dvs[1]).astype(dv_ref.dtype)
-    dq_ref[...]=acc[...].astype(dq_ref.dtype)
-
-def attend_back(q,k,v,do,stats,causal,out_dtype,tile=256):
-    rows,width=q.shape; keys=k.shape[0]
-    bq=pl.BlockSpec((rows,128),lambda i:(0,i)); bk=pl.BlockSpec((keys,128),lambda i:(0,i))
-    return pl.pallas_call(functools.partial(attend_back_kernel,causal,tile),grid=(width//128,),
-        in_specs=[bq,bk,bk,bq,pl.BlockSpec((1,4,rows),lambda i:(i,0,0))],out_specs=[bq,bk,bk],
-        out_shape=[jax.ShapeDtypeStruct((rows,width),out_dtype),jax.ShapeDtypeStruct((keys,width),out_dtype),jax.ShapeDtypeStruct((keys,width),out_dtype)],
-        scratch_shapes=[pltpu.VMEM((rows,128),jnp.float32)],
-        compiler_params=pltpu.CompilerParams(vmem_limit_bytes=40<<20),
-        cost_estimate=pl.CostEstimate(flops=10*rows*keys*width,bytes_accessed=16*rows*width,transcendentals=rows*keys*width//64))(q,k,v,do,stats)
-
 def feed_kernel(h_ref,cot_ref,res_ref,up_ref,down_ref,out_ref,g_ref,dup_ref,ddown_ref,acc):
     i=pl.program_id(0)
     @pl.when(i==0)
@@ -1241,6 +1198,46 @@
         put(start, n, jnp.where(low, dks[0], dks[1]) * HEAD_DIM**-0.5, jnp.where(low, dvs[0], dvs[1]))
 
 
+def pair_stats(pair, mix_ref, do_ref, logs_ref):
+    lane = lax.broadcasted_iota(jnp.int32, (8, 128), 1)
+    line = lax.broadcasted_iota(jnp.int32, (8, 128), 0)
+    picked = ((line < 2) & (line + 2 * pair == lane)).astype(jnp.float32)
+    halves = (((line == 2) & (lane < HEAD_DIM)) | ((line == 3) & (lane >= HEAD_DIM))).astype(jnp.float32)
+    products = mix_ref[...].astype(jnp.float32) * do_ref[...].astype(jnp.float32)
+    logs = lax.dot_general(
+        picked, logs_ref[...], NT, precision=lax.Precision.HIGHEST, preferred_element_type=jnp.float32)
+    return logs + lax.dot_general(
+        halves, products, NT, precision=lax.Precision.HIGHEST, preferred_element_type=jnp.float32)
+
+
+def cross_back_kernel(q_ref, k_ref, v_ref, do_ref, mix_ref, logs_ref, dq_ref, dk_ref, dv_ref, acc, stats):
+    stats[...] = pair_stats(pl.program_id(0), mix_ref, do_ref, logs_ref)
+
+    def put(start, n, dk, dv):
+        dk_ref[start : start + n, :] = dk.astype(dk_ref.dtype)
+        dv_ref[start : start + n, :] = dv.astype(dv_ref.dtype)
+
+    back_pair(k_ref.shape[0], False, q_ref, k_ref, v_ref, do_ref, stats, acc, put)
+    dq_ref[...] = acc[...].astype(dq_ref.dtype)
+
+
+def cross_back(q, k, v, do, mix, logs):
+    rows, width = q.shape
+    keys = k.shape[0]
+    long, short = pl.BlockSpec((rows, 128), lambda i: (0, i)), pl.BlockSpec((keys, 128), lambda i: (0, i))
+    return pl.pallas_call(
+        cross_back_kernel,
+        grid=(width // 128,),
+        in_specs=[long, short, short, long, long, pl.BlockSpec((rows, 128), lambda i: (0, 0))],
+        out_specs=[long, short, short],
+        out_shape=[jax.ShapeDtypeStruct(a.shape, jnp.bfloat16) for a in (q, k, v)],
+        scratch_shapes=[pltpu.VMEM((rows, 128), jnp.float32), pltpu.VMEM((8, rows), jnp.float32)],
+        compiler_params=pltpu.CompilerParams(vmem_limit_bytes=40 << 20),
+        cost_estimate=pl.CostEstimate(
+            flops=10 * rows * keys * width, bytes_accessed=10 * rows * width, transcendentals=rows * keys * width // HEAD_DIM),
+    )(q, k, v, do, mix, logs)
+
+
 def pair_back_kernel(tile, far_tile, units, count, events, *refs):
     q_ref, k_ref, v_ref, do_ref, mix_ref, logs_ref, do_any, fq_any, fk_any, fv_any = refs[:10]
     grads, (dq_ref, dk_ref, dv_ref) = refs[10 : 10 + count], refs[10 + count : 13 + count]
@@ -1254,8 +1251,6 @@
     fars = pairs // 2
     first, second = place.y == 0, place.y == 1
     partner = place.across("y")
-    lane = lax.broadcasted_iota(jnp.int32, (8, 128), 1)
-    line = lax.broadcasted_iota(jnp.int32, (8, 128), 0)
 
     def columns(pair):
         return pl.ds(pl.multiple_of(pair * 128, 128), 128)
@@ -1314,14 +1309,7 @@
     @pl.when(step < pairs)
     def _():
         pair = lax.rem(step + fars, pairs)
-        picked = ((line < 2) & (line + 2 * pair == lane)).astype(jnp.float32)
-        halves = (((line == 2) & (lane < HEAD_DIM)) | ((line == 3) & (lane >= HEAD_DIM))).astype(jnp.float32)
-        products = mix_ref[...].astype(jnp.float32) * do_ref[...].astype(jnp.float32)
-        both = lax.dot_general(
-            picked, logs_ref[...], NT, precision=lax.Precision.HIGHEST, preferred_element_type=jnp.float32)
-        both += lax.dot_general(
-            halves, products, NT, precision=lax.Precision.HIGHEST, preferred_element_type=jnp.float32)
-        stats[pair] = both
+        stats[pair] = pair_stats(pair, mix_ref, do_ref, logs_ref)
 
         def put(start, n, dk, dv):
             near[1, pair, start : start + n, :] = dk
@@ -1429,14 +1417,11 @@
                     back_over(which, j).wait_send()
 
 
-BACK_ORDERS = ("yzx", "yzx", "xzy", "yzx", "yzx", "zyx", "yzx", "yxz", "yzx")
-
-
 def pair_back(q, k, v, do, mix, logs, far, grads, collective_id, events, tile=384, far_tile=256):
     rows, width = q.shape
     pairs = width // 128
     fars = pairs // 2
-    blocks, units, scratch = scatter_plan(grads, 256, BACK_ORDERS)
+    blocks, units, scratch = scatter_plan(grads, 256, ORDERS)
     count = len(grads)
     block = pl.BlockSpec((rows, 128), lambda i: (0, lax.rem(jnp.minimum(i, pairs - 1) + fars, pairs)))
     joined = pl.BlockSpec((rows, 128), lambda i: (0, jnp.maximum(i - pairs - fars, 0)))
@@ -1504,11 +1489,11 @@
     def flat(array):
         return array.reshape(-1, array.shape[-1])
 
-    early = gather_blocks([small(self_query), small(self_key), small(self_value), gains], 1, 128)
+    early = gather_blocks(
+        [small(self_query), small(self_key), small(self_value), gains, small(self_output), small(cross_query),
+         small(cross_key), small(cross_value), small(cross_output)], 1, 128)
     query_self, key_self, value_self = [flat(w) for w in early[:3]]
-    between = jnp.stack([self_output, cross_query, cross_key, cross_value, cross_output])
-    between = lax.all_gather(between, everyone).reshape(*places, *between.shape).transpose(2, 0, 3, 1, 4)
-    out_self, query_cross, key_cross, value_cross, out_cross = between.reshape(-1, width, width)
+    out_self, query_cross, key_cross, value_cross, out_cross = [flat(w) for w in early[4:]]
     norm_params = early[3].reshape(pairs * 2, 16, -1, 128)[:, :6, :, :piece].transpose(1, 0, 2, 3)
     norm_params = norm_params.reshape(6, width).astype(jnp.float32)
 
@@ -1518,7 +1503,6 @@
     self_v = matmul(hidden_one, value_self).astype(jnp.bfloat16)
     self_q = matmul(hidden_one, query_self).astype(jnp.bfloat16)
     self_mix, log_lanes, far_q, far_k, far_v = pair_attend(self_q, self_k, self_v, 5)
-    half_heads = half // HEAD_DIM
     resid_one = frames + matmul(self_mix, out_self)
     hidden_two = norm_forward(resid_one, norm_params[2], norm_params[3]).astype(jnp.bfloat16)
     cross_q = matmul(hidden_two, query_cross).astype(jnp.bfloat16)
@@ -1529,17 +1513,10 @@
     text_k = matmul(clip_text, key_cross).astype(jnp.bfloat16)
     text_v = matmul(clip_text, value_cross).astype(jnp.bfloat16)
     cross_mix, cross_logs = attend(cross_q, text_k, text_v, False, jnp.bfloat16)
-    cross_logs = cross_logs[:, : 2 * half_heads]
     resid_two = resid_one + matmul(cross_mix, out_cross)
     hidden_three = norm_forward(resid_two, norm_params[4], norm_params[5]).astype(jnp.bfloat16)
     layer_out, grad_three, up_grad, down_grad = feed(hidden_three, cotangent, resid_two, up_blocks, down_blocks)
     up_sum = lax.psum_scatter(up_grad.reshape(-1, *up_weight.shape), everyone, scatter_dimension=0).astype(jnp.float32)
-
-    def stats_of(logs, mix, grad):
-        products = mix.astype(jnp.float32) * grad.astype(jnp.float32)
-        dots = jnp.sum(products.reshape(rows, -1, HEAD_DIM), axis=-1)
-        both = jnp.stack([logs.T.reshape(-1, 2, rows), dots.T.reshape(-1, 2, rows)], axis=1)
-        return both.reshape(-1, 4, rows)
 
     cotan_full = cotangent.astype(jnp.float32)
     unused_three, pull_three = jax.vjp(norm_forward, resid_two, norm_params[4], norm_params[5])
@@ -1548,8 +1525,7 @@
     grad_cross = grad_resid_two.astype(jnp.bfloat16)
     cross_out_grad = over_tokens(cross_mix, grad_cross)
     grad_cross_mix = by_transposed(grad_cross, out_cross).astype(jnp.bfloat16)
-    grad_cross_q, text_k_part, text_v_part = attend_back(
-        cross_q, text_k, text_v, grad_cross_mix, stats_of(cross_logs, cross_mix, grad_cross_mix), False, jnp.bfloat16)
+    grad_cross_q, text_k_part, text_v_part = cross_back(cross_q, text_k, text_v, grad_cross_mix, cross_mix, cross_logs)
     text_rows = text_states.shape[0]
     text_parts = jnp.concatenate([text_k_part, text_v_part], axis=1)
     given = lax.ppermute(by_side(text_parts[text_rows:], text_parts[:text_rows]), "row", swap)
@@ -1574,7 +1550,7 @@
     (grad_self_q, grad_self_k, grad_self_v), early_sums = pair_back(
         self_q, self_k, self_v, grad_self_mix, self_mix, log_lanes, (far_q, far_k, far_v),
         [by_place(g, 1) for g in (self_out_grad, cross_query_part, cross_key_part, cross_value_part, cross_out_grad)]
-        + [by_place(down_grad, down_weight.shape[0] // block_rows)], 4, [4] * 12)
+        + [by_place(down_grad, down_weight.shape[0] // block_rows)], 4, [5] * 12)
     self_query_part = over_tokens(hidden_one, grad_self_q)
     self_key_part = over_tokens(hidden_one, grad_self_k)
     self_value_part = over_tokens(hidden_one, grad_self_v)

time: 675 us -> 638 us (0.945)
  waiting for transfers between devices: 83.1 us -> 1.4 us
  Pallas kernels: 422 us -> 500 us
  local copies, waits for them, and re-layouts: 55.3 us -> 18.7 us
    pallas_call x1, Pallas kernels: 58.8 us -> 138 us  [gather_blocks(): pl.pallas_call(functools.partial(gather_kernel, units, count), out_shape=...]
    all_gather x1, waiting for transfers between devices: 78.9 us -> 0.01 us  [fast(): lax.all_gather(down_weight, everyone).reshape(*places, *down_weight.shape)]
    pallas_call x1, Pallas kernels: 186 us -> 165 us  [pair_back(): pl.pallas_call(functools.partial(pair_back_kernel, tile, far_tile, units,...]
    reshape x2 -> x0, local copies, waits for them, and re-layouts: 16.6 us -> none  [the longest x1 16.5 us: fast(): lax.all_gather(between, everyone).reshape(*places, *between.shape)]
    pallas_call x1, Pallas kernels: 58.3 us -> 69.9 us  [pair_attend(): pl.pallas_call(functools.partial(pair_attend_kernel, tile), grid=(pairs +...]
    unnamed x157 -> x103, local copies, waits for them, and re-layouts: 22.8 us -> 13.2 us
    pallas_call x1, Pallas kernels: 10.6 us -> 19.3 us  [cross_back(): pl.pallas_call(cross_back_kernel, grid=(width // 128,), in_specs=[long, s...]
  transfers between devices with their start and end apart: 6 -> 5, of which waited for: 2 -> 0; matrix products, arithmetic and copies ran while one was open for 18% -> 14% of each run, Pallas kernels for 56% -> 72%
where the time goes in v6:
time: 638 us; the launch traced here: 630 us
  Pallas kernels  500 us (78%)
  matrix products  65.7 us (10%)
  other arithmetic  21.3 us (3%)
  local copies, waits for them, and re-layouts  18.7 us (3%)
  between operations  14.7 us (2%)
  starting transfers between devices  8.07 us (1%)
    pallas_call x1, Pallas kernels, pair_back(): pl.pallas_call(functools.partial(pair_back_kernel, tile, far_tile, units,...  165 us
    pallas_call x1, Pallas kernels, gather_blocks(): pl.pallas_call(functools.partial(gather_kernel, units, count), out_shape=...  138 us
    pallas_call x1, Pallas kernels, pair_attend(): pl.pallas_call(functools.partial(pair_attend_kernel, tile), grid=(pairs +...  69.9 us
    pallas_call x1, Pallas kernels, feed(): pl.pallas_call(feed_kernel, grid=(ff // chunk,), in_specs=[whole, whole,...  48.8 us
    pallas_call x1, Pallas kernels, scatter_blocks(): pl.pallas_call(functools.partial(scatter_kernel, units, count), out_shape...  47.5 us
    dot_general x8, matrix products, over_tokens(): lax.dot_general(left, right, (((0,), (0,)), ((), ())), preferred_element_...  25.9 us
    dot_general x8, matrix products, by_transposed(): lax.dot_general(left, right, (((1,), (1,)), ((), ())), preferred_element_...  22.1 us
    pallas_call x1, Pallas kernels, cross_back(): pl.pallas_call(cross_back_kernel, grid=(width // 128,), in_specs=[long, s...  19.3 us
  transfers between devices with their start and end apart: 5, of which 0 were waited for; matrix products, arithmetic and copies ran while one was open for 14% of the time, Pallas kernels for 72%

profile of v6, /device:TPU:0, one launch (start us, length us, event | category | flops | bytes accessed | tf_op | source)
XLA Modules:
  0.0 630.1 jit_solution(17100965321770833247)
XLA Ops:
  8.7 3.0 collective-permute-start
  13.1 138.3 %shard_map.330 = (bf16[4,2,1,128,1024]{4,3,2,1,0:T(8,128)(2,1)}, bf16[4,2,1,128,1024]{4,3,2,1,0:T(8,128)(2,1)}, bf16[4,2,1,128,1024]{4,3,2,1,0:T(8,128)(2,1)}, b...) custom-call(bf16[1,128,256]{2,1,0:T(8,128)(2,1)} %bitcast.136, ...), custom_call_target="tpu_custom_call" | custom-call | bytes 33816576 | tf_op jit(solution)/shard_map/pallas_call | solution.py:732
  155.2 3.0 convolution_convert_fusion.12.k_ref.k_any.refs_1_
  158.2 3.0 convolution_convert_fusion.11.v_ref.v_any.refs_2_
  163.0 69.9 %shard_map.331 = (bf16[750,1024]{1,0:T(8,128)(2,1)S(1)}, f32[750,128]{1,0:T(8,128)S(1)}, bf16[4,750,128]{2,1,0:T(8,128)(2,1)S(1)}, bf16[4,750,128]{2,1,0:T(8,128)(2,1)S(1)}, bf16[4,750,128]{2,1,0:T(8,128)(2,1)S(1)}) custom-call(bf16[750,1024]{1,0:T(8,128)(2,1)S(1)} %convolution_convert_fusion.13.q_ref.q_any.refs_0_, ...), custom_call_target="tpu_custom_call" | custom-call | flops 2304000000 | bytes 12288000 | tf_op jit(solution)/shard_map/pallas_call | solution.py:1148
  244.1 11.6 %shard_map.332 = (bf16[750,1024]{1,0:T(8,128)(2,1)S(1)}, f32[750,128]{1,0:T(8,128)S(1)}) custom-call(bf16[750,1024]{1,0:T(8,128)(2,1)S(1)} %convolution_convert_fusion.10.q_ref, bf16[64,1024]{1,0:T(8,128)(2,1)S(1)} %convolution_convert_fusion.15.k_ref, bf16[64,1024]{1,0:T(8,128)(2,1)S(1)} %convolution_convert_fusion.14.v_ref), custom_call_target="tpu_custom_call" | custom-call | flops 196608000 | bytes 6144000 | tf_op jit(solution)/shard_map/pallas_call | solution.py:484
  261.0 48.8 %shard_map.333 = (bf16[750,1024]{1,0:T(8,128)(2,1)}, f32[750,1024]{1,0:T(8,128)}, bf16[8,4,128,1024]{3,2,1,0:T(8,128)(2,1)}, bf16[4096,1024]{1,0:T(8,128)(2,1)}) custom-call(bf16[750,1024]{1,0:T(8,128)(2,1)} %add_convert_fusion.h_ref, bf16[750,1024]{1,0:T(8,128)(2,1)} %cot_ref.1, f32[750,1024]{1,0:T(8,128)} %copy-done.9, ...), custom_call_target="tpu_custom_call" | custom-call | flops 37748736000 | bytes 45842432 | tf_op jit(solution)/shard_map/pallas_call | solution.py:523
  309.9 4.0 multiply_reduce_fusion
  319.3 19.3 %shard_map.334 = (bf16[750,1024]{1,0:T(8,128)(2,1)S(1)}, bf16[64,1024]{1,0:T(8,128)(2,1)S(1)}, bf16[64,1024]{1,0:T(8,128)(2,1)S(1)}) custom-call(bf16[750,1024]{1,0:T(8,128)(2,1)S(1)} %convolution_convert_fusion.10.q_ref, bf16[64,1024]{1,0:T(8,128)(2,1)S(1)} %convolution_convert_fusion.15.k_ref, bf16[64,1024]{1,0:T(8,128)(2,1)S(1)} %convolution_convert_fusion.14.v_ref, ...), custom_call_target="tpu_custom_call" | custom-call | flops 491520000 | bytes 7680000 | tf_op jit(solution)/shard_map/pallas_call | solution.py:1228
  338.7 4.9 collective-permute-start.1
  348.4 3.2 convolution_convert_fusion.7
  351.6 3.0 convolution_convert_fusion.8.refs_3_.refs_6_
  354.6 3.4 convolution_convert_fusion.6
  357.9 3.2 convolution_convert_fusion.5
  365.7 164.7 %shard_map.335 = (bf16[750,1024]{1,0:T(8,128)(2,1)}, bf16[750,1024]{1,0:T(8,128)(2,1)}, bf16[750,1024]{1,0:T(8,128)(2,1)}, f32[1,128,256]{2,1,0:T(8,128)}, f32[1...) custom-call(bf16[750,1024]{1,0:T(8,128)(2,1)} %copy-done, ...), custom_call_target="tpu_custom_call" | custom-call | flops 5760000000 | bytes 12288000 | tf_op jit(solution)/shard_map/pallas_call | solution.py:1431
  530.5 4.0 fusion.37
  537.0 3.9 fusion.31
  541.0 3.3 fusion.8
  545.2 5.0 convolution_convert_fusion.4
  550.3 3.4 convolution_convert_fusion.2
  553.7 3.4 convolution_convert_fusion.3
  557.2 47.5 %shard_map.336 = (f32[1,128,256]{2,1,0:T(8,128)}, f32[1,128,256]{2,1,0:T(8,128)}, f32[1,128,256]{2,1,0:T(8,128)}, f32[1,16,128]{2,1,0:T(8,128)}) custom-call(bf16[4,2,1,128,1024]{4,3,2,1,0:T(8,128)(2,1)} %bitcast.123, bf16[4,2,1,128,1024]{4,3,2,1,0:T(8,128)(2,1)} %bitcast.125, bf16[4,2,1,128,1024]{4,3,2,1,0:T(8,128)(2,1)} %bitcast.124, ...), custom_call_target="tpu_custom_call" | custom-call | flops 3211264 | bytes 12845056 | tf_op jit(solution)/shard_map/pallas_call | solution.py:935
  608.4 3.0 convolution_add_fusion.1
  611.5 3.9 add_add_fusion.3
  (172 shorter events, 54.5 us)
Async XLA Ops:
  7.2 147.4 %copy-start.11 = (bf16[750,1024]{1,0:T(8,128)(2,1)S(1)}, bf16[750,1024]{1,0:T(8,128)(2,1)}, u32[]{:S(2)}) copy-start(bf16[750,1024]{1,0:T(8,128)(2,1)} %param.21) | copy-start | bytes 4608004
  7.2 253.8 %all-gather.5.cloned.1.call-start = ((), (), s32[]{:S(2)}) async-start(), calls=%async_computation.2 | async-start | bytes 8650752 | tf_op jit(solution)/shard_map/all_gather | solution.py:1483
  7.9 253.0 %all-gather.7.cloned.1.call-start = ((), (), s32[]{:S(2)}) async-start(), calls=%async_computation.3 | async-start | bytes 8650752 | tf_op jit(solution)/shard_map/all_gather | solution.py:1484
  8.7 606.7 %reduce-scatter.2.cloned.1.call-start = ((), (), s32[]{:S(2)}) async-start(), calls=%async_computation.1 | async-start | bytes 8650752 | tf_op jit(solution)/shard_map/reduce_scatter | solution.py:1519
  8.7 231.1 %collective-permute-start = (bf16[32,1024]{1,0:T(8,128)(2,1)}, bf16[32,1024]{1,0:T(8,128)(2,1)S(1)}, u32[]{:S(2)}, u32[]{:S(2)}) collective-permute-start(bf16[32,1024]{1,0:T(8,128)(2,1)} %param.22), channel_id=1, source_target_pairs={{0,4},{8,12},{16,20},{24,28},{4,0},{12,8},{20,16},{28,24},{1,5},{9... | collective-permute-start | bytes 196616 | tf_op jit(solution)/shard_map/ppermute | solution.py:1509
  163.0 70.0 %copy-start = (bf16[750,1024]{1,0:T(8,128)(2,1)}, bf16[750,1024]{1,0:T(8,128)(2,1)S(1)}, u32[]{:S(2)}) copy-start(bf16[750,1024]{1,0:T(8,128)(2,1)S(1)} %convolution_convert_fusion.13.q_ref.q_any.refs_0_) | copy-start | bytes 4608004
  163.0 70.0 %copy-start.35 = (bf16[4,2,1,128,1024]{4,3,2,1,0:T(8,128)(2,1)S(1)}, bf16[4,2,1,128,1024]{4,3,2,1,0:T(8,128)(2,1)}, u32[]{:S(2)}) copy-start(bf16[4,2,1,128,1024]{4,3,2,1,0:T(8,128)(2,1)} %get-tuple-element.72) | copy-start | bytes 6291460
  239.8 15.9 %copy-start.16 = (f32[750,1024]{1,0:T(8,128)S(1)}, f32[750,1024]{1,0:T(8,128)}, u32[]{:S(2)}) copy-start(f32[750,1024]{1,0:T(8,128)} %copy-done.15) | copy-start | bytes 9216004
  239.8 15.9 %copy-start.39 = (bf16[4,2,1,128,1024]{4,3,2,1,0:T(8,128)(2,1)S(1)}, bf16[4,2,1,128,1024]{4,3,2,1,0:T(8,128)(2,1)}, u32[]{:S(2)}) copy-start(bf16[4,2,1,128,1024]{4,3,2,1,0:T(8,128)(2,1)} %get-tuple-element.77) | copy-start | bytes 6291460
  309.8 4.6 copy-start.18
  319.3 24.4 %copy-start.17 = (f32[750,1024]{1,0:T(8,128)S(1)}, f32[750,1024]{1,0:T(8,128)}, u32[]{:S(2)}) copy-start(f32[750,1024]{1,0:T(8,128)} %copy-done.15) | copy-start | bytes 9216004
  319.3 24.3 %copy-start.38 = (bf16[4,2,1,128,1024]{4,3,2,1,0:T(8,128)(2,1)S(1)}, bf16[4,2,1,128,1024]{4,3,2,1,0:T(8,128)(2,1)}, u32[]{:S(2)}) copy-start(bf16[4,2,1,128,1024]{4,3,2,1,0:T(8,128)(2,1)} %get-tuple-element.73) | copy-start | bytes 6291460
  338.7 22.8 %collective-permute-start.1 = (bf16[32,2048]{1,0:T(8,128)(2,1)S(1)}, bf16[32,2048]{1,0:T(8,128)(2,1)S(1)}, u32[]{:S(2)}, u32[]{:S(2)}) collective-permute-start(bf16[32,2048]{1,0:T(8,128)(2,1)S(1)} %broadcast_select_fusion), channel_id=1, source_target_pairs={{0,4},{8,12},{16,20},{24,28},{4,0},{12,8},{20,16},{28,24},{1,5},{9... | collective-permute-start | bytes 393224 | tf_op jit(solution)/shard_map/ppermute | solution.py:1531
  545.2 5.0 copy-start.43
  604.7 6.7 %copy-start.14 = (f32[750,1024]{1,0:T(8,128)S(1)}, f32[750,1024]{1,0:T(8,128)}, u32[]{:S(2)}) copy-start(f32[750,1024]{1,0:T(8,128)} %copy-done.13) | copy-start | bytes 9216004
  611.4 5.8 copy-start.29
  611.4 6.5 %copy-start.28 = (f32[1,128,256]{2,1,0:T(8,128)S(1)}, f32[1,128,256]{2,1,0:T(8,128)}, u32[]{:S(2)}) copy-start(f32[1,128,256]{2,1,0:T(8,128)} %get-tuple-element.93) | copy-start | bytes 393220
  611.4 7.1 %copy-start.27 = (f32[1,128,256]{2,1,0:T(8,128)S(1)}, f32[1,128,256]{2,1,0:T(8,128)}, u32[]{:S(2)}) copy-start(f32[1,128,256]{2,1,0:T(8,128)} %get-tuple-element.94) | copy-start | bytes 393220
  611.4 7.8 %copy-start.26 = (f32[1,128,256]{2,1,0:T(8,128)S(1)}, f32[1,128,256]{2,1,0:T(8,128)}, u32[]{:S(2)}) copy-start(f32[1,128,256]{2,1,0:T(8,128)} %get-tuple-element.95) | copy-start | bytes 393220
  611.4 8.4 %copy-start.25 = (f32[1,128,256]{2,1,0:T(8,128)S(1)}, f32[1,128,256]{2,1,0:T(8,128)}, u32[]{:S(2)}) copy-start(f32[1,128,256]{2,1,0:T(8,128)} %get-tuple-element.96) | copy-start | bytes 393220
  611.4 9.1 %copy-start.24 = (f32[1,128,256]{2,1,0:T(8,128)S(1)}, f32[1,128,256]{2,1,0:T(8,128)}, u32[]{:S(2)}) copy-start(f32[1,128,256]{2,1,0:T(8,128)} %get-tuple-element.97) | copy-start | bytes 393220
  611.5 9.7 %copy-start.23 = (f32[1,128,256]{2,1,0:T(8,128)S(1)}, f32[1,128,256]{2,1,0:T(8,128)}, u32[]{:S(2)}) copy-start(f32[1,128,256]{2,1,0:T(8,128)} %get-tuple-element.98) | copy-start | bytes 393220
  611.5 10.4 %copy-start.22 = (f32[1,128,256]{2,1,0:T(8,128)S(1)}, f32[1,128,256]{2,1,0:T(8,128)}, u32[]{:S(2)}) copy-start(f32[1,128,256]{2,1,0:T(8,128)} %get-tuple-element.99) | copy-start | bytes 393220
  615.4 7.1 %copy-start.21 = (f32[4,128,256]{2,1,0:T(8,128)S(1)}, f32[4,128,256]{2,1,0:T(8,128)}, u32[]{:S(2)}) copy-start(f32[4,128,256]{2,1,0:T(8,128)} %get-tuple-element.101) | copy-start | bytes 1572868
  (25 other events, 62.0 us)
Sparse Core Ops, SparseCore 0:
  10.9 109.2 all-gather.4
  123.1 84.3 all-gather.6
  310.0 159.6 reduce-scatter.1

commit v7 on v6

--- a/solution.py
+++ b/solution.py
@@ -618,50 +618,73 @@
             for at, (source, target) in enumerate(pairs)
         ]
 
-    def start(self, device, pairs, condition, semaphore):
-        copies = self.copies(device, pairs, semaphore, self.sent)
-        self.sent += len(copies)
-        when(condition, lambda: [copy.start() for copy in copies] and None)
-        self.started.append((condition, copies))
-        return condition, copies
+    def start(self, device, pairs, wide, condition, semaphore):
+        send = self.sent
+        self.sent += wide
+
+        def make():
+            return self.copies(device(), pairs(), semaphore, send)
+
+        when(condition(), lambda: [copy.start() for copy in make()] and None)
+        self.started.append((condition, make))
+        return condition, make
 
     def arrive(self, sent):
-        condition, copies = sent
-        when(condition, lambda: [copy.wait_recv() for copy in copies] and None)
+        condition, make = sent
+        when(condition(), lambda: [copy.wait_recv() for copy in make()] and None)
 
     def stages(self):
         place, along = self.place, self.place.along
         done = []
+
+        def always():
+            return None
+
+        def width(axes):
+            return 2 if "x" in axes else 1
+
         for axis in self.before:
-            sent = self.start(place.across(axis), self.pairs(done, place.z, not done), None, self.semaphore())
+            axes = tuple(done)
+            sent = self.start(
+                lambda axis=axis: place.across(axis), lambda axes=axes: self.pairs(axes, place.z, not axes),
+                width(axes), always, self.semaphore())
             yield
             self.arrive(sent)
             done.append(axis)
         first = not done
+        axes_z = tuple(done)
         from_left = [self.semaphore() for _ in range(along - 1)]
         from_right = [self.semaphore() for _ in range(along - 1)]
 
         def pass_on(turn, step):
-            axes = done + list(self.after[:turn])
-            device = place.across(self.after[turn])
-            if step == 0:
-                return turn, step, [self.start(device, self.pairs(axes, place.z, not axes), None, self.semaphore())]
-            return turn, step, [
-                self.start(device, self.pairs(axes, z, False), (z >= 0) & (z < along), self.semaphore())
-                for z in (place.z - step, place.z + step)
-            ]
+            axes = axes_z + tuple(self.after[:turn])
+            sent = []
+            for way in ((-1, 1) if step else (0,)):
+
+                def inside(way=way):
+                    z = place.z + way * step
+                    return (z >= 0) & (z < along) if way else None
+
+                sent.append(self.start(
+                    lambda: place.across(self.after[turn]),
+                    lambda way=way: self.pairs(axes, place.z + way * step, not axes and not step),
+                    width(axes), inside, self.semaphore()))
+            return turn, step, sent
 
         def step_out(step):
-            left, right = place.z - (step - 1), place.z + (step - 1)
-            self.start(place.device(dz=1), self.pairs(done, left, first and step == 1),
-                       (left >= 0) & (place.z + 1 < along), from_left[step - 1])
-            self.start(place.device(dz=-1), self.pairs(done, right, first and step == 1),
-                       (right < along) & (place.z > 0), from_right[step - 1])
+            self.start(
+                lambda: place.device(dz=1), lambda: self.pairs(axes_z, place.z - (step - 1), first and step == 1),
+                width(axes_z), lambda: (place.z - (step - 1) >= 0) & (place.z + 1 < along), from_left[step - 1])
+            self.start(
+                lambda: place.device(dz=-1), lambda: self.pairs(axes_z, place.z + (step - 1), first and step == 1),
+                width(axes_z), lambda: (place.z + (step - 1) < along) & (place.z > 0), from_right[step - 1])
 
         def step_in(step):
-            for z, semaphore in ((place.z - step, from_left), (place.z + step, from_right)):
-                copies = self.copies(place.across("k"), self.pairs(done, z, False), semaphore[step - 1])
-                self.arrive(((z >= 0) & (z < along), copies))
+            for way, semaphore in ((-1, from_left), (1, from_right)):
+                z = place.z + way * step
+                self.arrive((
+                    lambda: (z >= 0) & (z < along),
+                    lambda: self.copies(place.across("k"), self.pairs(axes_z, z, False), semaphore[step - 1])))
 
         step_out(1)
         waiting = [pass_on(0, 0)] if self.after else []
@@ -680,35 +703,57 @@
             if self.after and step < along:
                 following.append(pass_on(0, step))
             waiting = following
-        everything = [self.region(slice(None), slice(None), x) for x in range(2)]
-        sent = self.start(place.across("k"), [(r, r) for r in everything], None, self.semaphore())
+        sent = self.start(
+            lambda: place.across("k"), lambda: [(r, r) for r in [self.region(slice(None), slice(None), x) for x in range(2)]],
+            2, always, self.semaphore())
         yield
         self.arrive(sent)
 
     def finish(self):
-        for condition, copies in self.started:
-            when(condition, lambda copies=copies: [copy.wait_send() for copy in copies] and None)
-
-
-def gather_kernel(units, count, *refs):
-    blocks, fulls = refs[:count], refs[count : 2 * count]
-    send, recv, local_sem = refs[2 * count :]
-    place = Place()
-    place.greet()
-    own = []
-    for at, (block, full) in enumerate(zip(blocks, fulls)):
-        width = block.shape[-1]
-        columns = pl.ds(pl.multiple_of((place.x * 2 + place.k) * width, 128), width)
-        copy = pltpu.make_async_copy(block, full.at[place.z, place.y, :, :, columns], local_sem.at[at])
-        copy.start()
-        own.append(copy)
-    gathers = [
+        for condition, make in self.started:
+            when(condition(), lambda make=make: [copy.wait_send() for copy in make()] and None)
+
+
+class OwnBlocks:
+    def __init__(self, place, blocks, fulls, local):
+        self.place, self.blocks, self.fulls, self.local = place, blocks, fulls, local
+
+    def copies(self):
+        place = self.place
+        for at, (block, full) in enumerate(zip(self.blocks, self.fulls)):
+            width = block.shape[-1]
+            columns = pl.ds(pl.multiple_of((place.x * 2 + place.k) * width, 128), width)
+            yield pltpu.make_async_copy(block, full.at[place.z, place.y, :, :, columns], self.local.at[at])
+
+    def start(self):
+        for copy in self.copies():
+            copy.start()
+
+    def wait(self):
+        for copy in self.copies():
+            copy.wait()
+
+
+def gathers_of(place, units, blocks, fulls, send, recv):
+    return [
         Gather(place, blocks[which], fulls[which], strip, order, send.at[at], recv.at[at])
         for at, (which, strip, order) in enumerate(units)
     ]
+
+
+def gather_kernel(units, count, *refs):
+    blocks, fulls = refs[:count], refs[count : 2 * count]
+    send, recv, local = refs[2 * count :]
+    place = Place()
+    place.greet()
+    own = OwnBlocks(place, blocks, fulls, local)
+    own.start()
+    gathers = gathers_of(place, units, blocks, fulls, send, recv)
+    waited = False
     for unused in in_turn([gather.stages() for gather in gathers], 0.0):
-        while own:
-            own.pop().wait()
+        if not waited:
+            own.wait()
+            waited = True
     for gather in gathers:
         gather.finish()
 
@@ -723,26 +768,30 @@
     return [strip + (orders[at % len(orders)],) for at, strip in enumerate(strips)]
 
 
+def gather_plan(blocks, least, orders):
+    along, cols = lax.axis_size("row") // 2, lax.axis_size("col")
+    units = gather_units(blocks, least, orders)
+    fulls = [jax.ShapeDtypeStruct((along, 2) + b.shape[:2] + (cols * b.shape[2],), b.dtype) for b in blocks]
+    scratch = [
+        pltpu.SemaphoreType.DMA((len(units), 8 * along)),
+        pltpu.SemaphoreType.DMA((len(units), 12 * along)),
+        pltpu.SemaphoreType.DMA((len(blocks),)),
+    ]
+    return fulls, units, scratch
+
+
 def gather_blocks(blocks, collective_id, least):
-    along, cols = lax.axis_size("row") // 2, lax.axis_size("col")
-    units = gather_units(blocks, least, ORDERS)
+    fulls, units, scratch = gather_plan(blocks, least, ORDERS)
     count = len(blocks)
     anywhere = pl.BlockSpec(memory_space=pl.ANY)
-    moved = sum(block.size for block in blocks) * 2 * along * 2 * cols
     return pl.pallas_call(
         functools.partial(gather_kernel, units, count),
-        out_shape=[
-            jax.ShapeDtypeStruct((along, 2) + b.shape[:2] + (cols * b.shape[2],), b.dtype) for b in blocks
-        ],
+        out_shape=fulls,
         in_specs=[anywhere] * count,
         out_specs=[anywhere] * count,
-        scratch_shapes=[
-            pltpu.SemaphoreType.DMA((len(units), 8 * along)),
-            pltpu.SemaphoreType.DMA((len(units), 12 * along)),
-            pltpu.SemaphoreType.DMA((count,)),
-        ],
+        scratch_shapes=scratch,
         compiler_params=pltpu.CompilerParams(collective_id=collective_id, has_side_effects=True),
-        cost_estimate=pl.CostEstimate(flops=0, bytes_accessed=2 * moved, transcendentals=0),
+        cost_estimate=pl.CostEstimate(flops=0, bytes_accessed=4 * sum(f.size for f in fulls), transcendentals=0),
     )(*blocks)
 
 
@@ -943,6 +992,9 @@
         cost_estimate=pl.CostEstimate(
             flops=sum(g.size for g in grads), bytes_accessed=4 * sum(g.size for g in grads), transcendentals=0),
     )(*grads)
+
+
+ACROSS = ("yzx", "yzx", "yzx", "yzx", "yxz")
 
 
 def attend_rows(q, key_ref, value_ref, spans, diagonal, put):
@@ -979,11 +1031,19 @@
         preferred_element_type=jnp.float32)
 
 
-def pair_attend_kernel(tile, q_ref, k_ref, v_ref, q_any, k_any, v_any, mix_ref, logs_ref, fq_out, fk_out, fv_out,
-                       near, near_logs, far_q, far_k, far_v, far, far_logs, got, far_rows, got_rows,
-                       send, recv, local, keep):
+def pair_attend_kernel(tile, units, count, events, *refs):
+    q_ref, k_ref, v_ref, q_any, k_any, v_any = refs[:6]
+    blocks = refs[6 : 6 + count]
+    mix_ref, logs_ref, fq_out, fk_out, fv_out = refs[6 + count : 11 + count]
+    fulls = refs[11 + count : 11 + 2 * count]
+    (near, near_logs, far_q, far_k, far_v, far, far_logs, got, far_rows, got_rows,
+     send, recv, local, keep) = refs[11 + 2 * count : 25 + 2 * count]
+    gather_send, gather_recv, gather_local = refs[25 + 2 * count :]
     step = pl.program_id(0)
     place = Place()
+    own = OwnBlocks(place, blocks, fulls, gather_local)
+    gathers = gathers_of(place, units, blocks, fulls, gather_send, gather_recv)
+    turns = in_turn([gather.stages() for gather in gathers], 0.25)
     pairs = near.shape[0]
     fars = pairs // 2
     rows = q_ref.shape[0]
@@ -1022,9 +1082,8 @@
 
     @pl.when(step == 0)
     def _():
-        barrier = pltpu.get_barrier_semaphore()
-        pl.semaphore_signal(barrier, inc=1, device_id=partner, device_id_type=MESH)
-        pl.semaphore_wait(barrier, 1)
+        place.greet()
+        own.start()
         near_logs[...] = jnp.zeros_like(near_logs)
         far_logs[...] = jnp.zeros_like(far_logs)
         for j in range(fars):
@@ -1046,6 +1105,15 @@
                     sending(which, j - 1).wait_send()
 
                 sending(which, j).start()
+
+    for at, number in enumerate(events):
+
+        @pl.when(step == at)
+        def _(at=at, number=number):
+            if at == 0:
+                own.wait()
+            for unused in range(number):
+                next(turns, None)
 
     @pl.when(step < pairs)
     def _():
@@ -1135,9 +1203,13 @@
 
         for which in range(3):
             saving(which).wait()
-
-
-def pair_attend(q, k, v, collective_id, tile=384):
+        for unused in turns:
+            pass
+        for gather in gathers:
+            gather.finish()
+
+
+def pair_attend(q, k, v, blocks, collective_id, events, tile=384):
     rows, width = q.shape
     pairs = width // 128
     fars = pairs // 2
@@ -1145,25 +1217,28 @@
     anywhere = pl.BlockSpec(memory_space=pl.ANY)
     kept = jax.ShapeDtypeStruct((fars, rows, 128), jnp.bfloat16)
     half = pltpu.VMEM((fars, rows, 128), jnp.bfloat16)
-    return pl.pallas_call(
-        functools.partial(pair_attend_kernel, tile),
+    fulls, units, scratch = gather_plan(blocks, 256, ACROSS)
+    count = len(blocks)
+    result = pl.pallas_call(
+        functools.partial(pair_attend_kernel, tile, units, count, events),
         grid=(pairs + fars + 1,),
-        in_specs=[block] * 3 + [anywhere] * 3,
-        out_specs=[pl.BlockSpec((rows, width), lambda i: (0, 0)), pl.BlockSpec((rows, 128), lambda i: (0, 0))] + [anywhere] * 3,
+        in_specs=[block] * 3 + [anywhere] * (3 + count),
+        out_specs=[pl.BlockSpec((rows, width), lambda i: (0, 0)), pl.BlockSpec((rows, 128), lambda i: (0, 0))] + [anywhere] * (3 + count),
         out_shape=[
-            jax.ShapeDtypeStruct((rows, width), jnp.bfloat16), jax.ShapeDtypeStruct((rows, 128), jnp.float32), kept, kept, kept],
+            jax.ShapeDtypeStruct((rows, width), jnp.bfloat16), jax.ShapeDtypeStruct((rows, 128), jnp.float32), kept, kept, kept, *fulls],
         scratch_shapes=[
             pltpu.VMEM((pairs, rows, 128), jnp.float32), pltpu.VMEM((rows, 128), jnp.float32),
             half, half, half, half, pltpu.VMEM((rows, 128), jnp.float32), half,
             pltpu.VMEM((8, rows), jnp.float32), pltpu.VMEM((8, rows), jnp.float32),
             pltpu.SemaphoreType.DMA((5, fars)), pltpu.SemaphoreType.DMA((5, fars)),
-            pltpu.SemaphoreType.DMA((3, fars)), pltpu.SemaphoreType.DMA((3,)),
+            pltpu.SemaphoreType.DMA((3, fars)), pltpu.SemaphoreType.DMA((3,)), *scratch,
         ],
         compiler_params=pltpu.CompilerParams(
             collective_id=collective_id, has_side_effects=True, vmem_limit_bytes=48 << 20),
         cost_estimate=pl.CostEstimate(
             flops=4 * rows * rows * width, bytes_accessed=16 * rows * width, transcendentals=rows * rows * pairs * 2),
-    )(q, k, v, q, k, v)
+    )(q, k, v, q, k, v, *blocks)
+    return result[:5], result[5:]
 
 
 def back_pair(tile, causal, q_ref, k_ref, v_ref, do_ref, stats, acc, put):
@@ -1490,10 +1565,8 @@
         return array.reshape(-1, array.shape[-1])
 
     early = gather_blocks(
-        [small(self_query), small(self_key), small(self_value), gains, small(self_output), small(cross_query),
-         small(cross_key), small(cross_value), small(cross_output)], 1, 128)
+        [small(self_query), small(self_key), small(self_value), gains], 1, 128)
     query_self, key_self, value_self = [flat(w) for w in early[:3]]
-    out_self, query_cross, key_cross, value_cross, out_cross = [flat(w) for w in early[4:]]
     norm_params = early[3].reshape(pairs * 2, 16, -1, 128)[:, :6, :, :piece].transpose(1, 0, 2, 3)
     norm_params = norm_params.reshape(6, width).astype(jnp.float32)
 
@@ -1502,7 +1575,10 @@
     self_k = matmul(hidden_one, key_self).astype(jnp.bfloat16)
     self_v = matmul(hidden_one, value_self).astype(jnp.bfloat16)
     self_q = matmul(hidden_one, query_self).astype(jnp.bfloat16)
-    self_mix, log_lanes, far_q, far_k, far_v = pair_attend(self_q, self_k, self_v, 5)
+    (self_mix, log_lanes, far_q, far_k, far_v), late = pair_attend(
+        self_q, self_k, self_v, [small(w) for w in (self_output, cross_query, cross_key, cross_value, cross_output)],
+        5, [3] * 12)
+    out_self, query_cross, key_cross, value_cross, out_cross = [flat(w) for w in late]
     resid_one = frames + matmul(self_mix, out_self)
     hidden_two = norm_forward(resid_one, norm_params[2], norm_params[3]).astype(jnp.bfloat16)
     cross_q = matmul(hidden_two, query_cross).astype(jnp.bfloat16)

time: 638 us -> 612 us (0.959)
  Pallas kernels: 500 us -> 472 us
    pallas_call x1, Pallas kernels: 138 us -> 58.6 us  [gather_blocks(): pl.pallas_call(functools.partial(gather_kernel, units, count), out_shape=...]
    pallas_call x1, Pallas kernels: 69.9 us -> 119 us  [pair_attend(): pl.pallas_call(functools.partial(pair_attend_kernel, tile, units, count,...]
    unnamed x103 -> x111, local copies, waits for them, and re-layouts: 13.2 us -> 13.2 us
  transfers between devices with their start and end apart: 5 -> 5, of which waited for: 0 -> 0; matrix products, arithmetic and copies ran while one was open for 14% -> 16% of each run, Pallas kernels for 72% -> 70%
where the time goes in v7:
time: 612 us; the launch traced here: 605 us
  Pallas kernels  472 us (77%)
  matrix products  68.8 us (11%)
  other arithmetic  21.3 us (3%)
  local copies, waits for them, and re-layouts  18.7 us (3%)
  between operations  14.8 us (2%)
  starting transfers between devices  7.94 us (1%)
    pallas_call x1, Pallas kernels, pair_back(): pl.pallas_call(functools.partial(pair_back_kernel, tile, far_tile, units,...  167 us
    pallas_call x1, Pallas kernels, pair_attend(): pl.pallas_call(functools.partial(pair_attend_kernel, tile, units, count,...  119 us
    pallas_call x1, Pallas kernels, gather_blocks(): pl.pallas_call(functools.partial(gather_kernel, units, count), out_shape=...  58.6 us
    pallas_call x1, Pallas kernels, feed(): pl.pallas_call(feed_kernel, grid=(ff // chunk,), in_specs=[whole, whole,...  49.1 us
    pallas_call x1, Pallas kernels, scatter_blocks(): pl.pallas_call(functools.partial(scatter_kernel, units, count), out_shape...  47.9 us
    dot_general x8, matrix products, over_tokens(): lax.dot_general(left, right, (((0,), (0,)), ((), ())), preferred_element_...  26 us
    dot_general x8, matrix products, by_transposed(): lax.dot_general(left, right, (((1,), (1,)), ((), ())), preferred_element_...  22.1 us
    dot_general x8, matrix products, matmul(): return jnp.dot(left, right, preferred_element_type=jnp.float32)  20.7 us
  transfers between devices with their start and end apart: 5, of which 0 were waited for; matrix products, arithmetic and copies ran while one was open for 16% of the time, Pallas kernels for 70%

profile of v7, /device:TPU:0, one launch (start us, length us, event | category | flops | bytes accessed | tf_op | source)
XLA Modules:
  0.0 605.1 jit_solution(6105169940493875473)
XLA Ops:
  8.7 3.0 collective-permute-start
  13.1 58.6 %shard_map.330 = (bf16[4,2,1,128,1024]{4,3,2,1,0:T(8,128)(2,1)}, bf16[4,2,1,128,1024]{4,3,2,1,0:T(8,128)(2,1)}, bf16[4,2,1,128,1024]{4,3,2,1,0:T(8,128)(2,1)}, bf16[4,2,1,16,512]{4,3,2,1,0:T(8,128)(2,1)}) custom-call(bf16[1,128,256]{2,1,0:T(8,128)(2,1)} %bitcast.141, bf16[1,128,256]{2,1,0:T(8,128)(2,1)} %bitcast.142, bf16[1,128,256]{2,1,0:T(8,128)(2,1)} %bitcast.143, ...), custom_call_target="tpu_custom_call" | custom-call | bytes 12845056 | tf_op jit(solution)/shard_map/pallas_call | solution.py:787
  78.5 3.0 convolution_convert_fusion.11.refs_2_.refs_5_
  83.4 119.2 %shard_map.331 = (bf16[750,1024]{1,0:T(8,128)(2,1)S(1)}, f32[750,128]{1,0:T(8,128)S(1)}, bf16[4,750,128]{2,1,0:T(8,128)(2,1)S(1)}, bf16[4,750,128]{2,1,0:T(8,128...) custom-call(bf16[750,1024]{1,0:T(8,128)(2,1)S(1)} %convolution_conve, ...), custom_call_target="tpu_custom_call" | custom-call | flops 2304000000 | bytes 12288000 | tf_op jit(solution)/shard_map/pallas_call | solution.py:1222
  202.6 4.9 fusion.35
  216.7 11.4 %shard_map.332 = (bf16[750,1024]{1,0:T(8,128)(2,1)S(1)}, f32[750,128]{1,0:T(8,128)S(1)}) custom-call(bf16[750,1024]{1,0:T(8,128)(2,1)S(1)} %convolution_convert_fusion.10.q_ref, bf16[64,1024]{1,0:T(8,128)(2,1)S(1)} %convolution_convert_fusion.15.k_ref, bf16[64,1024]{1,0:T(8,128)(2,1)S(1)} %convolution_convert_fusion.14.v_ref), custom_call_target="tpu_custom_call" | custom-call | flops 196608000 | bytes 6144000 | tf_op jit(solution)/shard_map/pallas_call | solution.py:484
  233.3 49.1 %shard_map.333 = (bf16[750,1024]{1,0:T(8,128)(2,1)}, f32[750,1024]{1,0:T(8,128)}, bf16[8,4,128,1024]{3,2,1,0:T(8,128)(2,1)}, bf16[4096,1024]{1,0:T(8,128)(2,1)}) custom-call(bf16[750,1024]{1,0:T(8,128)(2,1)} %add_convert_fusion.h_ref, bf16[750,1024]{1,0:T(8,128)(2,1)} %cot_ref.1, f32[750,1024]{1,0:T(8,128)} %copy-done.14, ...), custom_call_target="tpu_custom_call" | custom-call | flops 37748736000 | bytes 45842432 | tf_op jit(solution)/shard_map/pallas_call | solution.py:523
  282.4 4.0 multiply_reduce_fusion
  291.9 19.5 %shard_map.334 = (bf16[750,1024]{1,0:T(8,128)(2,1)S(1)}, bf16[64,1024]{1,0:T(8,128)(2,1)S(1)}, bf16[64,1024]{1,0:T(8,128)(2,1)S(1)}) custom-call(bf16[750,1024]{1,0:T(8,128)(2,1)S(1)} %convolution_convert_fusion.10.q_ref, bf16[64,1024]{1,0:T(8,128)(2,1)S(1)} %convolution_convert_fusion.15.k_ref, bf16[64,1024]{1,0:T(8,128)(2,1)S(1)} %convolution_convert_fusion.14.v_ref, ...), custom_call_target="tpu_custom_call" | custom-call | flops 491520000 | bytes 7680000 | tf_op jit(solution)/shard_map/pallas_call | solution.py:1303
  311.5 4.8 collective-permute-start.1
  321.1 3.2 convolution_convert_fusion.7
  324.3 3.0 convolution_convert_fusion.8.refs_3_.refs_6_
  327.3 3.4 convolution_convert_fusion.6
  330.7 3.2 convolution_convert_fusion.5
  338.5 166.5 %shard_map.335 = (bf16[750,1024]{1,0:T(8,128)(2,1)}, bf16[750,1024]{1,0:T(8,128)(2,1)}, bf16[750,1024]{1,0:T(8,128)(2,1)}, f32[1,128,256]{2,1,0:T(8,128)}, f32[1...) custom-call(bf16[750,1024]{1,0:T(8,128)(2,1)} %copy-done, ...), custom_call_target="tpu_custom_call" | custom-call | flops 5760000000 | bytes 12288000 | tf_op jit(solution)/shard_map/pallas_call | solution.py:1506
  505.0 4.0 fusion.37
  511.6 3.9 fusion.31
  515.5 3.3 fusion.8
  519.8 5.1 convolution_convert_fusion.4
  524.9 3.4 convolution_convert_fusion.2
  528.3 3.4 convolution_convert_fusion.3
  531.8 47.9 %shard_map.336 = (f32[1,128,256]{2,1,0:T(8,128)}, f32[1,128,256]{2,1,0:T(8,128)}, f32[1,128,256]{2,1,0:T(8,128)}, f32[1,16,128]{2,1,0:T(8,128)}) custom-call(bf16[4,2,1,128,1024]{4,3,2,1,0:T(8,128)(2,1)} %bitcast.128, bf16[4,2,1,128,1024]{4,3,2,1,0:T(8,128)(2,1)} %bitcast.130, bf16[4,2,1,128,1024]{4,3,2,1,0:T(8,128)(2,1)} %bitcast.129, ...), custom_call_target="tpu_custom_call" | custom-call | flops 3211264 | bytes 12845056 | tf_op jit(solution)/shard_map/pallas_call | solution.py:984
  583.4 3.0 convolution_add_fusion.1
  586.5 3.9 add_add_fusion.3
  (180 shorter events, 55.6 us)
Async XLA Ops:
  7.2 67.7 %copy-start.16 = (bf16[750,1024]{1,0:T(8,128)(2,1)S(1)}, bf16[750,1024]{1,0:T(8,128)(2,1)}, u32[]{:S(2)}) copy-start(bf16[750,1024]{1,0:T(8,128)(2,1)} %param.21) | copy-start | bytes 4608004
  7.2 226.1 %all-gather.5.cloned.1.call-start = ((), (), s32[]{:S(2)}) async-start(), calls=%async_computation.2 | async-start | bytes 8650752 | tf_op jit(solution)/shard_map/all_gather | solution.py:1558
  7.9 225.4 %all-gather.7.cloned.1.call-start = ((), (), s32[]{:S(2)}) async-start(), calls=%async_computation.3 | async-start | bytes 8650752 | tf_op jit(solution)/shard_map/all_gather | solution.py:1559
  8.7 581.7 %reduce-scatter.2.cloned.1.call-start = ((), (), s32[]{:S(2)}) async-start(), calls=%async_computation.1 | async-start | bytes 8650752 | tf_op jit(solution)/shard_map/reduce_scatter | solution.py:1595
  8.7 203.6 %collective-permute-start = (bf16[32,1024]{1,0:T(8,128)(2,1)}, bf16[32,1024]{1,0:T(8,128)(2,1)S(1)}, u32[]{:S(2)}, u32[]{:S(2)}) collective-permute-start(bf16[32,1024]{1,0:T(8,128)(2,1)} %param.22), channel_id=1, source_target_pairs={{0,4},{8,12},{16,20},{24,28},{4,0},{12,8},{20,16},{28,24},{1,5},{9... | collective-permute-start | bytes 196616 | tf_op jit(solution)/shard_map/ppermute | solution.py:1585
  83.3 119.2 %copy-start = (bf16[750,1024]{1,0:T(8,128)(2,1)}, bf16[750,1024]{1,0:T(8,128)(2,1)S(1)}, u32[]{:S(2)}) copy-start(bf16[750,1024]{1,0:T(8,128)(2,1)S(1)} %convolution_convert_fusion.13.refs_0_.refs_3_) | copy-start | bytes 4608004
  202.6 5.0 copy-start.1
  202.6 5.0 copy-start.3
  212.4 15.8 %copy-start.21 = (f32[750,1024]{1,0:T(8,128)S(1)}, f32[750,1024]{1,0:T(8,128)}, u32[]{:S(2)}) copy-start(f32[750,1024]{1,0:T(8,128)} %copy-done.20) | copy-start | bytes 9216004
  212.4 15.8 %copy-start.46 = (bf16[4,2,1,128,1024]{4,3,2,1,0:T(8,128)(2,1)S(1)}, bf16[4,2,1,128,1024]{4,3,2,1,0:T(8,128)(2,1)}, u32[]{:S(2)}) copy-start(bf16[4,2,1,128,1024]{4,3,2,1,0:T(8,128)(2,1)} %get-tuple-element.77) | copy-start | bytes 6291460
  291.9 24.4 %copy-start.22 = (f32[750,1024]{1,0:T(8,128)S(1)}, f32[750,1024]{1,0:T(8,128)}, u32[]{:S(2)}) copy-start(f32[750,1024]{1,0:T(8,128)} %copy-done.20) | copy-start | bytes 9216004
  291.9 24.4 %copy-start.45 = (bf16[4,2,1,128,1024]{4,3,2,1,0:T(8,128)(2,1)S(1)}, bf16[4,2,1,128,1024]{4,3,2,1,0:T(8,128)(2,1)}, u32[]{:S(2)}) copy-start(bf16[4,2,1,128,1024]{4,3,2,1,0:T(8,128)(2,1)} %get-tuple-element.73) | copy-start | bytes 6291460
  311.5 22.8 %collective-permute-start.1 = (bf16[32,2048]{1,0:T(8,128)(2,1)S(1)}, bf16[32,2048]{1,0:T(8,128)(2,1)S(1)}, u32[]{:S(2)}, u32[]{:S(2)}) collective-permute-start(bf16[32,2048]{1,0:T(8,128)(2,1)S(1)} %broadcast_select_fusion), channel_id=1, source_target_pairs={{0,4},{8,12},{16,20},{24,28},{4,0},{12,8},{20,16},{28,24},{1,5},{9... | collective-permute-start | bytes 393224 | tf_op jit(solution)/shard_map/ppermute | solution.py:1607
  519.8 5.1 copy-start.42
  579.7 6.8 %copy-start.19 = (f32[750,1024]{1,0:T(8,128)S(1)}, f32[750,1024]{1,0:T(8,128)}, u32[]{:S(2)}) copy-start(f32[750,1024]{1,0:T(8,128)} %copy-done.18) | copy-start | bytes 9216004
  586.4 5.8 copy-start.34
  586.4 6.5 %copy-start.33 = (f32[1,128,256]{2,1,0:T(8,128)S(1)}, f32[1,128,256]{2,1,0:T(8,128)}, u32[]{:S(2)}) copy-start(f32[1,128,256]{2,1,0:T(8,128)} %get-tuple-element.93) | copy-start | bytes 393220
  586.4 7.1 %copy-start.32 = (f32[1,128,256]{2,1,0:T(8,128)S(1)}, f32[1,128,256]{2,1,0:T(8,128)}, u32[]{:S(2)}) copy-start(f32[1,128,256]{2,1,0:T(8,128)} %get-tuple-element.94) | copy-start | bytes 393220
  586.4 7.8 %copy-start.31 = (f32[1,128,256]{2,1,0:T(8,128)S(1)}, f32[1,128,256]{2,1,0:T(8,128)}, u32[]{:S(2)}) copy-start(f32[1,128,256]{2,1,0:T(8,128)} %get-tuple-element.95) | copy-start | bytes 393220
  586.4 8.4 %copy-start.30 = (f32[1,128,256]{2,1,0:T(8,128)S(1)}, f32[1,128,256]{2,1,0:T(8,128)}, u32[]{:S(2)}) copy-start(f32[1,128,256]{2,1,0:T(8,128)} %get-tuple-element.96) | copy-start | bytes 393220
  586.4 9.1 %copy-start.29 = (f32[1,128,256]{2,1,0:T(8,128)S(1)}, f32[1,128,256]{2,1,0:T(8,128)}, u32[]{:S(2)}) copy-start(f32[1,128,256]{2,1,0:T(8,128)} %get-tuple-element.97) | copy-start | bytes 393220
  586.5 9.7 %copy-start.28 = (f32[1,128,256]{2,1,0:T(8,128)S(1)}, f32[1,128,256]{2,1,0:T(8,128)}, u32[]{:S(2)}) copy-start(f32[1,128,256]{2,1,0:T(8,128)} %get-tuple-element.98) | copy-start | bytes 393220
  586.5 10.4 %copy-start.27 = (f32[1,128,256]{2,1,0:T(8,128)S(1)}, f32[1,128,256]{2,1,0:T(8,128)}, u32[]{:S(2)}) copy-start(f32[1,128,256]{2,1,0:T(8,128)} %get-tuple-element.99) | copy-start | bytes 393220
  590.4 7.1 %copy-start.26 = (f32[4,128,256]{2,1,0:T(8,128)S(1)}, f32[4,128,256]{2,1,0:T(8,128)}, u32[]{:S(2)}) copy-start(f32[4,128,256]{2,1,0:T(8,128)} %get-tuple-element.101) | copy-start | bytes 1572868
  (29 other events, 81.3 us)
Sparse Core Ops, SparseCore 0:
  10.9 86.3 all-gather.4
  100.2 91.2 all-gather.6
  282.5 161.2 reduce-scatter.1

commit v8 on v7

--- a/solution.py
+++ b/solution.py
@@ -439,55 +439,6 @@
 NT=(((1,),(1,)),((),())); NN=(((1,),(0,)),((),())); TN=(((0,),(0,)),((),()))
 def dg(a,b,dims): return lax.dot_general(a,b,dims,preferred_element_type=jnp.float32)
 
-def attend_kernel(causal,tile,q_ref,k_ref,v_ref,o_ref,lse_ref):
-    pair=pl.program_id(0)
-    rows=q_ref.shape[0]
-    low=lax.broadcasted_iota(jnp.int32,(1,128),1)<HEAD_DIM
-    lane=lax.broadcasted_iota(jnp.int32,(1,128),1)
-    value=v_ref[...]
-    ones=jnp.ones_like(value)
-    @pl.when(pair==0)
-    def _(): lse_ref[...]=jnp.zeros_like(lse_ref)
-    for start in range(0,rows,tile):
-        n=min(tile,rows-start)
-        q=q_ref[start:start+n,:]*jnp.bfloat16(HEAD_DIM**-0.5)
-        mixed=[]; sums=[]
-        lse=lse_ref[start:start+n,:]
-        for h in range(2):
-            mine=low if h==0 else jnp.logical_not(low)
-            qh=jnp.where(mine,q,jnp.bfloat16(0))
-            vh=jnp.where(mine,value,ones)
-            if causal:
-                spans=([(0,start)] if start else [])+[(start,n)]
-            else: spans=[(0,k_ref.shape[0])]
-            scores=[]
-            for at,length in spans:
-                s=dg(qh,k_ref[at:at+length,:],NT)
-                if causal and at==start:
-                    ok=lax.broadcasted_iota(jnp.int32,s.shape,0)>=lax.broadcasted_iota(jnp.int32,s.shape,1)
-                    s=jnp.where(ok,s,-1e30)
-                scores.append(s)
-            top=functools.reduce(jnp.maximum,[jnp.max(s,axis=1,keepdims=True) for s in scores])
-            out=None
-            for (at,length),s in zip(spans,scores):
-                p=jnp.exp(s-top).astype(jnp.bfloat16)
-                part=dg(p,vh[at:at+length,:],NN)
-                out=part if out is None else out+part
-            total=out[:,HEAD_DIM:HEAD_DIM+1] if h==0 else out[:,0:1]
-            mixed.append(out/total)
-            lse=jnp.where(lane==2*pair+h,top+jnp.log(total),lse)
-        lse_ref[start:start+n,:]=lse
-        o_ref[start:start+n,:]=jnp.where(low,mixed[0],mixed[1]).astype(o_ref.dtype)
-
-def attend(q,k,v,causal,out_dtype,tile=256):
-    rows,width=q.shape; keys=k.shape[0]
-    return pl.pallas_call(functools.partial(attend_kernel,causal,tile),grid=(width//128,),
-        in_specs=[pl.BlockSpec((rows,128),lambda i:(0,i)),pl.BlockSpec((keys,128),lambda i:(0,i)),pl.BlockSpec((keys,128),lambda i:(0,i))],
-        out_specs=[pl.BlockSpec((rows,128),lambda i:(0,i)),pl.BlockSpec((rows,128),lambda i:(0,0))],
-        out_shape=[jax.ShapeDtypeStruct((rows,width),out_dtype),jax.ShapeDtypeStruct((rows,128),jnp.float32)],
-        compiler_params=pltpu.CompilerParams(vmem_limit_bytes=40<<20),
-        cost_estimate=pl.CostEstimate(flops=4*rows*keys*width,bytes_accessed=8*rows*width,transcendentals=rows*keys*width//64))(q,k,v)
-
 def feed_kernel(h_ref,cot_ref,res_ref,up_ref,down_ref,out_ref,g_ref,dup_ref,ddown_ref,acc):
     i=pl.program_id(0)
     @pl.when(i==0)
@@ -960,7 +911,7 @@
     place = Place()
     place.greet()
     scatters = scatters_of(place, units, grads, outs, *refs[2 * count : 2 * count + 3], refs[2 * count + 3 :])
-    for unused in in_turn([scatter.stages() for scatter in scatters], 0.5):
+    for unused in in_turn([scatter.stages() for scatter in scatters], 0.25):
         pass
     for scatter in scatters:
         scatter.finish()
@@ -978,7 +929,7 @@
 
 
 def scatter_blocks(grads, collective_id, least):
-    blocks, units, scratch = scatter_plan(grads, least, ORDERS)
+    blocks, units, scratch = scatter_plan(grads, least, ("xyz", "yxz", "zxy", "zyx", "xzy", "yzx"))
     count = len(grads)
     anywhere = pl.BlockSpec(memory_space=pl.ANY)
     return pl.pallas_call(
@@ -1280,20 +1231,76 @@
     halves = (((line == 2) & (lane < HEAD_DIM)) | ((line == 3) & (lane >= HEAD_DIM))).astype(jnp.float32)
     products = mix_ref[...].astype(jnp.float32) * do_ref[...].astype(jnp.float32)
     logs = lax.dot_general(
-        picked, logs_ref[...], NT, precision=lax.Precision.HIGHEST, preferred_element_type=jnp.float32)
+        picked, logs_ref[...], NT, precision=lax.Precision.HIGH, preferred_element_type=jnp.float32)
     return logs + lax.dot_general(
-        halves, products, NT, precision=lax.Precision.HIGHEST, preferred_element_type=jnp.float32)
-
-
-def cross_back_kernel(q_ref, k_ref, v_ref, do_ref, mix_ref, logs_ref, dq_ref, dk_ref, dv_ref, acc, stats):
-    stats[...] = pair_stats(pl.program_id(0), mix_ref, do_ref, logs_ref)
-
-    def put(start, n, dk, dv):
-        dk_ref[start : start + n, :] = dk.astype(dk_ref.dtype)
-        dv_ref[start : start + n, :] = dv.astype(dv_ref.dtype)
-
-    back_pair(k_ref.shape[0], False, q_ref, k_ref, v_ref, do_ref, stats, acc, put)
-    dq_ref[...] = acc[...].astype(dq_ref.dtype)
+        halves, products, NT, precision=lax.Precision.HIGH, preferred_element_type=jnp.float32)
+
+
+def both_heads(array):
+    low = lax.broadcasted_iota(jnp.int32, (1, 128), 1) < HEAD_DIM
+    zero = jnp.zeros_like(array)
+    return jnp.concatenate([jnp.where(low, array, zero), jnp.where(low, zero, array)], axis=0)
+
+
+def one_head_each(array):
+    low = lax.broadcasted_iota(jnp.int32, (1, 128), 1) < HEAD_DIM
+    half = array.shape[0] // 2
+    return jnp.where(low, array[:half], array[half:])
+
+
+def cross_kernel(q_ref, k_ref, v_ref, mix_ref, logs_ref):
+    pair = pl.program_id(0)
+    keys = k_ref.shape[0]
+    lane = lax.broadcasted_iota(jnp.int32, (1, 128), 1)
+    lower = lax.broadcasted_iota(jnp.int32, (1, 2 * keys), 1) < keys
+
+    @pl.when(pair == 0)
+    def _():
+        logs_ref[...] = jnp.zeros_like(logs_ref)
+
+    scores = dg(q_ref[...] * jnp.bfloat16(HEAD_DIM**-0.5), both_heads(k_ref[...]), NT)
+    tops = [
+        jnp.max(jnp.where(lower if h == 0 else jnp.logical_not(lower), scores, -1e30), axis=1, keepdims=True) for h in range(2)
+    ]
+    powers = jnp.exp(scores - jnp.where(lower, tops[0], tops[1])).astype(jnp.bfloat16)
+    values = both_heads(v_ref[...])
+    ones = both_heads(jnp.ones(v_ref.shape, v_ref.dtype))
+    out = dg(powers, jnp.concatenate([values, ones], axis=1), NN)
+    totals = out[:, 128:]
+    mix_ref[...] = (out[:, :128] / totals).astype(mix_ref.dtype)
+    sums = jnp.log(totals)
+    logs = logs_ref[...]
+    for h in range(2):
+        logs = jnp.where(lane == 2 * pair + h, tops[h] + sums[:, h * HEAD_DIM : h * HEAD_DIM + 1], logs)
+    logs_ref[...] = logs
+
+
+def cross(q, k, v):
+    rows, width = q.shape
+    keys = k.shape[0]
+    long, short = pl.BlockSpec((rows, 128), lambda i: (0, i)), pl.BlockSpec((keys, 128), lambda i: (0, i))
+    return pl.pallas_call(
+        cross_kernel,
+        grid=(width // 128,),
+        in_specs=[long, short, short],
+        out_specs=[long, pl.BlockSpec((rows, 128), lambda i: (0, 0))],
+        out_shape=[jax.ShapeDtypeStruct((rows, width), jnp.bfloat16), jax.ShapeDtypeStruct((rows, 128), jnp.float32)],
+        compiler_params=pltpu.CompilerParams(vmem_limit_bytes=40 << 20),
+        cost_estimate=pl.CostEstimate(
+            flops=4 * rows * keys * width, bytes_accessed=6 * rows * width, transcendentals=rows * keys * width // HEAD_DIM),
+    )(q, k, v)
+
+
+def cross_back_kernel(q_ref, k_ref, v_ref, do_ref, mix_ref, logs_ref, dq_ref, dk_ref, dv_ref):
+    keys = k_ref.shape[0]
+    stats = pair_stats(pl.program_id(0), mix_ref, do_ref, logs_ref)
+    upper = lax.broadcasted_iota(jnp.int32, (2 * keys, 1), 0) < keys
+    k, v, do = both_heads(k_ref[...] * jnp.bfloat16(HEAD_DIM**-0.5)), both_heads(v_ref[...]), do_ref[...]
+    p = jnp.exp(dg(k, q_ref[...], NT) - jnp.where(upper, stats[0:1, :], stats[1:2, :]))
+    ds = (p * (dg(v, do, NT) - jnp.where(upper, stats[2:3, :], stats[3:4, :]))).astype(jnp.bfloat16)
+    dv_ref[...] = one_head_each(dg(p.astype(jnp.bfloat16), do, NN)).astype(dv_ref.dtype)
+    dk_ref[...] = (one_head_each(dg(ds, q_ref[...], NN)) * HEAD_DIM**-0.5).astype(dk_ref.dtype)
+    dq_ref[...] = dg(ds, k, TN).astype(dq_ref.dtype)
 
 
 def cross_back(q, k, v, do, mix, logs):
@@ -1306,7 +1313,6 @@
         in_specs=[long, short, short, long, long, pl.BlockSpec((rows, 128), lambda i: (0, 0))],
         out_specs=[long, short, short],
         out_shape=[jax.ShapeDtypeStruct(a.shape, jnp.bfloat16) for a in (q, k, v)],
-        scratch_shapes=[pltpu.VMEM((rows, 128), jnp.float32), pltpu.VMEM((8, rows), jnp.float32)],
         compiler_params=pltpu.CompilerParams(vmem_limit_bytes=40 << 20),
         cost_estimate=pl.CostEstimate(
             flops=10 * rows * keys * width, bytes_accessed=10 * rows * width, transcendentals=rows * keys * width // HEAD_DIM),
@@ -1588,7 +1594,7 @@
     )
     text_k = matmul(clip_text, key_cross).astype(jnp.bfloat16)
     text_v = matmul(clip_text, value_cross).astype(jnp.bfloat16)
-    cross_mix, cross_logs = attend(cross_q, text_k, text_v, False, jnp.bfloat16)
+    cross_mix, cross_logs = cross(cross_q, text_k, text_v)
     resid_two = resid_one + matmul(cross_mix, out_cross)
     hidden_three = norm_forward(resid_two, norm_params[4], norm_params[5]).astype(jnp.bfloat16)
     layer_out, grad_three, up_grad, down_grad = feed(hidden_three, cotangent, resid_two, up_blocks, down_blocks)

time: 612 us -> 595 us (0.972)
  Pallas kernels: 472 us -> 456 us
    pallas_call x1, Pallas kernels: 19.5 us -> 10.5 us  [cross_back(): pl.pallas_call(cross_back_kernel, grid=(width // 128,), in_specs=[long, s...]
  transfers between devices with their start and end apart: 5 -> 5, of which waited for: 0 -> 0; matrix products, arithmetic and copies ran while one was open for 16% -> 16% of each run, Pallas kernels for 70% -> 69%
where the time goes in v8:
time: 595 us; the launch traced here: 589 us
  Pallas kernels  456 us (77%)
  matrix products  68.8 us (12%)
  other arithmetic  21.3 us (4%)
  local copies, waits for them, and re-layouts  18.7 us (3%)
  between operations  14.8 us (2%)
  starting transfers between devices  7.95 us (1%)
    pallas_call x1, Pallas kernels, pair_back(): pl.pallas_call(functools.partial(pair_back_kernel, tile, far_tile, units,...  170 us
    pallas_call x1, Pallas kernels, pair_attend(): pl.pallas_call(functools.partial(pair_attend_kernel, tile, units, count,...  119 us
    pallas_call x1, Pallas kernels, gather_blocks(): pl.pallas_call(functools.partial(gather_kernel, units, count), out_shape=...  58.6 us
    pallas_call x1, Pallas kernels, feed(): pl.pallas_call(feed_kernel, grid=(ff // chunk,), in_specs=[whole, whole,...  49 us
    pallas_call x1, Pallas kernels, scatter_blocks(): pl.pallas_call(functools.partial(scatter_kernel, units, count), out_shape...  42.2 us
    dot_general x8, matrix products, over_tokens(): lax.dot_general(left, right, (((0,), (0,)), ((), ())), preferred_element_...  26 us
    dot_general x8, matrix products, by_transposed(): lax.dot_general(left, right, (((1,), (1,)), ((), ())), preferred_element_...  22.1 us
    dot_general x8, matrix products, matmul(): return jnp.dot(left, right, preferred_element_type=jnp.float32)  20.7 us
  transfers between devices with their start and end apart: 5, of which 0 were waited for; matrix products, arithmetic and copies ran while one was open for 16% of the time, Pallas kernels for 69%

profile of v8, /device:TPU:0, one launch (start us, length us, event | category | flops | bytes accessed | tf_op | source)
XLA Modules:
  0.0 589.0 jit_solution(5692069782672128918)
XLA Ops:
  8.7 3.0 collective-permute-start
  13.1 58.6 %shard_map.330 = (bf16[4,2,1,128,1024]{4,3,2,1,0:T(8,128)(2,1)}, bf16[4,2,1,128,1024]{4,3,2,1,0:T(8,128)(2,1)}, bf16[4,2,1,128,1024]{4,3,2,1,0:T(8,128)(2,1)}, bf16[4,2,1,16,512]{4,3,2,1,0:T(8,128)(2,1)}) custom-call(bf16[1,128,256]{2,1,0:T(8,128)(2,1)} %bitcast.141, bf16[1,128,256]{2,1,0:T(8,128)(2,1)} %bitcast.142, bf16[1,128,256]{2,1,0:T(8,128)(2,1)} %bitcast.143, ...), custom_call_target="tpu_custom_call" | custom-call | bytes 12845056 | tf_op jit(solution)/shard_map/pallas_call | solution.py:738
  78.5 3.0 convolution_convert_fusion.11.refs_2_.refs_5_
  83.4 119.2 %shard_map.331 = (bf16[750,1024]{1,0:T(8,128)(2,1)S(1)}, f32[750,128]{1,0:T(8,128)S(1)}, bf16[4,750,128]{2,1,0:T(8,128)(2,1)S(1)}, bf16[4,750,128]{2,1,0:T(8,128...) custom-call(bf16[750,1024]{1,0:T(8,128)(2,1)S(1)} %convolution_conve, ...), custom_call_target="tpu_custom_call" | custom-call | flops 2304000000 | bytes 12288000 | tf_op jit(solution)/shard_map/pallas_call | solution.py:1173
  202.6 4.9 fusion.35
  216.7 6.6 %shard_map.332 = (bf16[750,1024]{1,0:T(8,128)(2,1)S(1)}, f32[750,128]{1,0:T(8,128)S(1)}) custom-call(bf16[750,1024]{1,0:T(8,128)(2,1)S(1)} %convolution_convert_fusion.10.q_ref, bf16[64,1024]{1,0:T(8,128)(2,1)S(1)} %convolution_convert_fusion.15.k_ref, bf16[64,1024]{1,0:T(8,128)(2,1)S(1)} %convolution_convert_fusion.14.v_ref), custom_call_target="tpu_custom_call" | custom-call | flops 196608000 | bytes 4608000 | tf_op jit(solution)/shard_map/pallas_call | solution.py:1282
  228.5 49.0 %shard_map.333 = (bf16[750,1024]{1,0:T(8,128)(2,1)}, f32[750,1024]{1,0:T(8,128)}, bf16[8,4,128,1024]{3,2,1,0:T(8,128)(2,1)}, bf16[4096,1024]{1,0:T(8,128)(2,1)}) custom-call(bf16[750,1024]{1,0:T(8,128)(2,1)} %add_convert_fusion.h_ref, bf16[750,1024]{1,0:T(8,128)(2,1)} %cot_ref.1, f32[750,1024]{1,0:T(8,128)} %copy-done.14, ...), custom_call_target="tpu_custom_call" | custom-call | flops 37748736000 | bytes 45842432 | tf_op jit(solution)/shard_map/pallas_call | solution.py:474
  277.6 4.0 multiply_reduce_fusion
  287.0 10.5 %shard_map.334 = (bf16[750,1024]{1,0:T(8,128)(2,1)S(1)}, bf16[64,1024]{1,0:T(8,128)(2,1)S(1)}, bf16[64,1024]{1,0:T(8,128)(2,1)S(1)}) custom-call(bf16[750,1024]{1,0:T(8,128)(2,1)S(1)} %convolution_convert_fusion.10.q_ref, bf16[64,1024]{1,0:T(8,128)(2,1)S(1)} %convolution_convert_fusion.15.k_ref, bf16[64,1024]{1,0:T(8,128)(2,1)S(1)} %convolution_convert_fusion.14.v_ref, ...), custom_call_target="tpu_custom_call" | custom-call | flops 491520000 | bytes 7680000 | tf_op jit(solution)/shard_map/pallas_call | solution.py:1310
  297.5 4.8 collective-permute-start.1
  307.2 3.2 convolution_convert_fusion.7
  310.4 3.0 convolution_convert_fusion.8.refs_3_.refs_6_
  313.4 3.4 convolution_convert_fusion.6
  316.8 3.2 convolution_convert_fusion.5
  324.6 170.1 %shard_map.335 = (bf16[750,1024]{1,0:T(8,128)(2,1)}, bf16[750,1024]{1,0:T(8,128)(2,1)}, bf16[750,1024]{1,0:T(8,128)(2,1)}, f32[1,128,256]{2,1,0:T(8,128)}, f32[1...) custom-call(bf16[750,1024]{1,0:T(8,128)(2,1)} %copy-done, ...), custom_call_target="tpu_custom_call" | custom-call | flops 5760000000 | bytes 12288000 | tf_op jit(solution)/shard_map/pallas_call | solution.py:1512
  494.7 4.0 fusion.37
  501.2 3.9 fusion.31
  505.2 3.3 fusion.8
  509.5 5.1 convolution_convert_fusion.4
  514.5 3.4 convolution_convert_fusion.2
  518.0 3.4 convolution_convert_fusion.3
  521.4 42.2 %shard_map.336 = (f32[1,128,256]{2,1,0:T(8,128)}, f32[1,128,256]{2,1,0:T(8,128)}, f32[1,128,256]{2,1,0:T(8,128)}, f32[1,16,128]{2,1,0:T(8,128)}) custom-call(bf16[4,2,1,128,1024]{4,3,2,1,0:T(8,128)(2,1)} %bitcast.128, bf16[4,2,1,128,1024]{4,3,2,1,0:T(8,128)(2,1)} %bitcast.130, bf16[4,2,1,128,1024]{4,3,2,1,0:T(8,128)(2,1)} %bitcast.129, ...), custom_call_target="tpu_custom_call" | custom-call | flops 3211264 | bytes 12845056 | tf_op jit(solution)/shard_map/pallas_call | solution.py:935
  567.3 3.0 convolution_add_fusion.1
  570.4 3.9 add_add_fusion.3
  (180 shorter events, 55.6 us)
Async XLA Ops:
  7.2 67.7 %copy-start.16 = (bf16[750,1024]{1,0:T(8,128)(2,1)S(1)}, bf16[750,1024]{1,0:T(8,128)(2,1)}, u32[]{:S(2)}) copy-start(bf16[750,1024]{1,0:T(8,128)(2,1)} %param.21) | copy-start | bytes 4608004
  7.2 221.3 %all-gather.5.cloned.1.call-start = ((), (), s32[]{:S(2)}) async-start(), calls=%async_computation.2 | async-start | bytes 8650752 | tf_op jit(solution)/shard_map/all_gather | solution.py:1564
  7.9 220.5 %all-gather.7.cloned.1.call-start = ((), (), s32[]{:S(2)}) async-start(), calls=%async_computation.3 | async-start | bytes 8650752 | tf_op jit(solution)/shard_map/all_gather | solution.py:1565
  8.7 565.6 %reduce-scatter.2.cloned.1.call-start = ((), (), s32[]{:S(2)}) async-start(), calls=%async_computation.1 | async-start | bytes 8650752 | tf_op jit(solution)/shard_map/reduce_scatter | solution.py:1601
  8.7 203.6 %collective-permute-start = (bf16[32,1024]{1,0:T(8,128)(2,1)}, bf16[32,1024]{1,0:T(8,128)(2,1)S(1)}, u32[]{:S(2)}, u32[]{:S(2)}) collective-permute-start(bf16[32,1024]{1,0:T(8,128)(2,1)} %param.22), channel_id=1, source_target_pairs={{0,4},{8,12},{16,20},{24,28},{4,0},{12,8},{20,16},{28,24},{1,5},{9... | collective-permute-start | bytes 196616 | tf_op jit(solution)/shard_map/ppermute | solution.py:1591
  83.3 119.2 %copy-start = (bf16[750,1024]{1,0:T(8,128)(2,1)}, bf16[750,1024]{1,0:T(8,128)(2,1)S(1)}, u32[]{:S(2)}) copy-start(bf16[750,1024]{1,0:T(8,128)(2,1)S(1)} %convolution_convert_fusion.13.refs_0_.refs_3_) | copy-start | bytes 4608004
  202.6 5.0 copy-start.1
  202.6 5.0 copy-start.3
  212.4 10.9 %copy-start.21 = (f32[750,1024]{1,0:T(8,128)S(1)}, f32[750,1024]{1,0:T(8,128)}, u32[]{:S(2)}) copy-start(f32[750,1024]{1,0:T(8,128)} %copy-done.20) | copy-start | bytes 9216004
  212.4 10.9 %copy-start.46 = (bf16[4,2,1,128,1024]{4,3,2,1,0:T(8,128)(2,1)S(1)}, bf16[4,2,1,128,1024]{4,3,2,1,0:T(8,128)(2,1)}, u32[]{:S(2)}) copy-start(bf16[4,2,1,128,1024]{4,3,2,1,0:T(8,128)(2,1)} %get-tuple-element.77) | copy-start | bytes 6291460
  287.0 15.4 %copy-start.22 = (f32[750,1024]{1,0:T(8,128)S(1)}, f32[750,1024]{1,0:T(8,128)}, u32[]{:S(2)}) copy-start(f32[750,1024]{1,0:T(8,128)} %copy-done.20) | copy-start | bytes 9216004
  287.0 15.4 %copy-start.45 = (bf16[4,2,1,128,1024]{4,3,2,1,0:T(8,128)(2,1)S(1)}, bf16[4,2,1,128,1024]{4,3,2,1,0:T(8,128)(2,1)}, u32[]{:S(2)}) copy-start(bf16[4,2,1,128,1024]{4,3,2,1,0:T(8,128)(2,1)} %get-tuple-element.73) | copy-start | bytes 6291460
  297.5 22.8 %collective-permute-start.1 = (bf16[32,2048]{1,0:T(8,128)(2,1)S(1)}, bf16[32,2048]{1,0:T(8,128)(2,1)S(1)}, u32[]{:S(2)}, u32[]{:S(2)}) collective-permute-start(bf16[32,2048]{1,0:T(8,128)(2,1)S(1)} %broadcast_select_fusion), channel_id=1, source_target_pairs={{0,4},{8,12},{16,20},{24,28},{4,0},{12,8},{20,16},{28,24},{1,5},{9... | collective-permute-start | bytes 393224 | tf_op jit(solution)/shard_map/ppermute | solution.py:1613
  509.5 5.1 copy-start.42
  563.6 6.8 %copy-start.19 = (f32[750,1024]{1,0:T(8,128)S(1)}, f32[750,1024]{1,0:T(8,128)}, u32[]{:S(2)}) copy-start(f32[750,1024]{1,0:T(8,128)} %copy-done.18) | copy-start | bytes 9216004
  570.3 5.8 copy-start.34
  570.3 6.5 %copy-start.33 = (f32[1,128,256]{2,1,0:T(8,128)S(1)}, f32[1,128,256]{2,1,0:T(8,128)}, u32[]{:S(2)}) copy-start(f32[1,128,256]{2,1,0:T(8,128)} %get-tuple-element.93) | copy-start | bytes 393220
  570.3 7.1 %copy-start.32 = (f32[1,128,256]{2,1,0:T(8,128)S(1)}, f32[1,128,256]{2,1,0:T(8,128)}, u32[]{:S(2)}) copy-start(f32[1,128,256]{2,1,0:T(8,128)} %get-tuple-element.94) | copy-start | bytes 393220
  570.3 7.8 %copy-start.31 = (f32[1,128,256]{2,1,0:T(8,128)S(1)}, f32[1,128,256]{2,1,0:T(8,128)}, u32[]{:S(2)}) copy-start(f32[1,128,256]{2,1,0:T(8,128)} %get-tuple-element.95) | copy-start | bytes 393220
  570.4 8.4 %copy-start.30 = (f32[1,128,256]{2,1,0:T(8,128)S(1)}, f32[1,128,256]{2,1,0:T(8,128)}, u32[]{:S(2)}) copy-start(f32[1,128,256]{2,1,0:T(8,128)} %get-tuple-element.96) | copy-start | bytes 393220
  570.4 9.1 %copy-start.29 = (f32[1,128,256]{2,1,0:T(8,128)S(1)}, f32[1,128,256]{2,1,0:T(8,128)}, u32[]{:S(2)}) copy-start(f32[1,128,256]{2,1,0:T(8,128)} %get-tuple-element.97) | copy-start | bytes 393220
  570.4 9.7 %copy-start.28 = (f32[1,128,256]{2,1,0:T(8,128)S(1)}, f32[1,128,256]{2,1,0:T(8,128)}, u32[]{:S(2)}) copy-start(f32[1,128,256]{2,1,0:T(8,128)} %get-tuple-element.98) | copy-start | bytes 393220
  570.4 10.4 %copy-start.27 = (f32[1,128,256]{2,1,0:T(8,128)S(1)}, f32[1,128,256]{2,1,0:T(8,128)}, u32[]{:S(2)}) copy-start(f32[1,128,256]{2,1,0:T(8,128)} %get-tuple-element.99) | copy-start | bytes 393220
  574.3 7.1 %copy-start.26 = (f32[4,128,256]{2,1,0:T(8,128)S(1)}, f32[4,128,256]{2,1,0:T(8,128)}, u32[]{:S(2)}) copy-start(f32[4,128,256]{2,1,0:T(8,128)} %get-tuple-element.101) | copy-start | bytes 1572868
  (29 other events, 81.3 us)
Sparse Core Ops, SparseCore 0:
  10.9 86.3 all-gather.4
  100.2 91.2 all-gather.6
  277.7 162.5 reduce-scatter.1

commit v9 on v8

--- a/solution.py
+++ b/solution.py
@@ -439,7 +439,7 @@
 NT=(((1,),(1,)),((),())); NN=(((1,),(0,)),((),())); TN=(((0,),(0,)),((),()))
 def dg(a,b,dims): return lax.dot_general(a,b,dims,preferred_element_type=jnp.float32)
 
-def feed_kernel(h_ref,cot_ref,res_ref,up_ref,down_ref,out_ref,g_ref,dup_ref,ddown_ref,acc):
+def feed_kernel(h_ref,cot_ref,res_ref,up_ref,down_ref,out_ref,g_ref,dup_ref,ddown_ref,ddown_blocks_ref,acc):
     i=pl.program_id(0)
     @pl.when(i==0)
     def _():
@@ -457,7 +457,10 @@
         columns=slice(at*wide,(at+1)*wide)
         cot=cot_ref[:,columns]
         acc[:,columns]+=dg(inner,down_ref[0,at],NN)
-        ddown_ref[:,columns]=dg(inner,cot,TN).astype(ddown_ref.dtype)
+        ddown=dg(inner,cot,TN).astype(ddown_ref.dtype)
+        split=ddown_ref.shape[1]
+        ddown_ref[0,:,columns]=ddown[:split]
+        ddown_blocks_ref[0,at]=ddown[split:]
         part=dg(cot,down_ref[0,at],NT)
         grad=part if grad is None else grad+part
     gpre=(grad*slope).astype(jnp.bfloat16)
@@ -467,14 +470,14 @@
     def _(): out_ref[...]=acc[...].astype(out_ref.dtype)
 
 def feed(h,cot,res,up,down):
-    rows,d=h.shape; chunk=down.shape[2]; strips=up.shape[3]//chunk; ff=down.shape[0]*chunk
+    rows,d=h.shape; chunk=down.shape[2]; strips=up.shape[3]//chunk; ff=down.shape[0]*chunk; split=chunk//2
     whole=pl.BlockSpec((rows,d),lambda i:(0,0))
     up_spec=pl.BlockSpec((up.shape[0],1,up.shape[2],chunk),lambda i:(0,i//strips,0,i%strips))
     down_spec=pl.BlockSpec((1,)+down.shape[1:],lambda i:(i,0,0,0))
     return pl.pallas_call(feed_kernel,grid=(ff//chunk,),
         in_specs=[whole,whole,whole,up_spec,down_spec],
-        out_specs=[whole,whole,up_spec,pl.BlockSpec((chunk,d),lambda i:(i,0))],
-        out_shape=[jax.ShapeDtypeStruct((rows,d),jnp.bfloat16),jax.ShapeDtypeStruct((rows,d),jnp.float32),jax.ShapeDtypeStruct(up.shape,jnp.bfloat16),jax.ShapeDtypeStruct((ff,d),jnp.bfloat16)],
+        out_specs=[whole,whole,up_spec,pl.BlockSpec((1,split,d),lambda i:(i,0,0)),pl.BlockSpec((1,down.shape[1],chunk-split,down.shape[3]),lambda i:(i,0,0,0))],
+        out_shape=[jax.ShapeDtypeStruct((rows,d),jnp.bfloat16),jax.ShapeDtypeStruct((rows,d),jnp.float32),jax.ShapeDtypeStruct(up.shape,jnp.bfloat16),jax.ShapeDtypeStruct((down.shape[0],split,d),jnp.bfloat16),jax.ShapeDtypeStruct((*down.shape[:2],chunk-split,down.shape[3]),jnp.bfloat16)],
         scratch_shapes=[pltpu.VMEM((rows,d),jnp.float32)],
         compiler_params=pltpu.CompilerParams(vmem_limit_bytes=56<<20),
         cost_estimate=pl.CostEstimate(flops=12*rows*d*ff,bytes_accessed=8*d*ff+16*rows*d,transcendentals=2*rows*ff))(h,cot,res,up,down)
@@ -1564,6 +1567,9 @@
     up_blocks = lax.all_gather(up_weight, everyone).reshape(*places, *up_weight.shape)
     down_blocks = lax.all_gather(down_weight, everyone).reshape(*places, *down_weight.shape)
 
+    out_cross = lax.all_gather(cross_output, everyone).reshape(*places, *cross_output.shape)
+    out_cross = out_cross.transpose(0, 2, 1, 3).reshape(width, width)
+
     def small(block):
         return block.reshape(1, block_rows, block_cols)
 
@@ -1582,9 +1588,8 @@
     self_v = matmul(hidden_one, value_self).astype(jnp.bfloat16)
     self_q = matmul(hidden_one, query_self).astype(jnp.bfloat16)
     (self_mix, log_lanes, far_q, far_k, far_v), late = pair_attend(
-        self_q, self_k, self_v, [small(w) for w in (self_output, cross_query, cross_key, cross_value, cross_output)],
-        5, [3] * 12)
-    out_self, query_cross, key_cross, value_cross, out_cross = [flat(w) for w in late]
+        self_q, self_k, self_v, [small(w) for w in (self_output, cross_query, cross_key, cross_value)], 5, [3] * 12)
+    out_self, query_cross, key_cross, value_cross = [flat(w) for w in late]
     resid_one = frames + matmul(self_mix, out_self)
     hidden_two = norm_forward(resid_one, norm_params[2], norm_params[3]).astype(jnp.bfloat16)
     cross_q = matmul(hidden_two, query_cross).astype(jnp.bfloat16)
@@ -1597,8 +1602,11 @@
     cross_mix, cross_logs = cross(cross_q, text_k, text_v)
     resid_two = resid_one + matmul(cross_mix, out_cross)
     hidden_three = norm_forward(resid_two, norm_params[4], norm_params[5]).astype(jnp.bfloat16)
-    layer_out, grad_three, up_grad, down_grad = feed(hidden_three, cotangent, resid_two, up_blocks, down_blocks)
-    up_sum = lax.psum_scatter(up_grad.reshape(-1, *up_weight.shape), everyone, scatter_dimension=0).astype(jnp.float32)
+    layer_out, grad_three, up_grad, down_grad, down_grad_blocks = feed(hidden_three, cotangent, resid_two, up_blocks, down_blocks)
+    up_sum, down_sum = [
+        lax.psum_scatter(g.reshape(-1, *g.shape[2:]), everyone, scatter_dimension=0).astype(jnp.float32)
+        for g in (up_grad, down_grad_blocks)
+    ]
 
     cotan_full = cotangent.astype(jnp.float32)
     unused_three, pull_three = jax.vjp(norm_forward, resid_two, norm_params[4], norm_params[5])
@@ -1632,7 +1640,7 @@
     (grad_self_q, grad_self_k, grad_self_v), early_sums = pair_back(
         self_q, self_k, self_v, grad_self_mix, self_mix, log_lanes, (far_q, far_k, far_v),
         [by_place(g, 1) for g in (self_out_grad, cross_query_part, cross_key_part, cross_value_part, cross_out_grad)]
-        + [by_place(down_grad, down_weight.shape[0] // block_rows)], 4, [5] * 12)
+        + [by_place(down_grad, down_grad.shape[1] // block_rows)], 4, [5] * 12)
     self_query_part = over_tokens(hidden_one, grad_self_q)
     self_key_part = over_tokens(hidden_one, grad_self_k)
     self_value_part = over_tokens(hidden_one, grad_self_v)
@@ -1656,7 +1664,7 @@
     norm_parts = late_sums[3][0, :6, :piece]
     sums = [*late_sums[:3], *early_sums]
     sums = [total.reshape(-1, total.shape[-1]) for total in sums]
-    return (layer_out, input_grad, text_grad, *sums[:-1], up_sum, sums[-1], *norm_parts)
+    return (layer_out, input_grad, text_grad, *sums[:-1], up_sum, jnp.concatenate([sums[-1], down_sum]), *norm_parts)
 
 
 def local(*arrays):

time: 595 us -> 621 us (1.044)
  waiting for transfers between devices: 1.4 us -> 40.1 us
  Pallas kernels: 456 us -> 438 us
    all_gather x1, waiting for transfers between devices: 0.01 us -> 35.3 us  [fast(): lax.all_gather(down_weight, everyone).reshape(*places, *down_weight.shape)]
    pallas_call x1, Pallas kernels: 42.2 us -> 63.8 us  [scatter_blocks(): pl.pallas_call(functools.partial(scatter_kernel, units, count), out_shape...]
    pallas_call x1, Pallas kernels: 170 us -> 150 us  [pair_back(): pl.pallas_call(functools.partial(pair_back_kernel, tile, far_tile, units,...]
    pallas_call x1, Pallas kernels: 119 us -> 108 us  [pair_attend(): pl.pallas_call(functools.partial(pair_attend_kernel, tile, units, count,...]
    pallas_call x1, Pallas kernels: 58.6 us -> 49.6 us  [gather_blocks(): pl.pallas_call(functools.partial(gather_kernel, units, count), out_shape=...]
    unnamed x111 -> x108, local copies, waits for them, and re-layouts: 13.2 us -> 13.2 us
  transfers between devices with their start and end apart: 5 -> 7, of which waited for: 0 -> 2; matrix products, arithmetic and copies ran while one was open for 16% -> 17% of each run, Pallas kernels for 69% -> 63%
where the time goes in v9:
time: 621 us; the launch traced here: 615 us
  Pallas kernels  438 us (71%)
  matrix products  71.2 us (11%)
  waiting for transfers between devices  40.1 us (6%)
  local copies, waits for them, and re-layouts  23.3 us (4%)
  other arithmetic  23 us (4%)
  between operations  14.7 us (2%)
    pallas_call x1, Pallas kernels, pair_back(): pl.pallas_call(functools.partial(pair_back_kernel, tile, far_tile, units,...  150 us
    pallas_call x1, Pallas kernels, pair_attend(): pl.pallas_call(functools.partial(pair_attend_kernel, tile, units, count,...  108 us
    pallas_call x1, Pallas kernels, scatter_blocks(): pl.pallas_call(functools.partial(scatter_kernel, units, count), out_shape...  63.8 us
    pallas_call x1, Pallas kernels, gather_blocks(): pl.pallas_call(functools.partial(gather_kernel, units, count), out_shape=...  49.6 us
    pallas_call x1, Pallas kernels, feed(): pl.pallas_call(feed_kernel, grid=(ff // chunk,), in_specs=[whole, whole,...  49.2 us
    all_gather x1, waiting for transfers between devices, fast(): lax.all_gather(down_weight, everyone).reshape(*places, *down_weight.shape)  35.3 us
    dot_general x8, matrix products, over_tokens(): lax.dot_general(left, right, (((0,), (0,)), ((), ())), preferred_element_...  25.9 us
    dot_general x8, matrix products, matmul(): return jnp.dot(left, right, preferred_element_type=jnp.float32)  23.1 us
  transfers between devices with their start and end apart: 7, of which 2 were waited for; matrix products, arithmetic and copies ran while one was open for 17% of the time, Pallas kernels for 63%

profile of v9, /device:TPU:0, one launch (start us, length us, event | category | flops | bytes accessed | tf_op | source)
XLA Modules:
  0.0 614.5 jit_solution(10235383728265328197)
XLA Ops:
  9.5 3.0 collective-permute-start
  13.9 49.6 %shard_map.330 = (bf16[4,2,1,128,1024]{4,3,2,1,0:T(8,128)(2,1)}, bf16[4,2,1,128,1024]{4,3,2,1,0:T(8,128)(2,1)}, bf16[4,2,1,128,1024]{4,3,2,1,0:T(8,128)(2,1)}, bf16[4,2,1,16,512]{4,3,2,1,0:T(8,128)(2,1)}) custom-call(bf16[1,128,256]{2,1,0:T(8,128)(2,1)} %bitcast.161, bf16[1,128,256]{2,1,0:T(8,128)(2,1)} %bitcast.162, bf16[1,128,256]{2,1,0:T(8,128)(2,1)} %bitcast.163, ...), custom_call_target="tpu_custom_call" | custom-call | bytes 12845056 | tf_op jit(solution)/shard_map/pallas_call | solution.py:741
  75.1 108.4 %shard_map.331 = (bf16[750,1024]{1,0:T(8,128)(2,1)S(1)}, f32[750,128]{1,0:T(8,128)S(1)}, bf16[4,750,128]{2,1,0:T(8,128)(2,1)S(1)}, bf16[4,750,128]{2,1,0:T(8,128...) custom-call(bf16[750,1024]{1,0:T(8,128)(2,1)S(1)} %convolution_conve, ...), custom_call_target="tpu_custom_call" | custom-call | flops 2304000000 | bytes 12288000 | tf_op jit(solution)/shard_map/pallas_call | solution.py:1176
  183.5 4.9 fusion.47
  197.5 6.6 %shard_map.332 = (bf16[750,1024]{1,0:T(8,128)(2,1)S(1)}, f32[750,128]{1,0:T(8,128)S(1)}) custom-call(bf16[750,1024]{1,0:T(8,128)(2,1)S(1)} %convolution_convert_fusion.9.q_ref, bf16[64,1024]{1,0:T(8,128)(2,1)S(1)} %convolution_convert_fusion.14.k_ref, bf16[64,1024]{1,0:T(8,128)(2,1)S(1)} %convolution_convert_fusion.13.v_ref), custom_call_target="tpu_custom_call" | custom-call | flops 196608000 | bytes 4608000 | tf_op jit(solution)/shard_map/pallas_call | solution.py:1285
  204.8 4.7 copy.38
  209.5 4.4 fusion.48
  217.2 35.3 %all-gather.11.cloned.1.call-done = bf16[16384,256]{1,0:T(8,128)(2,1)} async-done(((bf16[512,256]{1,0:T(8,128)(2,1)}), bf16[16384,256]{1,0:T(8,128)(2,1)}) %all-gather.11.cloned.1.call-update) | async-done | bytes 8388624 | tf_op jit(solution)/shard_map/all_gather | solution.py:1568
  252.5 49.2 %shard_map.333 = (bf16[750,1024]{1,0:T(8,128)(2,1)}, f32[750,1024]{1,0:T(8,128)}, bf16[8,4,128,1024]{3,2,1,0:T(8,128)(2,1)}, bf16[8,256,1024]{2,1,0:T(8,128)(2,1)}, bf16[8,4,256,256]{3,2,1,0:T(8,128)(2,1)}) custom-call(bf16[750,1024]{1,0:T(8,128)(2,1)} %add_convert_fusion.h_ref, bf16[750,1024]{1,0:T(8,128)(2,1)} %cot_ref.1, f32[750,1024]{1,0:T(8,128)} %copy-done.15, ...), custom_call_target="tpu_custom_call" | custom-call | flops 37748736000 | bytes 45842432 | tf_op jit(solution)/shard_map/pallas_call | solution.py:477
  302.3 4.0 multiply_reduce_fusion
  311.8 10.2 %shard_map.334 = (bf16[750,1024]{1,0:T(8,128)(2,1)S(1)}, bf16[64,1024]{1,0:T(8,128)(2,1)S(1)}, bf16[64,1024]{1,0:T(8,128)(2,1)S(1)}) custom-call(bf16[750,1024]{1,0:T(8,128)(2,1)S(1)} %convolution_convert_fusion.9.q_ref, bf16[64,1024]{1,0:T(8,128)(2,1)S(1)} %convolution_convert_fusion.14.k_ref, bf16[64,1024]{1,0:T(8,128)(2,1)S(1)} %convolution_convert_fusion.13.v_ref, ...), custom_call_target="tpu_custom_call" | custom-call | flops 491520000 | bytes 7680000 | tf_op jit(solution)/shard_map/pallas_call | solution.py:1313
  328.4 3.2 convolution_convert_fusion.7
  334.6 3.5 convolution_convert_fusion.6
  338.1 3.2 convolution_convert_fusion.5
  345.9 149.7 %shard_map.335 = (bf16[750,1024]{1,0:T(8,128)(2,1)}, bf16[750,1024]{1,0:T(8,128)(2,1)}, bf16[750,1024]{1,0:T(8,128)(2,1)}, f32[1,128,256]{2,1,0:T(8,128)}, f32[1...) custom-call(bf16[750,1024]{1,0:T(8,128)(2,1)} %copy-done, ...), custom_call_target="tpu_custom_call" | custom-call | flops 5760000000 | bytes 12288000 | tf_op jit(solution)/shard_map/pallas_call | solution.py:1515
  495.6 4.0 fusion.49
  502.2 3.9 fusion.43
  506.1 3.3 fusion.8
  510.4 4.9 convolution_convert_fusion.4
  515.3 3.4 convolution_convert_fusion.2
  518.8 3.4 convolution_convert_fusion.3
  522.2 63.8 %shard_map.336 = (f32[1,128,256]{2,1,0:T(8,128)}, f32[1,128,256]{2,1,0:T(8,128)}, f32[1,128,256]{2,1,0:T(8,128)}, f32[1,16,128]{2,1,0:T(8,128)}) custom-call(bf16[4,2,1,128,1024]{4,3,2,1,0:T(8,128)(2,1)} %bitcast.145, bf16[4,2,1,128,1024]{4,3,2,1,0:T(8,128)(2,1)} %bitcast.147, bf16[4,2,1,128,1024]{4,3,2,1,0:T(8,128)(2,1)} %bitcast.146, ...), custom_call_target="tpu_custom_call" | custom-call | flops 3211264 | bytes 12845056 | tf_op jit(solution)/shard_map/pallas_call | solution.py:938
  589.8 3.0 convolution_add_fusion
  592.8 3.9 add_add_fusion.3
  (186 shorter events, 66.3 us)
Async XLA Ops:
  7.2 59.4 %copy-start.17 = (bf16[750,1024]{1,0:T(8,128)(2,1)S(1)}, bf16[750,1024]{1,0:T(8,128)(2,1)}, u32[]{:S(2)}) copy-start(bf16[750,1024]{1,0:T(8,128)(2,1)} %param.21) | copy-start | bytes 4608004
  7.2 197.6 %all-gather.7.cloned.1.call-start = ((), (), s32[]{:S(2)}) async-start(), calls=%async_computation.4 | async-start | bytes 2162688 | tf_op jit(solution)/shard_map/all_gather | solution.py:1570
  7.9 209.2 %all-gather.9.cloned.1.call-start = ((), (), s32[]{:S(2)}) async-start(), calls=%async_computation.5 | async-start | bytes 8650752 | tf_op jit(solution)/shard_map/all_gather | solution.py:1567
  8.7 243.8 %all-gather.11.cloned.1.call-start = ((), (), s32[]{:S(2)}) async-start(), calls=%async_computation.6 | async-start | bytes 8650752 | tf_op jit(solution)/shard_map/all_gather | solution.py:1568
  9.4 587.3 %reduce-scatter.5.cloned.1.call-start = ((), (), s32[]{:S(2)}) async-start(), calls=%async_computation.3 | async-start | bytes 4325376 | tf_op jit(solution)/shard_map/reduce_scatter | solution.py:1607
  9.5 183.9 %collective-permute-start = (bf16[32,1024]{1,0:T(8,128)(2,1)}, bf16[32,1024]{1,0:T(8,128)(2,1)S(1)}, u32[]{:S(2)}, u32[]{:S(2)}) collective-permute-start(bf16[32,1024]{1,0:T(8,128)(2,1)} %param.22), channel_id=1, source_target_pairs={{0,4},{8,12},{16,20},{24,28},{4,0},{12,8},{20,16},{28,24},{1,5},{9... | collective-permute-start | bytes 196616 | tf_op jit(solution)/shard_map/ppermute | solution.py:1596
  75.0 108.5 %copy-start = (bf16[750,1024]{1,0:T(8,128)(2,1)}, bf16[750,1024]{1,0:T(8,128)(2,1)S(1)}, u32[]{:S(2)}) copy-start(bf16[750,1024]{1,0:T(8,128)(2,1)S(1)} %convolution_convert_fusion.12.refs_0_.refs_3_) | copy-start | bytes 4608004
  183.5 5.0 copy-start.1
  183.5 5.0 copy-start.5
  183.5 5.0 copy-start.6
  204.8 107.0 %copy-start.3 = (bf16[750,1024]{1,0:T(8,128)(2,1)}, bf16[750,1024]{1,0:T(8,128)(2,1)S(1)}, u32[]{:S(2)}) copy-start(bf16[750,1024]{1,0:T(8,128)(2,1)S(1)} %get-tuple-element.76.mix_ref) | copy-start | bytes 4608004
  301.7 299.0 %reduce-scatter.3.cloned.1.call-start = ((), (), s32[]{:S(2)}) async-start(), calls=%async_computation.2 | async-start | bytes 8650752 | tf_op jit(solution)/shard_map/reduce_scatter | solution.py:1607
  311.8 11.8 %copy-start.22 = (f32[750,1024]{1,0:T(8,128)S(1)}, f32[750,1024]{1,0:T(8,128)}, u32[]{:S(2)}) copy-start(f32[750,1024]{1,0:T(8,128)} %copy-done.21) | copy-start | bytes 9216004
  311.8 11.8 %copy-start.46 = (bf16[4,2,1,128,1024]{4,3,2,1,0:T(8,128)(2,1)S(1)}, bf16[4,2,1,128,1024]{4,3,2,1,0:T(8,128)(2,1)}, u32[]{:S(2)}) copy-start(bf16[4,2,1,128,1024]{4,3,2,1,0:T(8,128)(2,1)} %get-tuple-element.73) | copy-start | bytes 6291460
  322.1 19.5 %collective-permute-start.1 = (bf16[32,2048]{1,0:T(8,128)(2,1)S(1)}, bf16[32,2048]{1,0:T(8,128)(2,1)S(1)}, u32[]{:S(2)}, u32[]{:S(2)}) collective-permute-start(bf16[32,2048]{1,0:T(8,128)(2,1)S(1)} %broadcast_select_fusion), channel_id=1, source_target_pairs={{0,4},{8,12},{16,20},{24,28},{4,0},{12,8},{20,16},{28,24},{1,5},{9... | collective-permute-start | bytes 393224 | tf_op jit(solution)/shard_map/ppermute | solution.py:1621
  586.0 6.8 %copy-start.20 = (f32[750,1024]{1,0:T(8,128)S(1)}, f32[750,1024]{1,0:T(8,128)}, u32[]{:S(2)}) copy-start(f32[750,1024]{1,0:T(8,128)} %copy-done.19) | copy-start | bytes 9216004
  592.8 9.8 %copy-start.35 = (f32[1,128,256]{2,1,0:T(8,128)S(1)}, f32[1,128,256]{2,1,0:T(8,128)}, u32[]{:S(2)}) copy-start(f32[1,128,256]{2,1,0:T(8,128)} %get-tuple-element.91) | copy-start | bytes 393220
  592.8 10.4 %copy-start.34 = (f32[1,128,256]{2,1,0:T(8,128)S(1)}, f32[1,128,256]{2,1,0:T(8,128)}, u32[]{:S(2)}) copy-start(f32[1,128,256]{2,1,0:T(8,128)} %get-tuple-element.92) | copy-start | bytes 393220
  592.8 11.1 %copy-start.33 = (f32[1,128,256]{2,1,0:T(8,128)S(1)}, f32[1,128,256]{2,1,0:T(8,128)}, u32[]{:S(2)}) copy-start(f32[1,128,256]{2,1,0:T(8,128)} %get-tuple-element.93) | copy-start | bytes 393220
  596.7 7.8 %copy-start.32 = (f32[1,128,256]{2,1,0:T(8,128)S(1)}, f32[1,128,256]{2,1,0:T(8,128)}, u32[]{:S(2)}) copy-start(f32[1,128,256]{2,1,0:T(8,128)} %get-tuple-element.94) | copy-start | bytes 393220
  596.7 8.5 %copy-start.31 = (f32[1,128,256]{2,1,0:T(8,128)S(1)}, f32[1,128,256]{2,1,0:T(8,128)}, u32[]{:S(2)}) copy-start(f32[1,128,256]{2,1,0:T(8,128)} %get-tuple-element.95) | copy-start | bytes 393220
  596.7 9.1 %copy-start.30 = (f32[1,128,256]{2,1,0:T(8,128)S(1)}, f32[1,128,256]{2,1,0:T(8,128)}, u32[]{:S(2)}) copy-start(f32[1,128,256]{2,1,0:T(8,128)} %get-tuple-element.96) | copy-start | bytes 393220
  596.7 9.8 %copy-start.29 = (f32[1,128,256]{2,1,0:T(8,128)S(1)}, f32[1,128,256]{2,1,0:T(8,128)}, u32[]{:S(2)}) copy-start(f32[1,128,256]{2,1,0:T(8,128)} %get-tuple-element.97) | copy-start | bytes 393220
  596.7 10.5 %copy-start.28 = (f32[1,128,256]{2,1,0:T(8,128)S(1)}, f32[1,128,256]{2,1,0:T(8,128)}, u32[]{:S(2)}) copy-start(f32[1,128,256]{2,1,0:T(8,128)} %get-tuple-element.98) | copy-start | bytes 393220
  (30 other events, 86.7 us)
Sparse Core Ops, SparseCore 0:
  10.9 60.0 all-gather.6
  73.9 92.3 all-gather.8
  169.2 83.2 all-gather.10
  301.8 145.0 reduce-scatter.4
  449.1 151.6 reduce-scatter.2

commit v10 on v8

--- a/solution.py
+++ b/solution.py
@@ -746,6 +746,9 @@
     )(*blocks)
 
 
+SCATTER_ORDERS = ("xyz", "yxz", "zxy", "zyx", "xzy", "yzx")
+
+
 def add_blocks(total, extra, leading):
     def one(at, unused):
         place = []
@@ -929,7 +932,7 @@
 
 
 def scatter_blocks(grads, collective_id, least):
-    blocks, units, scratch = scatter_plan(grads, least, ("xyz", "yxz", "zxy", "zyx", "xzy", "yzx"))
+    blocks, units, scratch = scatter_plan(grads, least, SCATTER_ORDERS)
     count = len(grads)
     anywhere = pl.BlockSpec(memory_space=pl.ANY)
     return pl.pallas_call(
@@ -1359,7 +1362,7 @@
         return pltpu.make_async_copy(source, target, local.at[which])
 
     scatters = scatters_of(place, units, grads, sums, *scatter_refs[:3], scatter_refs[3:])
-    turns = in_turn([scatter.stages() for scatter in scatters], 0.5)
+    turns = in_turn([scatter.stages() for scatter in scatters], 0.25)
 
     @pl.when(step == 0)
     def _():
@@ -1502,7 +1505,7 @@
     rows, width = q.shape
     pairs = width // 128
     fars = pairs // 2
-    blocks, units, scratch = scatter_plan(grads, 256, ORDERS)
+    blocks, units, scratch = scatter_plan(grads, 256, SCATTER_ORDERS)
     count = len(grads)
     block = pl.BlockSpec((rows, 128), lambda i: (0, lax.rem(jnp.minimum(i, pairs - 1) + fars, pairs)))
     joined = pl.BlockSpec((rows, 128), lambda i: (0, jnp.maximum(i - pairs - fars, 0)))

time: 595 us -> 588 us (0.988)
  Pallas kernels: 456 us -> 448 us
    pallas_call x1, Pallas kernels: 170 us -> 151 us  [pair_back(): pl.pallas_call(functools.partial(pair_back_kernel, tile, far_tile, units,...]
    pallas_call x1, Pallas kernels: 42.2 us -> 53.5 us  [scatter_blocks(): pl.pallas_call(functools.partial(scatter_kernel, units, count), out_shape...]
where the time goes in v10:
time: 588 us; the launch traced here: 581 us
  Pallas kernels  448 us (76%)
  matrix products  68.8 us (12%)
  other arithmetic  21.3 us (4%)
  local copies, waits for them, and re-layouts  18.7 us (3%)
  between operations  14.8 us (3%)
  starting transfers between devices  7.95 us (1%)
    pallas_call x1, Pallas kernels, pair_back(): pl.pallas_call(functools.partial(pair_back_kernel, tile, far_tile, units,...  151 us
    pallas_call x1, Pallas kernels, pair_attend(): pl.pallas_call(functools.partial(pair_attend_kernel, tile, units, count,...  119 us
    pallas_call x1, Pallas kernels, gather_blocks(): pl.pallas_call(functools.partial(gather_kernel, units, count), out_shape=...  58.6 us
    pallas_call x1, Pallas kernels, scatter_blocks(): pl.pallas_call(functools.partial(scatter_kernel, units, count), out_shape...  53.5 us
    pallas_call x1, Pallas kernels, feed(): pl.pallas_call(feed_kernel, grid=(ff // chunk,), in_specs=[whole, whole,...  49 us
    dot_general x8, matrix products, over_tokens(): lax.dot_general(left, right, (((0,), (0,)), ((), ())), preferred_element_...  26 us
    dot_general x8, matrix products, by_transposed(): lax.dot_general(left, right, (((1,), (1,)), ((), ())), preferred_element_...  22.1 us
    dot_general x8, matrix products, matmul(): return jnp.dot(left, right, preferred_element_type=jnp.float32)  20.7 us
  transfers between devices with their start and end apart: 5, of which 0 were waited for; matrix products, arithmetic and copies ran while one was open for 16% of the time, Pallas kernels for 69%

profile of v10, /device:TPU:0, one launch (start us, length us, event | category | flops | bytes accessed | tf_op | source)
XLA Modules:
  0.0 581.2 jit_solution(9408745684348684406)
XLA Ops:
  8.7 3.0 collective-permute-start
  13.1 58.6 %shard_map.330 = (bf16[4,2,1,128,1024]{4,3,2,1,0:T(8,128)(2,1)}, bf16[4,2,1,128,1024]{4,3,2,1,0:T(8,128)(2,1)}, bf16[4,2,1,128,1024]{4,3,2,1,0:T(8,128)(2,1)}, bf16[4,2,1,16,512]{4,3,2,1,0:T(8,128)(2,1)}) custom-call(bf16[1,128,256]{2,1,0:T(8,128)(2,1)} %bitcast.141, bf16[1,128,256]{2,1,0:T(8,128)(2,1)} %bitcast.142, bf16[1,128,256]{2,1,0:T(8,128)(2,1)} %bitcast.143, ...), custom_call_target="tpu_custom_call" | custom-call | bytes 12845056 | tf_op jit(solution)/shard_map/pallas_call | solution.py:738
  78.5 3.0 convolution_convert_fusion.11.refs_2_.refs_5_
  83.4 119.2 %shard_map.331 = (bf16[750,1024]{1,0:T(8,128)(2,1)S(1)}, f32[750,128]{1,0:T(8,128)S(1)}, bf16[4,750,128]{2,1,0:T(8,128)(2,1)S(1)}, bf16[4,750,128]{2,1,0:T(8,128...) custom-call(bf16[750,1024]{1,0:T(8,128)(2,1)S(1)} %convolution_conve, ...), custom_call_target="tpu_custom_call" | custom-call | flops 2304000000 | bytes 12288000 | tf_op jit(solution)/shard_map/pallas_call | solution.py:1176
  202.6 4.9 fusion.35
  216.7 6.6 %shard_map.332 = (bf16[750,1024]{1,0:T(8,128)(2,1)S(1)}, f32[750,128]{1,0:T(8,128)S(1)}) custom-call(bf16[750,1024]{1,0:T(8,128)(2,1)S(1)} %convolution_convert_fusion.10.q_ref, bf16[64,1024]{1,0:T(8,128)(2,1)S(1)} %convolution_convert_fusion.15.k_ref, bf16[64,1024]{1,0:T(8,128)(2,1)S(1)} %convolution_convert_fusion.14.v_ref), custom_call_target="tpu_custom_call" | custom-call | flops 196608000 | bytes 4608000 | tf_op jit(solution)/shard_map/pallas_call | solution.py:1285
  228.5 49.0 %shard_map.333 = (bf16[750,1024]{1,0:T(8,128)(2,1)}, f32[750,1024]{1,0:T(8,128)}, bf16[8,4,128,1024]{3,2,1,0:T(8,128)(2,1)}, bf16[4096,1024]{1,0:T(8,128)(2,1)}) custom-call(bf16[750,1024]{1,0:T(8,128)(2,1)} %add_convert_fusion.h_ref, bf16[750,1024]{1,0:T(8,128)(2,1)} %cot_ref.1, f32[750,1024]{1,0:T(8,128)} %copy-done.14, ...), custom_call_target="tpu_custom_call" | custom-call | flops 37748736000 | bytes 45842432 | tf_op jit(solution)/shard_map/pallas_call | solution.py:474
  277.6 4.0 multiply_reduce_fusion
  287.0 10.5 %shard_map.334 = (bf16[750,1024]{1,0:T(8,128)(2,1)S(1)}, bf16[64,1024]{1,0:T(8,128)(2,1)S(1)}, bf16[64,1024]{1,0:T(8,128)(2,1)S(1)}) custom-call(bf16[750,1024]{1,0:T(8,128)(2,1)S(1)} %convolution_convert_fusion.10.q_ref, bf16[64,1024]{1,0:T(8,128)(2,1)S(1)} %convolution_convert_fusion.15.k_ref, bf16[64,1024]{1,0:T(8,128)(2,1)S(1)} %convolution_convert_fusion.14.v_ref, ...), custom_call_target="tpu_custom_call" | custom-call | flops 491520000 | bytes 7680000 | tf_op jit(solution)/shard_map/pallas_call | solution.py:1313
  297.5 4.8 collective-permute-start.1
  307.2 3.2 convolution_convert_fusion.7
  310.4 3.0 convolution_convert_fusion.8.refs_3_.refs_6_
  313.4 3.4 convolution_convert_fusion.6
  316.8 3.2 convolution_convert_fusion.5
  324.6 150.9 %shard_map.335 = (bf16[750,1024]{1,0:T(8,128)(2,1)}, bf16[750,1024]{1,0:T(8,128)(2,1)}, bf16[750,1024]{1,0:T(8,128)(2,1)}, f32[1,128,256]{2,1,0:T(8,128)}, f32[1...) custom-call(bf16[750,1024]{1,0:T(8,128)(2,1)} %copy-done, ...), custom_call_target="tpu_custom_call" | custom-call | flops 5760000000 | bytes 12288000 | tf_op jit(solution)/shard_map/pallas_call | solution.py:1515
  475.5 4.0 fusion.37
  482.0 3.9 fusion.31
  486.0 3.3 fusion.8
  490.3 5.1 convolution_convert_fusion.4
  495.4 3.4 convolution_convert_fusion.2
  498.8 3.4 convolution_convert_fusion.3
  502.2 53.5 %shard_map.336 = (f32[1,128,256]{2,1,0:T(8,128)}, f32[1,128,256]{2,1,0:T(8,128)}, f32[1,128,256]{2,1,0:T(8,128)}, f32[1,16,128]{2,1,0:T(8,128)}) custom-call(bf16[4,2,1,128,1024]{4,3,2,1,0:T(8,128)(2,1)} %bitcast.128, bf16[4,2,1,128,1024]{4,3,2,1,0:T(8,128)(2,1)} %bitcast.130, bf16[4,2,1,128,1024]{4,3,2,1,0:T(8,128)(2,1)} %bitcast.129, ...), custom_call_target="tpu_custom_call" | custom-call | flops 3211264 | bytes 12845056 | tf_op jit(solution)/shard_map/pallas_call | solution.py:938
  559.5 3.0 convolution_add_fusion.1
  562.6 3.9 add_add_fusion.3
  (180 shorter events, 55.6 us)
Async XLA Ops:
  7.2 67.7 %copy-start.16 = (bf16[750,1024]{1,0:T(8,128)(2,1)S(1)}, bf16[750,1024]{1,0:T(8,128)(2,1)}, u32[]{:S(2)}) copy-start(bf16[750,1024]{1,0:T(8,128)(2,1)} %param.21) | copy-start | bytes 4608004
  7.2 221.3 %all-gather.5.cloned.1.call-start = ((), (), s32[]{:S(2)}) async-start(), calls=%async_computation.2 | async-start | bytes 8650752 | tf_op jit(solution)/shard_map/all_gather | solution.py:1567
  7.9 220.5 %all-gather.7.cloned.1.call-start = ((), (), s32[]{:S(2)}) async-start(), calls=%async_computation.3 | async-start | bytes 8650752 | tf_op jit(solution)/shard_map/all_gather | solution.py:1568
  8.7 557.8 %reduce-scatter.2.cloned.1.call-start = ((), (), s32[]{:S(2)}) async-start(), calls=%async_computation.1 | async-start | bytes 8650752 | tf_op jit(solution)/shard_map/reduce_scatter | solution.py:1604
  8.7 203.6 %collective-permute-start = (bf16[32,1024]{1,0:T(8,128)(2,1)}, bf16[32,1024]{1,0:T(8,128)(2,1)S(1)}, u32[]{:S(2)}, u32[]{:S(2)}) collective-permute-start(bf16[32,1024]{1,0:T(8,128)(2,1)} %param.22), channel_id=1, source_target_pairs={{0,4},{8,12},{16,20},{24,28},{4,0},{12,8},{20,16},{28,24},{1,5},{9... | collective-permute-start | bytes 196616 | tf_op jit(solution)/shard_map/ppermute | solution.py:1594
  83.3 119.2 %copy-start = (bf16[750,1024]{1,0:T(8,128)(2,1)}, bf16[750,1024]{1,0:T(8,128)(2,1)S(1)}, u32[]{:S(2)}) copy-start(bf16[750,1024]{1,0:T(8,128)(2,1)S(1)} %convolution_convert_fusion.13.refs_0_.refs_3_) | copy-start | bytes 4608004
  202.6 5.0 copy-start.1
  202.6 5.0 copy-start.3
  212.4 10.9 %copy-start.21 = (f32[750,1024]{1,0:T(8,128)S(1)}, f32[750,1024]{1,0:T(8,128)}, u32[]{:S(2)}) copy-start(f32[750,1024]{1,0:T(8,128)} %copy-done.20) | copy-start | bytes 9216004
  212.4 10.9 %copy-start.46 = (bf16[4,2,1,128,1024]{4,3,2,1,0:T(8,128)(2,1)S(1)}, bf16[4,2,1,128,1024]{4,3,2,1,0:T(8,128)(2,1)}, u32[]{:S(2)}) copy-start(bf16[4,2,1,128,1024]{4,3,2,1,0:T(8,128)(2,1)} %get-tuple-element.77) | copy-start | bytes 6291460
  287.0 15.4 %copy-start.22 = (f32[750,1024]{1,0:T(8,128)S(1)}, f32[750,1024]{1,0:T(8,128)}, u32[]{:S(2)}) copy-start(f32[750,1024]{1,0:T(8,128)} %copy-done.20) | copy-start | bytes 9216004
  287.0 15.4 %copy-start.45 = (bf16[4,2,1,128,1024]{4,3,2,1,0:T(8,128)(2,1)S(1)}, bf16[4,2,1,128,1024]{4,3,2,1,0:T(8,128)(2,1)}, u32[]{:S(2)}) copy-start(bf16[4,2,1,128,1024]{4,3,2,1,0:T(8,128)(2,1)} %get-tuple-element.73) | copy-start | bytes 6291460
  297.5 22.8 %collective-permute-start.1 = (bf16[32,2048]{1,0:T(8,128)(2,1)S(1)}, bf16[32,2048]{1,0:T(8,128)(2,1)S(1)}, u32[]{:S(2)}, u32[]{:S(2)}) collective-permute-start(bf16[32,2048]{1,0:T(8,128)(2,1)S(1)} %broadcast_select_fusion), channel_id=1, source_target_pairs={{0,4},{8,12},{16,20},{24,28},{4,0},{12,8},{20,16},{28,24},{1,5},{9... | collective-permute-start | bytes 393224 | tf_op jit(solution)/shard_map/ppermute | solution.py:1616
  490.3 5.1 copy-start.42
  555.7 6.8 %copy-start.19 = (f32[750,1024]{1,0:T(8,128)S(1)}, f32[750,1024]{1,0:T(8,128)}, u32[]{:S(2)}) copy-start(f32[750,1024]{1,0:T(8,128)} %copy-done.18) | copy-start | bytes 9216004
  562.5 5.8 %copy-start.34 = (f32[1,128,256]{2,1,0:T(8,128)S(1)}, f32[1,128,256]{2,1,0:T(8,128)}, u32[]{:S(2)}) copy-start(f32[1,128,256]{2,1,0:T(8,128)} %get-tuple-element.92) | copy-start | bytes 393220
  562.5 6.5 %copy-start.33 = (f32[1,128,256]{2,1,0:T(8,128)S(1)}, f32[1,128,256]{2,1,0:T(8,128)}, u32[]{:S(2)}) copy-start(f32[1,128,256]{2,1,0:T(8,128)} %get-tuple-element.93) | copy-start | bytes 393220
  562.5 7.1 %copy-start.32 = (f32[1,128,256]{2,1,0:T(8,128)S(1)}, f32[1,128,256]{2,1,0:T(8,128)}, u32[]{:S(2)}) copy-start(f32[1,128,256]{2,1,0:T(8,128)} %get-tuple-element.94) | copy-start | bytes 393220
  562.5 7.8 %copy-start.31 = (f32[1,128,256]{2,1,0:T(8,128)S(1)}, f32[1,128,256]{2,1,0:T(8,128)}, u32[]{:S(2)}) copy-start(f32[1,128,256]{2,1,0:T(8,128)} %get-tuple-element.95) | copy-start | bytes 393220
  562.5 8.4 %copy-start.30 = (f32[1,128,256]{2,1,0:T(8,128)S(1)}, f32[1,128,256]{2,1,0:T(8,128)}, u32[]{:S(2)}) copy-start(f32[1,128,256]{2,1,0:T(8,128)} %get-tuple-element.96) | copy-start | bytes 393220
  562.5 9.1 %copy-start.29 = (f32[1,128,256]{2,1,0:T(8,128)S(1)}, f32[1,128,256]{2,1,0:T(8,128)}, u32[]{:S(2)}) copy-start(f32[1,128,256]{2,1,0:T(8,128)} %get-tuple-element.97) | copy-start | bytes 393220
  562.5 9.7 %copy-start.28 = (f32[1,128,256]{2,1,0:T(8,128)S(1)}, f32[1,128,256]{2,1,0:T(8,128)}, u32[]{:S(2)}) copy-start(f32[1,128,256]{2,1,0:T(8,128)} %get-tuple-element.98) | copy-start | bytes 393220
  562.5 10.4 %copy-start.27 = (f32[1,128,256]{2,1,0:T(8,128)S(1)}, f32[1,128,256]{2,1,0:T(8,128)}, u32[]{:S(2)}) copy-start(f32[1,128,256]{2,1,0:T(8,128)} %get-tuple-element.99) | copy-start | bytes 393220
  566.5 7.1 %copy-start.26 = (f32[4,128,256]{2,1,0:T(8,128)S(1)}, f32[4,128,256]{2,1,0:T(8,128)}, u32[]{:S(2)}) copy-start(f32[4,128,256]{2,1,0:T(8,128)} %get-tuple-element.101) | copy-start | bytes 1572868
  (29 other events, 81.3 us)
Sparse Core Ops, SparseCore 0:
  10.9 86.3 all-gather.4
  100.2 91.2 all-gather.6
  277.7 170.8 reduce-scatter.1

commit v11 on v10

--- a/solution.py
+++ b/solution.py
@@ -1635,7 +1635,7 @@
     (grad_self_q, grad_self_k, grad_self_v), early_sums = pair_back(
         self_q, self_k, self_v, grad_self_mix, self_mix, log_lanes, (far_q, far_k, far_v),
         [by_place(g, 1) for g in (self_out_grad, cross_query_part, cross_key_part, cross_value_part, cross_out_grad)]
-        + [by_place(down_grad, down_weight.shape[0] // block_rows)], 4, [5] * 12)
+        + [by_place(down_grad, down_weight.shape[0] // block_rows)], 4, [6] * 11)
     self_query_part = over_tokens(hidden_one, grad_self_q)
     self_key_part = over_tokens(hidden_one, grad_self_k)
     self_value_part = over_tokens(hidden_one, grad_self_v)

time: 588 us -> 600 us (1.020)
  Pallas kernels: 448 us -> 461 us
    pallas_call x1, Pallas kernels: 151 us -> 161 us  [pair_back(): pl.pallas_call(functools.partial(pair_back_kernel, tile, far_tile, units,...]
where the time goes in v11:
time: 600 us; the launch traced here: 594 us
  Pallas kernels  461 us (77%)
  matrix products  68.8 us (11%)
  other arithmetic  21.3 us (4%)
  local copies, waits for them, and re-layouts  18.7 us (3%)
  between operations  14.8 us (2%)
  starting transfers between devices  7.95 us (1%)
    pallas_call x1, Pallas kernels, pair_back(): pl.pallas_call(functools.partial(pair_back_kernel, tile, far_tile, units,...  161 us
    pallas_call x1, Pallas kernels, pair_attend(): pl.pallas_call(functools.partial(pair_attend_kernel, tile, units, count,...  119 us
    pallas_call x1, Pallas kernels, gather_blocks(): pl.pallas_call(functools.partial(gather_kernel, units, count), out_shape=...  58.6 us
    pallas_call x1, Pallas kernels, scatter_blocks(): pl.pallas_call(functools.partial(scatter_kernel, units, count), out_shape...  55.6 us
    pallas_call x1, Pallas kernels, feed(): pl.pallas_call(feed_kernel, grid=(ff // chunk,), in_specs=[whole, whole,...  49 us
    dot_general x8, matrix products, over_tokens(): lax.dot_general(left, right, (((0,), (0,)), ((), ())), preferred_element_...  26 us
    dot_general x8, matrix products, by_transposed(): lax.dot_general(left, right, (((1,), (1,)), ((), ())), preferred_element_...  22.1 us
    dot_general x8, matrix products, matmul(): return jnp.dot(left, right, preferred_element_type=jnp.float32)  20.7 us
  transfers between devices with their start and end apart: 5, of which 0 were waited for; matrix products, arithmetic and copies ran while one was open for 16% of the time, Pallas kernels for 69%

profile of v11, /device:TPU:0, one launch (start us, length us, event | category | flops | bytes accessed | tf_op | source)
XLA Modules:
  0.0 593.5 jit_solution(17085132494070305166)
XLA Ops:
  8.7 3.0 collective-permute-start
  13.1 58.6 %shard_map.330 = (bf16[4,2,1,128,1024]{4,3,2,1,0:T(8,128)(2,1)}, bf16[4,2,1,128,1024]{4,3,2,1,0:T(8,128)(2,1)}, bf16[4,2,1,128,1024]{4,3,2,1,0:T(8,128)(2,1)}, bf16[4,2,1,16,512]{4,3,2,1,0:T(8,128)(2,1)}) custom-call(bf16[1,128,256]{2,1,0:T(8,128)(2,1)} %bitcast.141, bf16[1,128,256]{2,1,0:T(8,128)(2,1)} %bitcast.142, bf16[1,128,256]{2,1,0:T(8,128)(2,1)} %bitcast.143, ...), custom_call_target="tpu_custom_call" | custom-call | bytes 12845056 | tf_op jit(solution)/shard_map/pallas_call | solution.py:738
  78.5 3.0 convolution_convert_fusion.11.refs_2_.refs_5_
  83.4 119.2 %shard_map.331 = (bf16[750,1024]{1,0:T(8,128)(2,1)S(1)}, f32[750,128]{1,0:T(8,128)S(1)}, bf16[4,750,128]{2,1,0:T(8,128)(2,1)S(1)}, bf16[4,750,128]{2,1,0:T(8,128...) custom-call(bf16[750,1024]{1,0:T(8,128)(2,1)S(1)} %convolution_conve, ...), custom_call_target="tpu_custom_call" | custom-call | flops 2304000000 | bytes 12288000 | tf_op jit(solution)/shard_map/pallas_call | solution.py:1176
  202.6 4.9 fusion.35
  216.7 6.6 %shard_map.332 = (bf16[750,1024]{1,0:T(8,128)(2,1)S(1)}, f32[750,128]{1,0:T(8,128)S(1)}) custom-call(bf16[750,1024]{1,0:T(8,128)(2,1)S(1)} %convolution_convert_fusion.10.q_ref, bf16[64,1024]{1,0:T(8,128)(2,1)S(1)} %convolution_convert_fusion.15.k_ref, bf16[64,1024]{1,0:T(8,128)(2,1)S(1)} %convolution_convert_fusion.14.v_ref), custom_call_target="tpu_custom_call" | custom-call | flops 196608000 | bytes 4608000 | tf_op jit(solution)/shard_map/pallas_call | solution.py:1285
  228.5 49.0 %shard_map.333 = (bf16[750,1024]{1,0:T(8,128)(2,1)}, f32[750,1024]{1,0:T(8,128)}, bf16[8,4,128,1024]{3,2,1,0:T(8,128)(2,1)}, bf16[4096,1024]{1,0:T(8,128)(2,1)}) custom-call(bf16[750,1024]{1,0:T(8,128)(2,1)} %add_convert_fusion.h_ref, bf16[750,1024]{1,0:T(8,128)(2,1)} %cot_ref.1, f32[750,1024]{1,0:T(8,128)} %copy-done.14, ...), custom_call_target="tpu_custom_call" | custom-call | flops 37748736000 | bytes 45842432 | tf_op jit(solution)/shard_map/pallas_call | solution.py:474
  277.6 4.0 multiply_reduce_fusion
  287.0 10.5 %shard_map.334 = (bf16[750,1024]{1,0:T(8,128)(2,1)S(1)}, bf16[64,1024]{1,0:T(8,128)(2,1)S(1)}, bf16[64,1024]{1,0:T(8,128)(2,1)S(1)}) custom-call(bf16[750,1024]{1,0:T(8,128)(2,1)S(1)} %convolution_convert_fusion.10.q_ref, bf16[64,1024]{1,0:T(8,128)(2,1)S(1)} %convolution_convert_fusion.15.k_ref, bf16[64,1024]{1,0:T(8,128)(2,1)S(1)} %convolution_convert_fusion.14.v_ref, ...), custom_call_target="tpu_custom_call" | custom-call | flops 491520000 | bytes 7680000 | tf_op jit(solution)/shard_map/pallas_call | solution.py:1313
  297.5 4.8 collective-permute-start.1
  307.2 3.2 convolution_convert_fusion.7
  310.4 3.0 convolution_convert_fusion.8.refs_3_.refs_6_
  313.4 3.4 convolution_convert_fusion.6
  316.8 3.2 convolution_convert_fusion.5
  324.6 161.1 %shard_map.335 = (bf16[750,1024]{1,0:T(8,128)(2,1)}, bf16[750,1024]{1,0:T(8,128)(2,1)}, bf16[750,1024]{1,0:T(8,128)(2,1)}, f32[1,128,256]{2,1,0:T(8,128)}, f32[1...) custom-call(bf16[750,1024]{1,0:T(8,128)(2,1)} %copy-done, ...), custom_call_target="tpu_custom_call" | custom-call | flops 5760000000 | bytes 12288000 | tf_op jit(solution)/shard_map/pallas_call | solution.py:1515
  485.7 4.0 fusion.37
  492.2 3.9 fusion.31
  496.2 3.3 fusion.8
  500.5 5.0 convolution_convert_fusion.4
  505.5 3.4 convolution_convert_fusion.2
  509.0 3.4 convolution_convert_fusion.3
  512.4 55.6 %shard_map.336 = (f32[1,128,256]{2,1,0:T(8,128)}, f32[1,128,256]{2,1,0:T(8,128)}, f32[1,128,256]{2,1,0:T(8,128)}, f32[1,16,128]{2,1,0:T(8,128)}) custom-call(bf16[4,2,1,128,1024]{4,3,2,1,0:T(8,128)(2,1)} %bitcast.128, bf16[4,2,1,128,1024]{4,3,2,1,0:T(8,128)(2,1)} %bitcast.130, bf16[4,2,1,128,1024]{4,3,2,1,0:T(8,128)(2,1)} %bitcast.129, ...), custom_call_target="tpu_custom_call" | custom-call | flops 3211264 | bytes 12845056 | tf_op jit(solution)/shard_map/pallas_call | solution.py:938
  571.8 3.0 convolution_add_fusion.1
  574.9 3.9 add_add_fusion.3
  (180 shorter events, 55.6 us)
Async XLA Ops:
  7.2 67.7 %copy-start.16 = (bf16[750,1024]{1,0:T(8,128)(2,1)S(1)}, bf16[750,1024]{1,0:T(8,128)(2,1)}, u32[]{:S(2)}) copy-start(bf16[750,1024]{1,0:T(8,128)(2,1)} %param.21) | copy-start | bytes 4608004
  7.2 221.3 %all-gather.5.cloned.1.call-start = ((), (), s32[]{:S(2)}) async-start(), calls=%async_computation.2 | async-start | bytes 8650752 | tf_op jit(solution)/shard_map/all_gather | solution.py:1567
  7.9 220.5 %all-gather.7.cloned.1.call-start = ((), (), s32[]{:S(2)}) async-start(), calls=%async_computation.3 | async-start | bytes 8650752 | tf_op jit(solution)/shard_map/all_gather | solution.py:1568
  8.7 570.1 %reduce-scatter.2.cloned.1.call-start = ((), (), s32[]{:S(2)}) async-start(), calls=%async_computation.1 | async-start | bytes 8650752 | tf_op jit(solution)/shard_map/reduce_scatter | solution.py:1604
  8.7 203.6 %collective-permute-start = (bf16[32,1024]{1,0:T(8,128)(2,1)}, bf16[32,1024]{1,0:T(8,128)(2,1)S(1)}, u32[]{:S(2)}, u32[]{:S(2)}) collective-permute-start(bf16[32,1024]{1,0:T(8,128)(2,1)} %param.22), channel_id=1, source_target_pairs={{0,4},{8,12},{16,20},{24,28},{4,0},{12,8},{20,16},{28,24},{1,5},{9... | collective-permute-start | bytes 196616 | tf_op jit(solution)/shard_map/ppermute | solution.py:1594
  83.3 119.2 %copy-start = (bf16[750,1024]{1,0:T(8,128)(2,1)}, bf16[750,1024]{1,0:T(8,128)(2,1)S(1)}, u32[]{:S(2)}) copy-start(bf16[750,1024]{1,0:T(8,128)(2,1)S(1)} %convolution_convert_fusion.13.refs_0_.refs_3_) | copy-start | bytes 4608004
  202.6 5.0 copy-start.1
  202.6 5.0 copy-start.3
  212.4 10.9 %copy-start.21 = (f32[750,1024]{1,0:T(8,128)S(1)}, f32[750,1024]{1,0:T(8,128)}, u32[]{:S(2)}) copy-start(f32[750,1024]{1,0:T(8,128)} %copy-done.20) | copy-start | bytes 9216004
  212.4 10.9 %copy-start.46 = (bf16[4,2,1,128,1024]{4,3,2,1,0:T(8,128)(2,1)S(1)}, bf16[4,2,1,128,1024]{4,3,2,1,0:T(8,128)(2,1)}, u32[]{:S(2)}) copy-start(bf16[4,2,1,128,1024]{4,3,2,1,0:T(8,128)(2,1)} %get-tuple-element.77) | copy-start | bytes 6291460
  287.0 15.4 %copy-start.22 = (f32[750,1024]{1,0:T(8,128)S(1)}, f32[750,1024]{1,0:T(8,128)}, u32[]{:S(2)}) copy-start(f32[750,1024]{1,0:T(8,128)} %copy-done.20) | copy-start | bytes 9216004
  287.0 15.4 %copy-start.45 = (bf16[4,2,1,128,1024]{4,3,2,1,0:T(8,128)(2,1)S(1)}, bf16[4,2,1,128,1024]{4,3,2,1,0:T(8,128)(2,1)}, u32[]{:S(2)}) copy-start(bf16[4,2,1,128,1024]{4,3,2,1,0:T(8,128)(2,1)} %get-tuple-element.73) | copy-start | bytes 6291460
  297.5 22.8 %collective-permute-start.1 = (bf16[32,2048]{1,0:T(8,128)(2,1)S(1)}, bf16[32,2048]{1,0:T(8,128)(2,1)S(1)}, u32[]{:S(2)}, u32[]{:S(2)}) collective-permute-start(bf16[32,2048]{1,0:T(8,128)(2,1)S(1)} %broadcast_select_fusion), channel_id=1, source_target_pairs={{0,4},{8,12},{16,20},{24,28},{4,0},{12,8},{20,16},{28,24},{1,5},{9... | collective-permute-start | bytes 393224 | tf_op jit(solution)/shard_map/ppermute | solution.py:1616
  500.5 5.1 copy-start.42
  568.1 6.8 %copy-start.19 = (f32[750,1024]{1,0:T(8,128)S(1)}, f32[750,1024]{1,0:T(8,128)}, u32[]{:S(2)}) copy-start(f32[750,1024]{1,0:T(8,128)} %copy-done.18) | copy-start | bytes 9216004
  574.8 5.8 copy-start.34
  574.8 6.5 %copy-start.33 = (f32[1,128,256]{2,1,0:T(8,128)S(1)}, f32[1,128,256]{2,1,0:T(8,128)}, u32[]{:S(2)}) copy-start(f32[1,128,256]{2,1,0:T(8,128)} %get-tuple-element.93) | copy-start | bytes 393220
  574.9 7.1 %copy-start.32 = (f32[1,128,256]{2,1,0:T(8,128)S(1)}, f32[1,128,256]{2,1,0:T(8,128)}, u32[]{:S(2)}) copy-start(f32[1,128,256]{2,1,0:T(8,128)} %get-tuple-element.94) | copy-start | bytes 393220
  574.9 7.8 %copy-start.31 = (f32[1,128,256]{2,1,0:T(8,128)S(1)}, f32[1,128,256]{2,1,0:T(8,128)}, u32[]{:S(2)}) copy-start(f32[1,128,256]{2,1,0:T(8,128)} %get-tuple-element.95) | copy-start | bytes 393220
  574.9 8.4 %copy-start.30 = (f32[1,128,256]{2,1,0:T(8,128)S(1)}, f32[1,128,256]{2,1,0:T(8,128)}, u32[]{:S(2)}) copy-start(f32[1,128,256]{2,1,0:T(8,128)} %get-tuple-element.96) | copy-start | bytes 393220
  574.9 9.1 %copy-start.29 = (f32[1,128,256]{2,1,0:T(8,128)S(1)}, f32[1,128,256]{2,1,0:T(8,128)}, u32[]{:S(2)}) copy-start(f32[1,128,256]{2,1,0:T(8,128)} %get-tuple-element.97) | copy-start | bytes 393220
  574.9 9.7 %copy-start.28 = (f32[1,128,256]{2,1,0:T(8,128)S(1)}, f32[1,128,256]{2,1,0:T(8,128)}, u32[]{:S(2)}) copy-start(f32[1,128,256]{2,1,0:T(8,128)} %get-tuple-element.98) | copy-start | bytes 393220
  574.9 10.4 %copy-start.27 = (f32[1,128,256]{2,1,0:T(8,128)S(1)}, f32[1,128,256]{2,1,0:T(8,128)}, u32[]{:S(2)}) copy-start(f32[1,128,256]{2,1,0:T(8,128)} %get-tuple-element.99) | copy-start | bytes 393220
  578.8 7.1 %copy-start.26 = (f32[4,128,256]{2,1,0:T(8,128)S(1)}, f32[4,128,256]{2,1,0:T(8,128)}, u32[]{:S(2)}) copy-start(f32[4,128,256]{2,1,0:T(8,128)} %get-tuple-element.101) | copy-start | bytes 1572868
  (29 other events, 81.3 us)
Sparse Core Ops, SparseCore 0:
  10.9 86.3 all-gather.4
  100.2 91.2 all-gather.6
  277.7 170.7 reduce-scatter.1
